TPU v7x, 128 devices: a whole 4x4x4 slice. The times are simulated.
128 devices in a mesh: dp: 4 (over x_lo, core), tensor: 4 (over y), ctx: 8 (over x_hi, z).
Axes of the slice: x: 4 (x_hi: 2, x_lo: 2; x = x_hi * 2 + x_lo), y: 4, z: 4, core: 2. Of those that a mesh axis runs over, the one named last changes fastest.
Arguments:
- tokens: bfloat16 [4, 4096, 768], P('dp', 'ctx'), may hold values from -6 to 6
- norm_gain: bfloat16 [2, 768], P(None, ('dp', 'ctx')), may hold values from 0.099609375 to 1.8984375
- norm_bias: bfloat16 [2, 768], P(None, ('dp', 'ctx')), may hold values from -1.5 to 1.5
- qkv_weight: bfloat16 [768, 3, 768], P(('dp', 'ctx'), None, 'tensor'), may hold values from -0.21875 to 0.21875
- qkv_bias: bfloat16 [3, 12, 64], P(None, 'tensor', ('dp', 'ctx')), may hold values from -2.5 to 2.5
- dense_weight: bfloat16 [768, 768], P('tensor', ('dp', 'ctx')), may hold values from -3 to 3
- fc1_weight: bfloat16 [768, 3072], P(('dp', 'ctx'), 'tensor'), may hold values from -0.21875 to 0.21875
- fc1_bias: bfloat16 [48, 64], P('tensor', ('dp', 'ctx')), may hold values from -2.5 to 2.5
- fc2_weight: bfloat16 [3072, 768], P('tensor', ('dp', 'ctx')), may hold values from -0.109375 to 0.109375
- out_bias: bfloat16 [2, 768], P(None, ('dp', 'ctx')), may hold values from -1.5 to 1.5
- cotangent: bfloat16 [4, 4096, 768], P('dp', 'ctx', 'tensor'), may hold values from -6 to 6
Outputs:
- output: bfloat16 [4, 4096, 768], P('dp', 'ctx', 'tensor')
- input_grad: float32 [4, 4096, 768], P('dp', 'ctx', 'tensor')
- grad_norm_gain: float32 [2, 768], P(None, ('dp', 'ctx'))
- grad_norm_bias: float32 [2, 768], P(None, ('dp', 'ctx'))
- grad_qkv_weight: float32 [768, 3, 768], P(('dp', 'ctx'), None, 'tensor')
- grad_qkv_bias: float32 [3, 12, 64], P(None, 'tensor', ('dp', 'ctx'))
- grad_dense_weight: float32 [768, 768], P('tensor', ('dp', 'ctx'))
- grad_fc1_weight: float32 [768, 3072], P(('dp', 'ctx'), 'tensor')
- grad_fc1_bias: float32 [48, 64], P('tensor', ('dp', 'ctx'))
- grad_fc2_weight: float32 [3072, 768], P('tensor', ('dp', 'ctx'))
- grad_out_bias: float32 [2, 768], P(None, ('dp', 'ctx'))
All inputs are finite; a program needn't handle non-finite values.
Results may differ from a plain program's by a relative error of at most 0.023.
Values may be sent and summed in bfloat16 or wider, within the bound.
A program may use at most 64 MiB of HBM per device.

v0:
```python
import jax
import jax.numpy as jnp
from jax import lax
from jax.sharding import PartitionSpec as P

HD = 64
ROT = 16


EPSILON = 1e-05


def norm_rows(values_in, gain_row, shift_row):
    row_mean = jnp.mean(values_in, axis=-1, keepdims=True)
    centred = values_in - row_mean
    variance = jnp.mean(centred * centred, axis=-1, keepdims=True)
    return centred * lax.rsqrt(variance + EPSILON) * gain_row + shift_row


def angles(positions):
    frequency = 10000.0 ** (-2.0 * jnp.arange(ROT // 2, dtype=jnp.float32) / ROT)
    phases = positions.astype(jnp.float32)[:, None] * frequency[None, :]
    return (jnp.cos(phases)[:, None, :], jnp.sin(phases)[:, None, :])


def rotate(tensor_in, cosine, sine_table):
    half_rot = ROT // 2
    lower = tensor_in[..., :half_rot]
    upper = tensor_in[..., half_rot:ROT]
    return jnp.concatenate(
        [
            lower * cosine - upper * sine_table,
            upper * cosine + lower * sine_table,
            tensor_in[..., ROT:],
        ],
        axis=-1,
    )


def block_scores(query_block, key_block, query_pos, key_pos):
    scores = jnp.einsum(
        "sqhe,skhe->shqk", query_block, key_block, preferred_element_type=jnp.float32
    ) * HD ** (-0.5)
    causal = query_pos[:, None] >= key_pos[None, :]
    return (scores, causal)


def score_grads(
    query_block, key_block, value_block, dhead_block, lse_block, delta_block, query_pos, key_pos
):
    scores, causal = block_scores(query_block, key_block, query_pos, key_pos)
    attn_probs = jnp.where(causal, jnp.exp(scores - lse_block[..., None]), 0.0)
    d_probs = jnp.einsum(
        "sqhe,skhe->shqk", dhead_block, value_block, preferred_element_type=jnp.float32
    )
    d_scores = (attn_probs * (d_probs - delta_block[..., None])).astype(jnp.bfloat16)
    return (attn_probs.astype(jnp.bfloat16), d_scores)


def shards(
    tokens,
    norm_gain,
    norm_bias,
    qkv_weight,
    qkv_bias,
    dense_weight,
    fc1_weight,
    fc1_bias,
    fc2_weight,
    out_bias,
    cotangent,
):
    seq_count, tok_rows, features = tokens.shape
    width_part = features // lax.axis_size("tensor")
    tensor_place = lax.axis_index("tensor")
    block_place = lax.axis_index("ctx")
    gains, shifts, qkv_full, qkv_shift, dense_full, fc1_full, fc1_shift, fc2_full, out_shift = (
        lax.all_gather(norm_gain, ("dp", "ctx"), axis=1, tiled=True),
        lax.all_gather(norm_bias, ("dp", "ctx"), axis=1, tiled=True),
        lax.all_gather(qkv_weight, ("dp", "ctx"), axis=0, tiled=True),
        lax.all_gather(qkv_bias, ("dp", "ctx"), axis=2, tiled=True),
        lax.all_gather(dense_weight, ("dp", "ctx"), axis=1, tiled=True),
        lax.all_gather(fc1_weight, ("dp", "ctx"), axis=0, tiled=True),
        lax.all_gather(fc1_bias, ("dp", "ctx"), axis=1, tiled=True),
        lax.all_gather(fc2_weight, ("dp", "ctx"), axis=1, tiled=True),
        lax.all_gather(out_bias, ("dp", "ctx"), axis=1, tiled=True),
    )
    channels = qkv_full.shape[2]
    head_count = channels // HD
    scale = HD ** (-0.5)
    tokens_float = tokens.astype(jnp.float32)
    gain_float = gains.astype(jnp.float32)
    shift_float = shifts.astype(jnp.float32)
    norm_one = norm_rows(tokens_float, gain_float[0], shift_float[0]).astype(jnp.bfloat16)
    norm_two = norm_rows(tokens_float, gain_float[1], shift_float[1]).astype(jnp.bfloat16)
    projected = jnp.einsum("std,dce->stce", norm_one, qkv_full, preferred_element_type=jnp.float32)
    projected = projected + qkv_shift.astype(jnp.float32).reshape(3, channels)
    query_pos = block_place * tok_rows + jnp.arange(tok_rows)
    cosine, sine_table = angles(query_pos)
    queries = rotate(
        projected[:, :, 0].reshape(seq_count, tok_rows, head_count, HD), cosine, sine_table
    ).astype(jnp.bfloat16)
    key_flat = rotate(
        projected[:, :, 1].reshape(seq_count, tok_rows, head_count, HD), cosine, sine_table
    )
    key_flat = key_flat.astype(jnp.bfloat16).reshape(seq_count, tok_rows, channels)
    value_flat = projected[:, :, 2].astype(jnp.bfloat16)
    key_all, value_all = (
        lax.all_gather(key_flat, "ctx", axis=1, tiled=True),
        lax.all_gather(value_flat, "ctx", axis=1, tiled=True),
    )

    def key_block_at(source, block_number):
        piece = lax.dynamic_slice_in_dim(source, block_number * tok_rows, tok_rows, 1)
        return piece.reshape(seq_count, tok_rows, head_count, HD)

    def pass_one(block_number, carried):
        running, denominator = carried
        key_pos = block_number * tok_rows + jnp.arange(tok_rows)
        scores, causal = block_scores(
            queries, key_block_at(key_all, block_number), query_pos, key_pos
        )
        block_max = jnp.max(jnp.where(causal, scores, -1e30), axis=-1)
        new_max = jnp.maximum(running, block_max)
        unnormed = jnp.where(causal, jnp.exp(scores - new_max[..., None]), 0.0)
        denominator = denominator * jnp.exp(running - new_max) + jnp.sum(unnormed, axis=-1)
        return (new_max, denominator)

    initial = (
        jnp.full((seq_count, head_count, tok_rows), -1e30, jnp.float32),
        jnp.zeros((seq_count, head_count, tok_rows), jnp.float32),
    )
    running, denominator = lax.fori_loop(0, block_place + 1, pass_one, initial)
    log_total = running + jnp.log(denominator)

    def pass_two(block_number, numerator):
        key_pos = block_number * tok_rows + jnp.arange(tok_rows)
        scores, causal = block_scores(
            queries, key_block_at(key_all, block_number), query_pos, key_pos
        )
        probs_rounded = jnp.where(causal, jnp.exp(scores - log_total[..., None]), 0.0).astype(
            jnp.bfloat16
        )
        value_block = key_block_at(value_all, block_number)
        return numerator + jnp.einsum(
            "shqk,skhe->sqhe", probs_rounded, value_block, preferred_element_type=jnp.float32
        )

    heads_rows = lax.fori_loop(
        0, block_place + 1, pass_two, jnp.zeros((seq_count, tok_rows, head_count, HD), jnp.float32)
    )
    heads_rounded = heads_rows.reshape(seq_count, tok_rows, channels).astype(jnp.bfloat16)
    attended = jnp.einsum(
        "stc,cd->std", heads_rounded, dense_full, preferred_element_type=jnp.float32
    )
    hidden = jnp.einsum("std,df->stf", norm_two, fc1_full, preferred_element_type=jnp.float32)
    hidden = hidden + fc1_shift.astype(jnp.float32).reshape(-1)
    active = jax.nn.gelu(hidden, approximate=False).astype(jnp.bfloat16)
    partial_out = attended + jnp.einsum(
        "stf,fd->std", active, fc2_full, preferred_element_type=jnp.float32
    )
    summed = lax.psum_scatter(
        partial_out.astype(jnp.bfloat16), "tensor", scatter_dimension=2, tiled=True
    ).astype(jnp.float32)
    out_float = out_shift.astype(jnp.float32)
    bias_total = lax.dynamic_slice_in_dim(
        out_float[0] + out_float[1], tensor_place * width_part, width_part, 0
    )
    tokens_part = lax.dynamic_slice_in_dim(tokens_float, tensor_place * width_part, width_part, 2)
    output = (summed + tokens_part + bias_total).astype(jnp.bfloat16)
    gains_back, shifts_back, qkv_back, dense_back, fc1_back, fc2_back = (
        lax.all_gather(norm_gain, ("dp", "ctx"), axis=1, tiled=True),
        lax.all_gather(norm_bias, ("dp", "ctx"), axis=1, tiled=True),
        lax.all_gather(qkv_weight, ("dp", "ctx"), axis=0, tiled=True),
        lax.all_gather(dense_weight, ("dp", "ctx"), axis=1, tiled=True),
        lax.all_gather(fc1_weight, ("dp", "ctx"), axis=0, tiled=True),
        lax.all_gather(fc2_weight, ("dp", "ctx"), axis=1, tiled=True),
    )
    gain_back = gains_back.astype(jnp.float32)
    shift_back = shifts_back.astype(jnp.float32)
    key_all, value_all = (
        lax.all_gather(key_flat, "ctx", axis=1, tiled=True),
        lax.all_gather(value_flat, "ctx", axis=1, tiled=True),
    )
    grad_out = lax.all_gather(cotangent, "tensor", axis=2, tiled=True)
    bias_grad_row = jnp.sum(grad_out.astype(jnp.float32), axis=(0, 1))
    grad_out_bias = jnp.stack([bias_grad_row, bias_grad_row], axis=0)
    grad_fc2 = jnp.einsum("stf,std->fd", active, grad_out, preferred_element_type=jnp.float32)
    d_active = jnp.einsum("std,fd->stf", grad_out, fc2_back, preferred_element_type=jnp.float32)
    gelu_value, gelu_back = jax.vjp(lambda inner: jax.nn.gelu(inner, approximate=False), hidden)
    d_hidden = gelu_back(d_active)[0].astype(jnp.bfloat16)
    grad_fc1 = jnp.einsum("std,stf->df", norm_two, d_hidden, preferred_element_type=jnp.float32)
    grad_fc1_bias = jnp.sum(d_hidden.astype(jnp.float32), axis=(0, 1)).reshape(
        -1, fc1_shift.shape[1]
    )
    d_norm_two = jnp.einsum("stf,df->std", d_hidden, fc1_back, preferred_element_type=jnp.float32)
    grad_dense = jnp.einsum(
        "stc,std->cd", heads_rounded, grad_out, preferred_element_type=jnp.float32
    )
    d_heads = jnp.einsum(
        "std,cd->stc", grad_out, dense_back, preferred_element_type=jnp.float32
    ).astype(jnp.bfloat16)
    d_heads = d_heads.reshape(seq_count, tok_rows, head_count, HD)
    delta = jnp.transpose(jnp.sum(d_heads.astype(jnp.float32) * heads_rows, axis=-1), (0, 2, 1))
    length_all = key_all.shape[1]
    query_start = jnp.zeros((seq_count, tok_rows, head_count, HD), jnp.float32)

    def back_step(block_number, carried):
        d_query, d_keys_all, d_values_all = carried
        offset = block_number * tok_rows
        key_block = key_block_at(key_all, block_number)
        value_block = key_block_at(value_all, block_number)
        key_pos = offset + jnp.arange(tok_rows)
        probs_rounded, d_scores = score_grads(
            queries, key_block, value_block, d_heads, log_total, delta, query_pos, key_pos
        )
        d_query = (
            d_query
            + jnp.einsum("shqk,skhe->sqhe", d_scores, key_block, preferred_element_type=jnp.float32)
            * scale
        )
        d_key = (
            jnp.einsum("shqk,sqhe->skhe", d_scores, queries, preferred_element_type=jnp.float32)
            * scale
        )
        d_value = jnp.einsum(
            "shqk,sqhe->skhe", probs_rounded, d_heads, preferred_element_type=jnp.float32
        )
        d_keys_all = lax.dynamic_update_slice_in_dim(
            d_keys_all, d_key.reshape(seq_count, tok_rows, channels), offset, 1
        )
        d_values_all = lax.dynamic_update_slice_in_dim(
            d_values_all, d_value.reshape(seq_count, tok_rows, channels), offset, 1
        )
        return (d_query, d_keys_all, d_values_all)

    start_state = (
        query_start,
        jnp.zeros((seq_count, length_all, channels), jnp.float32),
        jnp.zeros((seq_count, length_all, channels), jnp.float32),
    )
    d_query, d_keys_all, d_values_all = lax.fori_loop(0, block_place + 1, back_step, start_state)
    d_key_own, d_value_own = (
        lax.psum_scatter(
            d_keys_all.astype(jnp.bfloat16), "ctx", scatter_dimension=1, tiled=True
        ).astype(jnp.float32),
        lax.psum_scatter(
            d_values_all.astype(jnp.bfloat16), "ctx", scatter_dimension=1, tiled=True
        ).astype(jnp.float32),
    )
    d_query_back = rotate(d_query, cosine, -sine_table).reshape(seq_count, tok_rows, channels)
    d_key_back = rotate(d_key_own.reshape(seq_count, tok_rows, head_count, HD), cosine, -sine_table)
    d_key_back = d_key_back.reshape(seq_count, tok_rows, channels)
    d_qkv = jnp.stack([d_query_back, d_key_back, d_value_own], axis=2).astype(jnp.bfloat16)
    grad_qkv = jnp.einsum("std,stce->dce", norm_one, d_qkv, preferred_element_type=jnp.float32)
    grad_qkv_bias = jnp.sum(d_qkv.astype(jnp.float32), axis=(0, 1)).reshape(3, head_count, HD)
    d_norm_one = jnp.einsum("stce,dce->std", d_qkv, qkv_back, preferred_element_type=jnp.float32)
    norm_value, back_one = jax.vjp(norm_rows, tokens_float, gain_back[0], shift_back[0])
    d_tokens_one, d_gain_one, d_shift_one = back_one(d_norm_one)
    norm_value, back_two = jax.vjp(norm_rows, tokens_float, gain_back[1], shift_back[1])
    d_tokens_two, d_gain_two, d_shift_two = back_two(d_norm_two)
    input_terms = lax.psum_scatter(
        (d_tokens_one + d_tokens_two).astype(jnp.bfloat16),
        "tensor",
        scatter_dimension=2,
        tiled=True,
    ).astype(jnp.float32)
    input_grad = input_terms + cotangent.astype(jnp.float32)
    grad_gain_part = jnp.stack([d_gain_one, d_gain_two], axis=0)
    grad_shift_part = jnp.stack([d_shift_one, d_shift_two], axis=0)
    owned = (
        lax.psum_scatter(
            grad_gain_part.astype(jnp.bfloat16), ("dp", "ctx"), scatter_dimension=1, tiled=True
        ).astype(jnp.float32),
        lax.psum_scatter(
            grad_shift_part.astype(jnp.bfloat16), ("dp", "ctx"), scatter_dimension=1, tiled=True
        ).astype(jnp.float32),
        lax.psum_scatter(
            grad_qkv.astype(jnp.bfloat16), ("dp", "ctx"), scatter_dimension=0, tiled=True
        ).astype(jnp.float32),
        lax.psum_scatter(
            grad_qkv_bias.astype(jnp.bfloat16), ("dp", "ctx"), scatter_dimension=2, tiled=True
        ).astype(jnp.float32),
        lax.psum_scatter(
            grad_dense.astype(jnp.bfloat16), ("dp", "ctx"), scatter_dimension=1, tiled=True
        ).astype(jnp.float32),
        lax.psum_scatter(
            grad_fc1.astype(jnp.bfloat16), ("dp", "ctx"), scatter_dimension=0, tiled=True
        ).astype(jnp.float32),
        lax.psum_scatter(
            grad_fc1_bias.astype(jnp.bfloat16), ("dp", "ctx"), scatter_dimension=1, tiled=True
        ).astype(jnp.float32),
        lax.psum_scatter(
            grad_fc2.astype(jnp.bfloat16), ("dp", "ctx"), scatter_dimension=1, tiled=True
        ).astype(jnp.float32),
        lax.psum_scatter(
            grad_out_bias.astype(jnp.bfloat16), ("dp", "ctx"), scatter_dimension=1, tiled=True
        ).astype(jnp.float32),
    )
    grad_norm_gain, grad_norm_bias = lax.psum((owned[0], owned[1]), "tensor")
    return (
        output,
        input_grad,
        grad_norm_gain,
        grad_norm_bias,
        owned[2],
        owned[3],
        owned[4],
        owned[5],
        owned[6],
        owned[7],
        owned[8],
    )


def solution(mesh):
    return jax.shard_map(
        shards,
        mesh=mesh,
        in_specs=(
            P("dp", "ctx", None),
            P(None, ("dp", "ctx")),
            P(None, ("dp", "ctx")),
            P(("dp", "ctx"), None, "tensor"),
            P(None, "tensor", ("dp", "ctx")),
            P("tensor", ("dp", "ctx")),
            P(("dp", "ctx"), "tensor"),
            P("tensor", ("dp", "ctx")),
            P("tensor", ("dp", "ctx")),
            P(None, ("dp", "ctx")),
            P("dp", "ctx", "tensor"),
        ),
        out_specs=(
            P("dp", "ctx", "tensor"),
            P("dp", "ctx", "tensor"),
            P(None, ("dp", "ctx")),
            P(None, ("dp", "ctx")),
            P(("dp", "ctx"), None, "tensor"),
            P(None, "tensor", ("dp", "ctx")),
            P("tensor", ("dp", "ctx")),
            P(("dp", "ctx"), "tensor"),
            P("tensor", ("dp", "ctx")),
            P("tensor", ("dp", "ctx")),
            P(None, ("dp", "ctx")),
        ),
        check_vma=False,
    )
```

profile of v0, /device:TPU:0, one launch (start us, length us, event | category | flops | bytes accessed | tf_op | source)
XLA Modules:
  0.0 1375.6 jit_solution(1733612472840033446)
XLA Ops:
  7.3 1.4 convert_reduce_fusion
  8.7 1.5 multiply_reduce_fusion
  10.2 68.7 %all-gather.1 = bf16[32,24,2]{1,2,0:T(2,128)(2,1)S(1)} all-gather(bf16[1,24,2]{1,2,0:T(2,128)(2,1)S(1)} %bitcast.362), channel_id=1, replica_groups=mesh['dp'=4,'tensor'=4,'ctx'=8] {'dp','ctx'}, dimensions={0}, use_global_device_ids=true | all-gather | bytes 3168 | tf_op jit(solution)/shard_map/all_gather | solution.py:78
  79.9 70.9 %all-gather.2 = bf16[32,24,2]{1,2,0:T(2,128)(2,1)S(1)} all-gather(bf16[1,24,2]{1,2,0:T(2,128)(2,1)S(1)} %bitcast.363), channel_id=1, replica_groups=mesh['dp'=4,'tensor'=4,'ctx'=8] {'dp','ctx'}, dimensions={0}, use_global_device_ids=true | all-gather | bytes 3168 | tf_op jit(solution)/shard_map/all_gather | solution.py:79
  151.7 78.1 %all_gather.45 = bf16[768,3,192]{2,0,1:T(8,128)(2,1)S(1)} all-gather(bf16[24,3,192]{2,0,1:T(8,128)(2,1)S(1)} %copy-done.13), channel_id=1, replica_groups=mesh['dp'=4,'tensor'=4,'ctx'=8] {'dp','ctx'}, dimensions={0}, use_global_device_ids=true | all-gather | bytes 912384 | tf_op jit(solution)/shard_map/all_gather | solution.py:80
  229.8 71.3 %all_gather.46 = bf16[3,3,64]{1,0,2:T(4,128)(2,1)S(1)} all-gather(bf16[3,3,2]{1,0,2:T(4,128)(2,1)S(1)} %copy.71), channel_id=1, replica_groups=mesh['dp'=4,'tensor'=4,'ctx'=8] {'dp','ctx'}, dimensions={2}, use_global_device_ids=true | all-gather | bytes 1188 | tf_op jit(solution)/shard_map/all_gather | solution.py:81
  301.3 1.0 fusion.44
  302.3 1.0 copy-done.5
  305.0 1.7 slice.130
  308.1 14.4 %all_gather.54 = bf16[1,512,768]{1,2,0:T(8,128)(2,1)S(1)} all-gather(bf16[1,512,192]{1,2,0:T(8,128)(2,1)S(1)} %copy-done.6), channel_id=1, replica_groups=mesh['dp'=4,'tensor'=4,'ctx'=8] {'tensor'}, dimensions={2}, use_global_device_ids=true | all-gather | bytes 983040 | tf_op jit(solution)/shard_map/all_gather | solution.py:185
  322.5 75.5 %all_gather.49 = bf16[192,768]{0,1:T(8,128)(2,1)S(1)} all-gather(bf16[192,24]{0,1:T(8,128)(2,1)S(1)} %copy-done.31), channel_id=1, replica_groups=mesh['dp'=4,'tensor'=4,'ctx'=8] {'dp','ctx'}, dimensions={1}, use_global_device_ids=true | all-gather | bytes 304128 | tf_op jit(solution)/shard_map/all_gather | solution.py:82
  398.4 2.7 while.39
  398.7 0.9 constant_dynamic-slice_fusion.12
  401.2 10.7 all-gather.16.cloned.1.call-done
  411.9 2.5 while.40
  411.9 1.1 constant_dynamic-slice_fusion.13
  413.2 1.1 fusion.124
  414.5 1.3 broadcast.396
  415.8 1.4 broadcast.396.clone
  417.2 6.7 while.41
  417.2 0.9 constant_dynamic-slice_fusion.14
  418.8 0.9 constant_dynamic-slice_fusion.15
  420.0 1.2 fusion.136
  421.8 0.8 fusion.138
  422.7 0.9 bitcast_dynamic-update-slice_fusion.3
  424.7 134.3 %all-gather.3 = bf16[32,2,12]{2,1,0:T(2,128)(2,1)S(1)} all-gather(bf16[1,2,12]{2,1,0:T(2,128)(2,1)S(1)} %bitcast.364), channel_id=1, replica_groups=mesh['dp'=4,'tensor'=4,'ctx'=8] {'dp','ctx'}, dimensions={0}, use_global_device_ids=true | all-gather | bytes 1584 | tf_op jit(solution)/shard_map/all_gather | solution.py:84
  559.1 6.8 multiply_convert_fusion
  565.9 1.1 convolution_convert_fusion.3
  567.1 1.6 fusion.74
  568.7 8.9 all-gather.14.cloned.1.call-done
  577.6 3.7 fusion.45
  581.3 3.5 copy.89
  584.9 1.1 copy.107
  586.1 4.1 fusion.73
  590.2 2.0 convolution_convert_fusion.1
  592.3 0.8 copy.76
  593.2 1.3 convert_element_type.213
  596.5 67.2 %all-gather.4 = bf16[32,24,2]{1,2,0:T(2,128)(2,1)S(1)} all-gather(bf16[1,24,2]{1,2,0:T(2,128)(2,1)S(1)} %bitcast.365), channel_id=1, replica_groups=mesh['dp'=4,'tensor'=4,'ctx'=8] {'dp','ctx'}, dimensions={0}, use_global_device_ids=true | all-gather | bytes 3168 | tf_op jit(solution)/shard_map/all_gather | solution.py:86
  664.7 3.0 convolution_convert_fusion
  668.4 3.7 fusion.72
  672.1 1.0 convert.80
  673.2 0.9 slice.106
  674.9 57.7 %reduce-scatter.19.cloned.1.call-done = bf16[1,512,192]{1,2,0:T(8,128)(2,1)} async-done(((bf16[1,4096,192]{1,2,0:T(8,128)(2,1)}), bf16[1,512,192]{1,2,0:T(8,128)(2,1)}) %reduce-scatter.19.cloned.1.call-update) | async-done | bytes 196624 | tf_op jit(solution)/shard_map/reduce_scatter | solution.py:247
  732.6 2.9 fusion.38
  735.6 2.1 fusion.36
  738.3 2.1 convolution_convert_fusion.2
  740.7 2.3 add_convert_fusion
  743.0 2.9 copy.91
  746.0 2.5 copy.106
  748.5 0.8 dynamic-slice_add_fusion
  749.4 128.5 %reduce-scatter.21.cloned.1.call-done = bf16[192,24]{0,1:T(8,128)(2,1)} async-done(((bf16[192,768]{0,1:T(8,128)(2,1)}), bf16[192,24]{0,1:T(8,128)(2,1)}) %reduce-scatter.21.cloned.1.call-update) | async-done | bytes 9232 | tf_op jit(solution)/shard_map/reduce_scatter | solution.py:284
  878.0 1.3 convert_element_type.244
  879.3 27.6 %reduce-scatter.27.cloned.1.call-done = bf16[192,512]{1,0:T(8,128)(2,1)} async-done(((bf16[768,512]{1,0:T(8,128)(2,1)}), bf16[192,512]{1,0:T(8,128)(2,1)}) %reduce-scatter.27.cloned.1.call-update) | async-done | bytes 196624
  906.9 1.1 reshape_bitcast_fusion.1
  908.4 1.3 add_convert_fusion.5
  910.6 143.7 %reduce-scatter.23.cloned.1.call-done = bf16[24,768]{1,0:T(8,128)(2,1)} async-done(((bf16[768,768]{1,0:T(8,128)(2,1)}), bf16[24,768]{1,0:T(8,128)(2,1)}) %reduce-scatter.23.cloned.1.call-update) | async-done | bytes 36880 | tf_op jit(solution)/shard_map/reduce_scatter | solution.py:287
  1054.4 1.4 convert_element_type.246
  1055.8 149.5 %reduce-scatter.25.cloned.1.call-done = bf16[768,24]{0,1:T(8,128)(2,1)} async-done(((bf16[768,768]{0,1:T(8,128)(2,1)}), bf16[768,24]{0,1:T(8,128)(2,1)}) %reduce-scatter.25.cloned.1.call-update) | async-done | bytes 36880 | tf_op jit(solution)/shard_map/reduce_scatter | solution.py:293
  1205.2 1.4 convert_element_type.250
  1207.3 144.1 %all-reduce.7 = (bf16[2,768]{1,0:T(2,128)(2,1)S(1)}, bf16[2,768]{1,0:T(2,128)(2,1)S(1)}, bf16[3,3,64]{1,0,2:T(4,128)(2,1)S(1)}, bf16[12,64]{1,0:T(8,128)(2,1)S(1)}, bf16[2,768]{1,0:T(2,128)(2,1)S(1)}) all-reduce(bf16[2,768]{1,0:T(2,128)(2,1)S(1)} %pad_maximum_fusion.5, ...), channel_id=7, replica_groups=mesh['dp'=4,'tensor'=4,'ctx'=8] {'dp','ctx'}, use_global_device_ids=true, to_apply=%region_21.22.clone | all-reduce | flops 5952 | bytes 23808
  1352.8 11.3 all-reduce.6
  1364.8 1.4 dynamic-slice_convert_fusion
  1366.2 1.1 reshape_bitcast_fusion
  1367.8 0.9 copy.80
  (212 shorter events, 19.0 us)
Async XLA Ops:
  7.2 3.0 copy-start.44
  7.2 72.7 %copy-start.45 = (bf16[2,24]{1,0:T(2,128)(2,1)S(1)}, bf16[2,24]{1,0:T(2,128)(2,1)}, u32[]{:S(2)}) copy-start(bf16[2,24]{1,0:T(2,128)(2,1)} %param.19) | copy-start | bytes 292
  7.2 144.5 %copy-start.13 = (bf16[24,3,192]{2,0,1:T(8,128)(2,1)S(1)}, bf16[24,3,192]{2,0,1:T(8,128)(2,1)}, u32[]{:S(2)}) copy-start(bf16[24,3,192]{2,0,1:T(8,128)(2,1)} %param.20) | copy-start | bytes 82948
  7.2 222.6 %copy-start.43 = (bf16[3,3,2]{1,2,0:T(2,128)(2,1)S(1)}, bf16[3,3,2]{1,2,0:T(2,128)(2,1)}, u32[]{:S(2)}) copy-start(bf16[3,3,2]{1,2,0:T(2,128)(2,1)} %param.21) | copy-start | bytes 112
  7.2 391.2 %all-gather.10.cloned.1.call-start = ((), (), s32[]{:S(2)}) async-start(), calls=%async_computation.7 | async-start | bytes 1769472 | tf_op jit(solution)/shard_map/all_gather | solution.py:109
  7.3 294.0 %copy-start = (bf16[1,512,768]{2,1,0:T(8,128)(2,1)S(1)}, bf16[1,512,768]{2,1,0:T(8,128)(2,1)}, u32[]{:S(2)}) copy-start(bf16[1,512,768]{2,1,0:T(8,128)(2,1)} %param.17) | copy-start | bytes 2359300
  8.7 292.6 %copy-start.19 = (f32[512]{0:T(512)}, f32[512]{0:T(512)S(1)}, u32[]{:S(2)}) copy-start(f32[512]{0:T(512)S(1)} %broadcast_multiply_fusion) | copy-start | bytes 6148
  10.2 68.9 %copy-start.29 = (f32[512]{0:T(512)}, f32[512]{0:T(512)S(1)}, u32[]{:S(2)}) copy-start(f32[512]{0:T(512)S(1)} %multiply_reduce_fusion) | copy-start | bytes 6148
  10.2 291.1 %copy-start.23 = (f32[512]{0:T(512)}, f32[512]{0:T(512)S(1)}, u32[]{:S(2)}) copy-start(f32[512]{0:T(512)S(1)} %fusion.57) | copy-start | bytes 6148
  79.9 221.5 %copy-start.17 = (f32[768]{0:T(1024)}, f32[768]{0:T(1024)S(1)}, u32[]{:S(2)}) copy-start(f32[768]{0:T(1024)S(1)} %get-tuple-element.299) | copy-start | bytes 9220
  151.7 149.6 %copy-start.37 = (f32[768]{0:T(1024)}, f32[768]{0:T(1024)S(1)}, u32[]{:S(2)}) copy-start(f32[768]{0:T(1024)S(1)} %get-tuple-element.301) | copy-start | bytes 9220
  229.8 72.5 %copy-start.2 = (bf16[768,3,192]{2,0,1:T(8,128)(2,1)}, bf16[768,3,192]{2,0,1:T(8,128)(2,1)S(1)}, u32[]{:S(2)}) copy-start(bf16[768,3,192]{2,0,1:T(8,128)(2,1)S(1)} %all_gather.45) | copy-start | bytes 2654212
  302.3 1.0 copy-start.5
  303.3 4.8 copy-start.6
  303.4 19.1 %copy-start.31 = (bf16[192,24]{0,1:T(8,128)(2,1)S(1)}, bf16[192,24]{0,1:T(8,128)(2,1)}, u32[]{:S(2)}) copy-start(bf16[192,24]{0,1:T(8,128)(2,1)} %param.22) | copy-start | bytes 27652
  304.9 106.9 %all-gather.16.cloned.1.call-start = ((), (), s32[]{:S(2)}) async-start(), calls=%async_computation.15 | async-start | bytes 1769472 | tf_op jit(solution)/shard_map/all_gather | solution.py:110
  306.7 252.4 %all-gather.12.cloned.1.call-start = ((), (), s32[]{:S(2)}) async-start(), calls=%async_computation.8 | async-start | bytes 1216512 | tf_op jit(solution)/shard_map/all_gather | solution.py:83
  307.5 270.2 %all-gather.14.cloned.1.call-start = ((), (), s32[]{:S(2)}) async-start(), calls=%async_computation.9 | async-start | bytes 1216512 | tf_op jit(solution)/shard_map/all_gather | solution.py:85
  308.0 364.1 %reduce-scatter.17.cloned.1.call-start = ((), (), s32[]{:S(2)}) async-start(), calls=%async_computation.10 | async-start | bytes 1769472 | tf_op jit(solution)/shard_map/reduce_scatter | solution.py:244
  414.4 1.4 copy-start.35
  418.2 1.8 copy-start.36
  423.9 0.7 copy-start.46
  424.0 135.2 %copy-start.14 = (f32[768]{0:T(1024)S(1)}, f32[768]{0:T(1024)}, u32[]{:S(2)}) copy-start(f32[768]{0:T(1024)} %get-tuple-element.298) | copy-start | bytes 9220
  424.0 135.1 %copy-start.20 = (f32[512]{0:T(512)S(1)}, f32[512]{0:T(512)}, u32[]{:S(2)}) copy-start(f32[512]{0:T(512)} %copy-done.19) | copy-start | bytes 6148
  424.0 135.1 %copy-start.24 = (f32[512]{0:T(512)S(1)}, f32[512]{0:T(512)}, u32[]{:S(2)}) copy-start(f32[512]{0:T(512)} %copy-done.23) | copy-start | bytes 6148
  424.0 135.1 %copy-start.39 = (f32[768]{0:T(1024)S(1)}, f32[768]{0:T(1024)}, u32[]{:S(2)}) copy-start(f32[768]{0:T(1024)} %get-tuple-element.300) | copy-start | bytes 9220
  424.0 308.5 %reduce-scatter.19.cloned.1.call-start = ((), (), s32[]{:S(2)}) async-start(), calls=%async_computation.11 | async-start | bytes 1769472 | tf_op jit(solution)/shard_map/reduce_scatter | solution.py:247
  424.6 453.4 %reduce-scatter.21.cloned.1.call-start = ((), (), s32[]{:S(2)}) async-start(), calls=%async_computation.12 | async-start | bytes 405504 | tf_op jit(solution)/shard_map/reduce_scatter | solution.py:284
  567.1 339.8 %reduce-scatter.27.cloned.1.call-start = ((), (), s32[]{:S(2)}) async-start(), calls=%async_computation.16 | async-start | bytes 983040
  586.0 468.4 %reduce-scatter.23.cloned.1.call-start = ((), (), s32[]{:S(2)}) async-start(), calls=%async_computation.13 | async-start | bytes 1216512 | tf_op jit(solution)/shard_map/reduce_scatter | solution.py:287
  586.0 4.1 copy-start.15
  586.1 4.1 copy-start.21
  586.1 4.1 copy-start.25
  586.1 4.1 copy-start.40
  590.2 2.1 copy-start.50
  590.2 2.1 copy-start.7
  592.2 613.0 %reduce-scatter.25.cloned.1.call-start = ((), (), s32[]{:S(2)}) async-start(), calls=%async_computation.14 | async-start | bytes 1216512 | tf_op jit(solution)/shard_map/reduce_scatter | solution.py:293
  593.2 1.5 copy-start.49
  593.2 3.4 copy-start.47
  664.7 3.7 copy-start.48
  667.7 697.0 %all-reduce.10.cloned.1.call-start = ((), (), s32[]{:S(2)}) async-start(), calls=%async_computation.18 | async-start | bytes 2359296
  668.4 5.7 copy-start.12
  672.0 60.5 %copy-start.3 = (bf16[768,3,192]{2,0,1:T(8,128)(2,1)S(1)}, bf16[768,3,192]{2,0,1:T(8,128)(2,1)}, u32[]{:S(2)}) copy-start(bf16[768,3,192]{2,0,1:T(8,128)(2,1)} %copy-done.2) | copy-start | bytes 2654212
  732.6 2.9 copy-start.30
  732.6 3.0 copy-start.1
  732.6 3.0 copy-start.16
  732.6 3.0 copy-start.18
  732.6 3.0 copy-start.22
  732.6 3.0 copy-start.26
  735.5 2.2 copy-start.27
  735.5 2.2 copy-start.28
  735.6 2.7 copy-start.8
  735.6 2.7 copy-start.9
  735.6 2.7 copy-start.10
  735.6 2.7 copy-start.38
  740.4 625.7 %reduce-scatter.29.cloned.1.call-start = ((), (), s32[]{:S(2)}) async-start(), calls=%async_computation.17 | async-start | bytes 983040
  745.9 3.4 copy-start.42
  745.9 3.4 copy-start.41
  748.5 458.1 %copy-start.11 = (bf16[1,512,192]{1,2,0:T(8,128)(2,1)S(1)}, bf16[1,512,192]{1,2,0:T(8,128)(2,1)}, u32[]{:S(2)}) copy-start(bf16[1,512,192]{1,2,0:T(8,128)(2,1)} %reduce-scatter.19.cloned.1.call-done) | copy-start | bytes 589828
  909.8 297.4 %copy-start.34 = (bf16[768]{0:T(1024)(128)(2,1)S(1)}, bf16[768]{0:T(1024)(128)(2,1)}, u32[]{:S(2)}) copy-start(bf16[768]{0:T(1024)(128)(2,1)} %get-tuple-element.290) | copy-start | bytes 4612
  909.8 297.4 %copy-start.33 = (bf16[768]{0:T(1024)(128)(2,1)S(1)}, bf16[768]{0:T(1024)(128)(2,1)}, u32[]{:S(2)}) copy-start(bf16[768]{0:T(1024)(128)(2,1)} %get-tuple-element.295) | copy-start | bytes 4612
  909.8 297.5 %copy-start.32 = (bf16[2,768]{1,0:T(2,128)(2,1)S(1)}, bf16[2,768]{1,0:T(2,128)(2,1)}, u32[]{:S(2)}) copy-start(bf16[2,768]{1,0:T(2,128)(2,1)} %pad_maximum_fusion.7) | copy-start | bytes 9220
  1206.9 160.8 %copy-start.4 = (bf16[1,512,192]{2,1,0:T(8,128)(2,1)S(1)}, bf16[1,512,192]{2,1,0:T(8,128)(2,1)}, u32[]{:S(2)}) copy-start(bf16[1,512,192]{2,1,0:T(8,128)(2,1)} %copy.76) | copy-start | bytes 589828
Sparse Core Ops, SparseCore 0:
  305.1 56.0 all-gather.9
  363.9 47.9 all-gather.15
  413.5 79.1 all-gather.11
  494.2 83.3 all-gather.13
  581.2 74.7 reduce-scatter.16
  659.9 72.6 reduce-scatter.18
  735.5 142.4 reduce-scatter.20
  880.5 26.3 reduce-scatter.26
  909.3 144.9 reduce-scatter.22
  1056.6 148.6 reduce-scatter.24
  1208.9 108.6 all-reduce.9
  1320.0 22.1 reduce-scatter.28
where the time goes:
time: 1380 us
  blocking collectives  736 us (53%)
  waiting for transfers between devices  528 us (38%)
  matrix products  37.9 us (3%)
  local copies, waits for them, and re-layouts  32.4 us (2%)
  other arithmetic  23.7 us (2%)
  between operations  16.4 us (1%)
    reduce_scatter x1, waiting for transfers between devices, shards(): lax.psum_scatter(grad_fc2.astype(jnp.bfloat16), ('dp', 'ctx'), scatter_di...  149 us
    unnamed x1, blocking collectives  144 us
    reduce_scatter x1, waiting for transfers between devices, shards(): lax.psum_scatter(grad_fc1.astype(jnp.bfloat16), ('dp', 'ctx'), scatter_di...  144 us
    all_gather x1, blocking collectives, shards(): lax.all_gather(fc1_bias, ('dp', 'ctx'), axis=1, tiled=True)  134 us
    reduce_scatter x1, waiting for transfers between devices, shards(): lax.psum_scatter(grad_dense.astype(jnp.bfloat16), ('dp', 'ctx'), scatter_...  129 us
    all_gather x1, blocking collectives, shards(): lax.all_gather(qkv_weight, ('dp', 'ctx'), axis=0, tiled=True)  78.1 us
    all_gather x1, blocking collectives, shards(): lax.all_gather(dense_weight, ('dp', 'ctx'), axis=1, tiled=True)  75.5 us
    all_gather x1, blocking collectives, shards(): lax.all_gather(qkv_bias, ('dp', 'ctx'), axis=2, tiled=True)  71.3 us
  transfers between devices with their start and end apart: 12, of which 7 were waited for; matrix products, arithmetic and copies ran while one was open for 6% of the time, Pallas kernels for 0%

commit v1 on v0

v1 whole, which is shorter than its diff:
```python
import jax
import jax.numpy as jnp
import numpy as np
from jax import lax
from jax.experimental import pallas as pl
from jax.experimental.pallas import tpu as pltpu
from jax.sharding import PartitionSpec as P

HD = 64
ROT = 16
EPSILON = 1e-05
ROWS = 512
WIDE = 768
HALF = 1280
PART = 192
TILE = 128
MESH = pl.DeviceIdType.MESH
VMEM_LIMIT = 60 << 20
F32 = jnp.float32
BF16 = jnp.bfloat16

QKV = slice(0, 640)
DENSE = slice(640, 896)
FC1 = slice(896, 1664)
FC2 = slice(1664, 2432)


def dot(a, b):
    return lax.dot_general(a, b, (((1,), (0,)), ((), ())), preferred_element_type=F32)


def dot_nt(a, b):
    return lax.dot_general(a, b, (((1,), (1,)), ((), ())), preferred_element_type=F32)


def dot_tn(a, b):
    return lax.dot_general(a, b, (((0,), (0,)), ((), ())), preferred_element_type=F32)


def place():
    dp = lax.axis_index("dp")
    cx = lax.axis_index("ctx")
    return dp // 2, dp % 2, cx // 4, cx % 4, lax.axis_index("tensor")


def device(x, y, z, core):
    return {"dp": (x % 2) * 2 + core, "ctx": (x // 2) * 4 + z, "tensor": y}


class Links:
    def __init__(self, send, recv):
        self.xlo, self.core, self.xhi, self.z, self.y = place()
        self.x = self.xhi * 2 + self.xlo
        self.send, self.recv, self.used = send, recv, 0

    def at_x(self, step):
        return device((self.x + step) % 4, self.y, self.z, self.core)

    def at_z(self, step):
        return device(self.x, self.y, (self.z + step) % 4, self.core)

    def at_y(self, step):
        return device(self.x, (self.y + step) % 4, self.z, self.core)

    def twin(self):
        return device(self.x, self.y, self.z, 1 - self.core)

    def greet(self):
        barrier = pltpu.get_barrier_semaphore()
        peers = [self.twin()]
        for step in (1, 2, 3):
            peers += [self.at_x(step), self.at_z(step), self.at_y(step)]
        for peer in peers:
            pl.semaphore_signal(barrier, inc=1, device_id=peer, device_id_type=MESH)
        pl.semaphore_wait(barrier, len(peers))

    def copy(self, source, target, peer):
        number = self.used
        self.used += 1
        return pltpu.make_async_remote_copy(
            src_ref=source,
            dst_ref=target,
            send_sem=self.send.at[number],
            recv_sem=self.recv.at[number],
            device_id=peer,
            device_id_type=MESH,
        )


def start(copies):
    for item in copies:
        item.start()


def wait(copies):
    for item in copies:
        item.wait()


def lanes(shape):
    return lax.broadcasted_iota(jnp.int32, shape, len(shape) - 1)


def low_half(tile):
    return jnp.where(lanes(tile.shape) < HD, tile, 0.0)


def high_half(tile):
    return jnp.where(lanes(tile.shape) >= HD, tile, 0.0)


def swap_halves(tile):
    return pltpu.roll(tile, HD, axis=1)


def turn(tile, cosine, sine_up, sine_down):
    return (
        tile * cosine
        + pltpu.roll(tile, ROT // 2, axis=1) * sine_up
        + pltpu.roll(tile, TILE - ROT // 2, axis=1) * sine_down
    )


def fold(block):
    rows, width = block.shape
    return jnp.sum(block.reshape(rows // 8, 8, width), axis=0)


def standardize(rows_in):
    values = rows_in.astype(F32)
    centred = values - jnp.mean(values, axis=-1, keepdims=True)
    scale = lax.rsqrt(jnp.mean(centred * centred, axis=-1, keepdims=True) + EPSILON)
    return centred * scale, scale


def norm_back(gradient, xhat, scale):
    return scale * (
        gradient
        - jnp.mean(gradient, axis=-1, keepdims=True)
        - xhat * jnp.mean(gradient * xhat, axis=-1, keepdims=True)
    )


def front_kernel(
    pack, cot, tok, cosine, sine_up, sine_down, perm,
    wq, qz, zd, kv, mlp, dx2, g12, srow, n1, cotb, small,
    slots, w2, n2, dhid, act, xhat, rstd, bias, send, recv,
):
    net = Links(send, recv)
    xlo, core, xhi, z, y = net.xlo, net.core, net.xhi, net.z, net.y
    own = ((xlo * 2 + core) * 2 + xhi) * 4 + z
    block = xhi * 4 + z
    net.greet()
    first_a = [
        net.copy(pack.at[:, 0:640], slots.at[own, :, 0:640], net.at_z(step)) for step in (1, 2, 3)
    ]
    first_b = [
        net.copy(pack.at[:, 640:HALF], slots.at[own, :, 640:HALF], net.at_x(step))
        for step in (1, 2, 3)
    ]
    gather_y = [net.copy(cot, cotb.at[y], net.at_y(step)) for step in (1, 2, 3)]
    start(first_a + first_b + gather_y)
    slots[own] = pack[...]
    cotb[y] = cot[...]

    @pl.loop(0, 4)
    def _(index):
        rows = pl.ds(pl.multiple_of(index * TILE, TILE), TILE)
        normed, scale = standardize(tok[rows, :])
        xhat[rows, :] = normed
        rstd[rows, :] = jnp.broadcast_to(scale, (TILE, TILE))

    wait(first_a)
    four = pl.ds(own - z, 4)
    second_a = [
        net.copy(slots.at[four, :, 0:640], slots.at[four, :, 0:640], net.at_x(step))
        for step in (1, 2, 3)
    ]
    start(second_a)
    wait(first_b)
    second_b = []
    for low in (0, 1):
        for high in (0, 1):
            slot = ((low * 2 + core) * 2 + high) * 4 + z
            piece = slots.at[slot, :, 640:HALF]
            second_b += [net.copy(piece, piece, net.at_z(step)) for step in (1, 2, 3)]
    start(second_b)
    wait(second_a)
    third_a, third_b = [], []
    for low in (0, 1):
        eight = pl.ds((low * 2 + core) * 8, 8)
        piece = slots.at[eight, :, 0:640]
        third_a.append(net.copy(piece, piece, net.twin()))
    start(third_a)
    wait(second_b)
    for low in (0, 1):
        eight = pl.ds((low * 2 + core) * 8, 8)
        piece = slots.at[eight, :, 640:HALF]
        third_b.append(net.copy(piece, piece, net.twin()))
    start(third_b)
    wait(third_a)

    def unpack(source, left, right):
        @pl.loop(0, 16)
        def _(pair):
            rows = pl.ds(pl.multiple_of(pair * 48, 16), 48)
            one = slots[2 * pair, :, source].astype(F32)
            two = slots[2 * pair + 1, :, source].astype(F32)
            width = right.stop - right.start
            w2[rows, left] = jnp.concatenate([one[0:24], two[0:24]], axis=0).astype(BF16)
            w2[rows, right] = jnp.concatenate(
                [one[24:48, 0:width], two[24:48, 0:width]], axis=0
            ).astype(BF16)

    unpack(slice(0, 640), slice(0, 640), slice(1280, 1920))
    turned = w2[:, 512:640].astype(F32).T
    small[...] = turned[64:80, :]
    spread = dot(turned[64:80, :].astype(BF16), perm[...])
    lane = lanes((1, 640))
    inner = lane % TILE
    bias[0:1, 0:640] = jnp.where(
        lane >= 384, spread[7:8, 0:640], jnp.where(inner < HD, spread[8:9, 0:640], spread[9:10, 0:640])
    )
    bias[1:2, :] = spread[6:7, 640:1408]

    @pl.loop(0, 4)
    def _(index):
        rows = pl.ds(pl.multiple_of(index * TILE, TILE), TILE)
        normed = xhat[rows, :]
        one = (normed * small[0:1, :] + small[2:3, :]).astype(BF16)
        n1[rows, :] = one
        n2[rows, :] = (normed * small[1:2, :] + small[3:4, :]).astype(BF16)
        projected = dot(one, w2[:, QKV]) + bias[0:1, 0:640]
        turning = (cosine[rows, :], sine_up[rows, :], sine_down[rows, :])
        for head in range(3):
            span = slice(head * TILE, head * TILE + TILE)
            kv[block, rows, span] = turn(projected[:, span], *turning).astype(BF16)
        pair, last = projected[:, 384:512], projected[:, 512:640]
        for head, tile in enumerate((pair, swap_halves(pair), last)):
            span = slice(head * TILE, head * TILE + TILE)
            qz[rows, span] = (low_half(turn(low_half(tile), *turning)) * 0.125).astype(BF16)

    mine = kv.at[block]
    across = net.copy(mine, mine, net.at_x(2))
    inside = [net.copy(mine, mine, net.at_z(step)) for step in (1, 2, 3)]
    prior = kv.at[z]
    before = [net.copy(prior, prior, net.at_z(step)) for step in (1, 2, 3)]

    @pl.when(xhi == 0)
    def _():
        across.start()

    for step in (1, 2, 3):
        pl.when(z + step <= 3)(inside[step - 1].start)

    wait(third_b)
    unpack(slice(640, HALF), slice(640, 1280), slice(1920, 2432))
    wq[...] = w2[:, 0:896]
    wait(gather_y)
    srow[...] = jnp.zeros_like(srow)

    @pl.when(xhi == 1)
    def _():
        across.wait_recv()
        start(before)

    @pl.loop(0, 4)
    def _(index):
        rows = pl.ds(pl.multiple_of(index * TILE, TILE), TILE)
        hidden = dot(n2[rows, :], w2[:, FC1]) + bias[1:2, :]
        spread_to = 0.5 + 0.5 * lax.erf(hidden * (0.5**0.5))
        active = (hidden * spread_to).astype(BF16)
        act[rows, :] = active
        slope = spread_to + hidden * jnp.exp(-0.5 * hidden * hidden) * 0.3989422804014327
        d_active = 0.0
        d_heads = 0.0
        for part in range(4):
            span = slice(part * PART, part * PART + PART)
            piece = cotb[part, rows, :]
            d_active = d_active + dot(piece, w2[span, FC2])
            d_heads = d_heads + dot(piece, w2[span, DENSE])
            mlp[part, rows, :] = dot_nt(active, w2[span, FC2])
        d_hidden = (slope * d_active).astype(BF16)
        dhid[rows, :] = d_hidden
        d_norm = dot_nt(d_hidden, w2[:, FC1])
        normed = xhat[rows, :]
        dx2[rows, :] = norm_back(small[1:2, :] * d_norm, normed, rstd[rows, 0:1])
        srow[0:8, :] += fold(d_norm * normed)
        srow[8:16, :] += fold(d_norm)
        srow[16:24, :] += fold(d_hidden.astype(F32))
        pair, last = d_heads[:, 0:TILE], d_heads[:, TILE : 2 * TILE]
        for head, tile in enumerate((swap_halves(pair), pair, swap_halves(last))):
            zd[rows, head * TILE : head * TILE + TILE] = high_half(tile).astype(BF16)

    for half in (0, 1):
        span = slice(half * 384, half * 384 + 384)
        g12[span, 0:WIDE] = dot_tn(n2[:, span], dhid[...]).astype(BF16)
    for part in range(4):
        span = slice(part * PART, part * PART + PART)
        g12[span, WIDE : 2 * WIDE] = dot_tn(cotb[part], act[...]).astype(BF16)

    @pl.when(xhi == 0)
    def _():
        across.wait_send()

    for step in (1, 2, 3):
        pl.when(z + step <= 3)(inside[step - 1].wait_send)
        pl.when(z - step >= 0)(inside[step - 1].wait_recv)

    @pl.when(xhi == 1)
    def _():
        wait(before)


def attention_kernel(
    qz, zd, kv, heads, dq, dkv, scores, weights, turned_kv, kept, d_query, limits, totals, summed
):
    block = lax.axis_index("ctx")

    @pl.loop(0, 3)
    def _(head):
        span = pl.ds(pl.multiple_of(head * TILE, TILE), TILE)
        query = qz[:, span]
        query_t = query.astype(F32).T.astype(BF16)

        def score(index, masked):
            tile = kv[index, :, span]
            value = dot(tile, query_t)
            if masked:
                key_at = lax.broadcasted_iota(jnp.int32, value.shape, 0)
                query_at = lax.broadcasted_iota(jnp.int32, value.shape, 1)
                value = jnp.where(key_at <= query_at, value, -1e30)
            scores[index] = value
            turned_kv[index] = tile.astype(F32).T.astype(BF16)
            limits[...] = jnp.maximum(
                limits[...], jnp.max(value.reshape(ROWS // 8, 8, ROWS), axis=0)
            )

        limits[...] = jnp.full_like(limits, -1e30)

        @pl.loop(0, block)
        def _(index):
            score(index, False)

        score(block, True)
        top = jnp.max(limits[...], axis=0, keepdims=True)
        totals[...] = jnp.zeros_like(totals)
        summed[...] = jnp.zeros_like(summed)

        @pl.loop(0, block + 1)
        def _(index):
            unnormed = jnp.exp(scores[index] - top)
            totals[...] += fold(unnormed)
            rounded = unnormed.astype(BF16)
            weights[index] = rounded
            summed[...] += dot(turned_kv[index], rounded)

        inverse = 1.0 / jnp.sum(totals[...], axis=0, keepdims=True)
        out_t = summed[...] * inverse
        kept[head] = out_t.T
        d_out_t = zd[:, span].astype(F32).T
        delta = jnp.sum(d_out_t * out_t, axis=0, keepdims=True) * inverse
        scaled = d_out_t * inverse
        d_out_t = scaled.astype(BF16)
        d_out = scaled.T.astype(BF16)
        d_query[...] = jnp.zeros_like(d_query)

        @pl.loop(0, block + 1)
        def _(index):
            weight = weights[index]
            d_weight = dot(kv[index, :, span], d_out_t)
            d_score = (weight.astype(F32) * (d_weight - delta)).astype(BF16)
            dkv[index, :, span] = (dot(d_score, query) + dot(weight, d_out)).astype(BF16)
            d_query[...] += dot(turned_kv[index], d_score)

        dq[:, span] = low_half((d_query[...] * 0.125).T)

    heads[:, 0:TILE] = jnp.where(
        lanes((ROWS, TILE)) < HD, swap_halves(kept[0]), kept[1]
    ).astype(BF16)
    heads[:, TILE : 2 * TILE] = low_half(swap_halves(kept[2])).astype(BF16)


def back_kernel(
    dkv, dq, heads, wq, mlp, cotb, n1, tok, tok_part, small, dx2, g12, srow, perm,
    cosine, sine_up, sine_down, cot,
    out, ingrad, final, final_y,
    from_z, from_prior, from_x, to_x, out_send, out_recv, dx_send, dx_recv, dqkv, gq, rowsum,
    slots, twin_recv, halves, recv_a, recv_b, sum_a, sum_b, last_a, last_b, y_send, y_recv,
    send, recv,
):
    net = Links(send, recv)
    xlo, core, xhi, z, y = net.xlo, net.core, net.xhi, net.z, net.y
    block = xhi * 4 + z
    net.greet()

    inside = [
        net.copy(dkv.at[xhi * 4 + (z - step) % 4], from_z.at[step - 1], net.at_z(4 - step))
        for step in (1, 2, 3)
    ]
    before = [
        net.copy(dkv.at[(z - step) % 4], from_prior.at[step - 1], net.at_z(4 - step))
        for step in (1, 2, 3)
    ]
    across = net.copy(to_x, from_x, net.at_x(2))

    @pl.when(xhi == 1)
    def _():
        start(before)

    for step in (1, 2, 3):
        pl.when(z - step >= 0)(inside[step - 1].start)

    for part in range(4):
        span = slice(part * PART, part * PART + PART)
        out_send[part] = (mlp[part] + dot_nt(heads[...], wq[span, DENSE])).astype(BF16)
    out_copies = [
        net.copy(out_send.at[(y + step) % 4], out_recv.at[step - 1], net.at_y(step))
        for step in (1, 2, 3)
    ]
    start(out_copies)
    ones = jnp.ones((ROWS, TILE), BF16)
    for part in range(4):
        span = slice(part * PART, part * PART + PART)
        gq[span, DENSE] = dot_tn(cotb[part], heads[...])
        gq[span, 896:1024] = dot_tn(cotb[part], ones)

    @pl.when(xhi == 1)
    def _():
        wait(before)

        @pl.loop(0, 4)
        def _(index):
            rows = pl.ds(pl.multiple_of(index * TILE, TILE), TILE)
            total = dkv[z, rows, :].astype(F32)
            for step in range(3):
                total = total + from_prior[step, rows, :].astype(F32)
            to_x[rows, :] = total.astype(BF16)

        across.start()

    for step in (1, 2, 3):
        pl.when(z - step >= 0)(inside[step - 1].wait_send)
        pl.when(z + step <= 3)(inside[step - 1].wait_recv)

        @pl.when(z + step > 3)
        def _():
            from_z[step - 1] = jnp.zeros((ROWS, 384), BF16)

    @pl.when(xhi == 0)
    def _():
        across.wait_recv()

    @pl.when(xhi == 1)
    def _():
        across.wait_send()
        from_x[...] = jnp.zeros_like(from_x)

    rowsum[...] = jnp.zeros_like(rowsum)

    @pl.loop(0, 4)
    def _(index):
        rows = pl.ds(pl.multiple_of(index * TILE, TILE), TILE)
        turning = (cosine[rows, :], -sine_up[rows, :], -sine_down[rows, :])
        total = dkv[block, rows, :].astype(F32) + from_x[rows, :].astype(F32)
        for step in range(3):
            total = total + from_z[step, rows, :].astype(F32)
        pieces = [
            turn(total[:, head * TILE : head * TILE + TILE], *turning) for head in range(3)
        ]
        query = [
            turn(dq[rows, head * TILE : head * TILE + TILE], *turning) for head in range(3)
        ]
        pieces.append(low_half(query[0]) + swap_halves(low_half(query[1])))
        pieces.append(low_half(query[2]))
        stacked = jnp.concatenate(pieces, axis=1).astype(BF16)
        dqkv[rows, :] = stacked
        d_norm = dot_nt(stacked, wq[:, QKV])
        normed, scale = standardize(tok[rows, :])
        d_input = dx2[rows, :] + norm_back(small[0:1, :] * d_norm, normed, scale)
        rowsum[0:8, :] += fold(d_norm * normed)
        rowsum[8:16, :] += fold(d_norm)
        rowsum[16:24, 0:640] += fold(stacked.astype(F32))
        dx_send[0, rows, :] = d_input[:, 0:PART].astype(BF16)
        for part in range(1, 4):
            moved = pltpu.roll(d_input, WIDE - part * PART, axis=1)
            dx_send[part, rows, :] = moved[:, 0:PART].astype(BF16)

    dx_copies = [
        net.copy(dx_send.at[(y + step) % 4], dx_recv.at[step - 1], net.at_y(step))
        for step in (1, 2, 3)
    ]
    start(dx_copies)
    for half in (0, 1):
        span = slice(half * 384, half * 384 + 384)
        gq[span, QKV] = dot_tn(n1[:, span], dqkv[...])

    def whole(ref, at):
        return jnp.sum(ref[at : at + 8, :], axis=0, keepdims=True)

    row_id = lax.broadcasted_iota(jnp.int32, (16, 640), 0)
    inner = lanes((16, 640)) % TILE
    query_lane = lanes((16, 640)) >= 384
    chosen = row_id == jnp.where(query_lane, 0, jnp.where(inner < HD, 1, 2))
    qkv_rows = jnp.where(chosen, whole(rowsum, 16)[:, 0:640], 0.0).astype(BF16)
    qkv_small = dot_nt(qkv_rows, perm[:, 0:640])
    fc1_rows = jnp.broadcast_to(whole(srow, 16), (16, WIDE)).astype(BF16)
    fc1_small = dot_nt(fc1_rows, perm[:, 640:1408])
    columns = jnp.concatenate(
        [
            jnp.zeros((64, WIDE), F32),
            whole(rowsum, 0),
            whole(srow, 0),
            whole(rowsum, 8),
            whole(srow, 8),
            jnp.zeros((2, WIDE), F32),
            fc1_small[0:1],
            qkv_small[0:3],
            jnp.zeros((54, WIDE), F32),
        ],
        axis=0,
    ).T
    lane = lanes((WIDE, TILE))
    columns = jnp.where((lane == 68) | (lane == 69), gq[:, 896:1024], columns)
    gq[:, 512:640] = jnp.where(lane < HD, gq[:, 512:640], columns)

    @pl.loop(0, 16)
    def _(pair):
        rows = pl.ds(pl.multiple_of(pair * 48, 16), 48)
        left = jnp.concatenate([gq[rows, 0:896], g12[rows, 0:384].astype(F32)], axis=1)
        right = jnp.concatenate(
            [g12[rows, 384:1536].astype(F32), jnp.zeros((48, TILE), F32)], axis=1
        )
        for index in (0, 1):
            part = slice(index * 24, index * 24 + 24)
            slots[2 * pair + index] = jnp.concatenate([left[part], right[part]], axis=0).astype(
                BF16
            )

    twins = [
        net.copy(
            slots.at[pl.ds((low * 2 + 1 - core) * 8, 8)], twin_recv.at[pl.ds(low * 8, 8)], net.twin()
        )
        for low in (0, 1)
    ]
    start(twins)
    wait(twins)

    @pl.loop(0, 16)
    def _(index):
        source = (index // 8 * 2 + core) * 8 + index % 8
        halves[index] = (slots[source].astype(F32) + twin_recv[index].astype(F32)).astype(BF16)

    def quad(position):
        return (position % 2) * 2 + position // 2

    stage_a = [
        net.copy(
            halves.at[pl.ds(quad((net.x + step) % 4) * 4, 4), :, 0:640],
            recv_a.at[step - 1],
            net.at_x(step),
        )
        for step in (1, 2, 3)
    ]
    stage_b = []
    for step in (1, 2, 3):
        for which in range(4):
            stage_b.append(
                net.copy(
                    halves.at[which * 4 + (z + step) % 4, :, 640:HALF],
                    recv_b.at[step - 1, which],
                    net.at_z(step),
                )
            )
    start(stage_a + stage_b)
    wait(stage_a)
    me = quad(net.x)

    @pl.loop(0, 4)
    def _(index):
        total = halves[me * 4 + index, :, 0:640].astype(F32)
        for step in range(3):
            total = total + recv_a[step, index].astype(F32)
        sum_a[index] = total.astype(BF16)

    end_a = [
        net.copy(sum_a.at[(z + step) % 4], last_a.at[step - 1], net.at_z(step))
        for step in (1, 2, 3)
    ]
    start(end_a)
    wait(stage_b)

    @pl.loop(0, 4)
    def _(index):
        total = halves[index * 4 + z, :, 640:HALF].astype(F32)
        for step in range(3):
            total = total + recv_b[step, index].astype(F32)
        sum_b[index] = total.astype(BF16)

    end_b = [
        net.copy(sum_b.at[quad((net.x + step) % 4)], last_b.at[step - 1], net.at_x(step))
        for step in (1, 2, 3)
    ]
    start(end_b)
    wait(end_a)
    total = sum_a[z].astype(F32)
    for step in range(3):
        total = total + last_a[step].astype(F32)
    final[:, 0:640] = total
    y_send[...] = total[:, 512:640]
    y_copies = [net.copy(y_send, y_recv.at[step - 1], net.at_y(step)) for step in (1, 2, 3)]
    start(y_copies)

    wait(out_copies + dx_copies)
    out_bias = small[4:5, :] + small[5:6, :]
    bias_part = jnp.where(y == 0, out_bias[:, 0:PART], 0.0)
    for part in range(1, 4):
        moved = pltpu.roll(jnp.broadcast_to(out_bias, (8, WIDE)), WIDE - part * PART, axis=1)
        bias_part = bias_part + jnp.where(y == part, moved[0:1, 0:PART], 0.0)

    @pl.loop(0, 4)
    def _(index):
        rows = pl.ds(pl.multiple_of(index * TILE, TILE), TILE)
        total = out_send[y, rows, :].astype(F32)
        grad = dx_send[y, rows, :].astype(F32)
        for step in range(3):
            total = total + out_recv[step, rows, :].astype(F32)
            grad = grad + dx_recv[step, rows, :].astype(F32)
        out[rows, :] = (total + tok_part[rows, :].astype(F32) + bias_part).astype(BF16)
        ingrad[rows, :] = grad + cot[rows, :].astype(F32)

    wait(end_b)
    total = sum_b[me].astype(F32)
    for step in range(3):
        total = total + last_b[step].astype(F32)
    final[:, 640:HALF] = total
    wait(y_copies)
    final_y[...] = y_send[...] + y_recv[0] + y_recv[1] + y_recv[2]


def permutation():
    table = np.zeros((WIDE, 1408), np.float32)
    for number in range(32):
        for row in range(12):
            for j in range(2):
                source = 24 * number + 2 * row + j
                table[source, 640 + 64 * row + 2 * number + j] = 1
                if row < 3:
                    at = 2 * number + j
                    table[source, 128 * row + at] = 1
                    table[source, 128 * row + 64 + at] = 1
                    table[source, 384 + 64 * row + at] = 1
    return table


def tables(first):
    frequency = 10000.0 ** (-2.0 * jnp.arange(ROT // 2, dtype=F32) / ROT)
    positions = (first + jnp.arange(ROWS)).astype(F32)
    phases = positions[:, None] * frequency[None, :]
    cosine, sine = jnp.cos(phases), jnp.sin(phases)
    blank = jnp.zeros_like(sine)
    pad = ((0, 0), (0, TILE - ROT))
    return (
        jnp.pad(jnp.concatenate([cosine, cosine], axis=1), pad, constant_values=1.0),
        jnp.pad(jnp.concatenate([blank, sine], axis=1), pad),
        jnp.pad(jnp.concatenate([-sine, blank], axis=1), pad),
    )


def call(kernel, name, shapes, scratch, collective, inputs):
    options = dict(vmem_limit_bytes=VMEM_LIMIT)
    if collective is not None:
        options.update(collective_id=collective, has_side_effects=True)
    return pl.pallas_call(
        kernel,
        name=name,
        out_shape=[jax.ShapeDtypeStruct(shape, kind) for shape, kind in shapes],
        in_specs=[pl.BlockSpec(memory_space=pltpu.VMEM)] * len(inputs),
        out_specs=[pl.BlockSpec(memory_space=pltpu.VMEM)] * len(shapes),
        scratch_shapes=scratch,
        compiler_params=pltpu.CompilerParams(**options),
    )(*inputs)


def shards(
    tokens,
    norm_gain,
    norm_bias,
    qkv_weight,
    qkv_bias,
    dense_weight,
    fc1_weight,
    fc1_bias,
    fc2_weight,
    out_bias,
    cotangent,
):
    tok = tokens[0]
    cot = cotangent[0]
    query, key, value = (qkv_weight[:, which].reshape(24, 3, HD) for which in range(3))
    key_value = jnp.concatenate([key, value], axis=2).reshape(24, 384)
    small_in = jnp.concatenate(
        [
            norm_gain.T,
            norm_bias.T,
            out_bias.T,
            fc1_bias.reshape(24, 1),
            jnp.pad(qkv_bias.reshape(3, 6).T, ((0, 18), (0, 0))),
            jnp.zeros((24, 54), BF16),
        ],
        axis=1,
    )
    blank = jnp.zeros((24, TILE), BF16)
    left = jnp.concatenate(
        [
            key_value,
            query.reshape(24, PART),
            small_in,
            dense_weight.T,
            blank[:, 0:64],
            fc1_weight[:, 0:384],
        ],
        axis=1,
    )
    right = jnp.concatenate([fc1_weight[:, 384:], fc2_weight.T, blank], axis=1)
    pack = jnp.concatenate([left, right], axis=0)
    turning = tables(lax.axis_index("ctx") * ROWS)
    perm = jnp.asarray(permutation(), BF16)
    vm = pltpu.VMEM
    dma = pltpu.SemaphoreType.DMA

    wq, qz, zd, kv, mlp, dx2, g12, srow, n1, cotb, small = call(
        front_kernel,
        "front",
        [
            ((WIDE, 896), BF16),
            ((ROWS, 384), BF16),
            ((ROWS, 384), BF16),
            ((8, ROWS, 384), BF16),
            ((4, ROWS, PART), F32),
            ((ROWS, WIDE), F32),
            ((WIDE, 2 * WIDE), BF16),
            ((24, WIDE), F32),
            ((ROWS, WIDE), BF16),
            ((4, ROWS, PART), BF16),
            ((16, WIDE), F32),
        ],
        [
            vm((32, 48, HALF), BF16),
            vm((WIDE, 2432), BF16),
            vm((ROWS, WIDE), BF16),
            vm((ROWS, WIDE), BF16),
            vm((ROWS, WIDE), BF16),
            vm((ROWS, WIDE), F32),
            vm((ROWS, TILE), F32),
            vm((8, WIDE), F32),
            dma((40,)),
            dma((40,)),
        ],
        0,
        [pack, cot, tok, *turning, perm],
    )
    heads, dq, dkv = call(
        attention_kernel,
        "attention",
        [((ROWS, 256), BF16), ((ROWS, 384), F32), ((8, ROWS, 384), BF16)],
        [
            vm((8, ROWS, ROWS), F32),
            vm((8, ROWS, ROWS), BF16),
            vm((8, TILE, ROWS), BF16),
            vm((3, ROWS, TILE), F32),
            vm((TILE, ROWS), F32),
            vm((8, ROWS), F32),
            vm((8, ROWS), F32),
            vm((TILE, ROWS), F32),
        ],
        None,
        [qz, zd, kv],
    )
    tok_part = lax.dynamic_slice_in_dim(tok, lax.axis_index("tensor") * PART, PART, 1)
    output, input_grad, final, final_y = call(
        back_kernel,
        "back",
        [
            ((ROWS, PART), BF16),
            ((ROWS, PART), F32),
            ((48, HALF), F32),
            ((48, TILE), F32),
        ],
        [
            vm((3, ROWS, 384), BF16),
            vm((3, ROWS, 384), BF16),
            vm((ROWS, 384), BF16),
            vm((ROWS, 384), BF16),
            vm((4, ROWS, PART), BF16),
            vm((3, ROWS, PART), BF16),
            vm((4, ROWS, PART), BF16),
            vm((3, ROWS, PART), BF16),
            vm((ROWS, 640), BF16),
            vm((WIDE, 1024), F32),
            vm((24, WIDE), F32),
            vm((32, 48, HALF), BF16),
            vm((16, 48, HALF), BF16),
            vm((16, 48, HALF), BF16),
            vm((3, 4, 48, 640), BF16),
            vm((3, 4, 48, 640), BF16),
            vm((4, 48, 640), BF16),
            vm((4, 48, 640), BF16),
            vm((3, 48, 640), BF16),
            vm((3, 48, 640), BF16),
            vm((48, TILE), F32),
            vm((3, 48, TILE), F32),
            dma((48,)),
            dma((48,)),
        ],
        1,
        [
            dkv, dq, heads, wq, mlp, cotb, n1, tok, tok_part, small, dx2, g12, srow, perm,
            *turning, cot,
        ],
    )
    grads = jnp.concatenate([final[0:24], final[24:48]], axis=1)
    summed = final_y[0:24, 64:68].T
    key_value = grads[:, 0:384].reshape(24, 3, 2, HD)
    grad_qkv = jnp.stack(
        [
            grads[:, 384:576],
            key_value[:, :, 0].reshape(24, PART),
            key_value[:, :, 1].reshape(24, PART),
        ],
        axis=1,
    )
    return (
        output[None],
        input_grad[None],
        summed[0:2],
        summed[2:4],
        grad_qkv,
        grads[0:6, 583:586].T.reshape(3, 3, 2),
        grads[:, 640:832].T,
        grads[:, 896:1664],
        grads[:, 582].reshape(12, 2),
        grads[:, 1664:2432].T,
        grads[:, 580:582].T,
    )


def solution(mesh):
    return jax.shard_map(
        shards,
        mesh=mesh,
        in_specs=(
            P("dp", "ctx", None),
            P(None, ("dp", "ctx")),
            P(None, ("dp", "ctx")),
            P(("dp", "ctx"), None, "tensor"),
            P(None, "tensor", ("dp", "ctx")),
            P("tensor", ("dp", "ctx")),
            P(("dp", "ctx"), "tensor"),
            P("tensor", ("dp", "ctx")),
            P("tensor", ("dp", "ctx")),
            P(None, ("dp", "ctx")),
            P("dp", "ctx", "tensor"),
        ),
        out_specs=(
            P("dp", "ctx", "tensor"),
            P("dp", "ctx", "tensor"),
            P(None, ("dp", "ctx")),
            P(None, ("dp", "ctx")),
            P(("dp", "ctx"), None, "tensor"),
            P(None, "tensor", ("dp", "ctx")),
            P("tensor", ("dp", "ctx")),
            P(("dp", "ctx"), "tensor"),
            P("tensor", ("dp", "ctx")),
            P("tensor", ("dp", "ctx")),
            P(None, ("dp", "ctx")),
        ),
        check_vma=False,
    )
```

time: 1380 us -> 215 us (0.16)
  blocking collectives: 736 us -> 0 us
  waiting for transfers between devices: 528 us -> 0 us
  Pallas kernels: 0 us -> 185 us
  matrix products: 37.9 us -> 0 us
  other arithmetic: 23.7 us -> 5.57 us
  between operations: 16.4 us -> 0.76 us
    all_gather x8 -> x0, blocking collectives: 580 us -> none  [the longest x1 134 us: shards(): lax.all_gather(fc1_bias, ('dp', 'ctx'), axis=1, tiled=True)]
    reduce_scatter x5 -> x0, waiting for transfers between devices: 479 us -> none  [the longest x1 149 us: shards(): lax.psum_scatter(grad_fc2.astype(jnp.bfloat16), ('dp', 'ctx'), scatter_di...]
    pallas_call x0 -> x3, Pallas kernels: none -> 185 us  [call(): pl.pallas_call(kernel, name=name, out_shape=[jax.ShapeDtypeStruct(shape,...]
    unnamed x1 -> x0, blocking collectives: 144 us -> none
    dot_general x19 -> x0, matrix products: 37.9 us -> none  [the longest x1 6.8 us: shards(): jnp.einsum('std,df->stf', norm_two, fc1_full, preferred_element_type=jnp....]
    unnamed x15 -> x0, waiting for transfers between devices: 29.5 us -> none
    all_gather x4 -> x0, waiting for transfers between devices: 19.6 us -> none  [the longest x1 10.7 us: shards(): lax.all_gather(value_flat, 'ctx', axis=1, tiled=True)]
  transfers between devices with their start and end apart: 12 -> 0, of which waited for: 7 -> 0; matrix products, arithmetic and copies ran while one was open for 6% -> 0% of each run, Pallas kernels for 0% -> 0%
where the time goes in v1:
time: 215 us; the launch traced here: 214 us
  Pallas kernels  185 us (86%)
  local copies, waits for them, and re-layouts  23 us (11%)
  other arithmetic  5.57 us (3%)
    pallas_call x3, Pallas kernels, call(): pl.pallas_call(kernel, name=name, out_shape=[jax.ShapeDtypeStruct(shape,...  185 us
    unnamed x20, local copies, waits for them, and re-layouts  10.7 us

profile of v1, /device:TPU:0, one launch (start us, length us, event | category | flops | bytes accessed | tf_op | source)
XLA Modules:
  0.0 214.2 jit_solution(13156339391389837653)
XLA Ops:
  0.6 0.0 copy-start.1
  0.7 0.8 slice_bitcast_fusion.5
  1.4 0.1 reshape_squeeze.10
  1.5 0.1 reshape_squeeze.9
  1.6 0.1 pad_maximum_fusion.2
  1.7 0.7 fusion.2
  2.5 0.7 copy.85
  3.2 0.1 reshape.53
  3.3 0.8 copy.86
  4.1 0.7 copy.82
  4.9 0.7 copy.83
  5.6 0.7 copy.84
  6.4 0.8 concatenate.25
  7.2 1.4 maximum_maximum_fusion.pack
  8.6 1.0 fusion
  9.6 0.8 pad.36.sine_up
  10.5 0.7 pad.37.sine_down
  11.2 0.9 select_maximum_fusion.cosine
  12.1 0.0 copy-done.1
  12.1 0.8 copy.88
  12.9 53.9 %front.1 = (bf16[768,896]{1,0:T(8,128)(2,1)}, bf16[512,384]{1,0:T(8,128)(2,1)}, bf16[512,384]{1,0:T(8,128)(2,1)}, bf16[8,512,384]{2,1,0:T(8,128)(2,1)}, f32[4,51...) custom-call(bf16[48,1280]{1,0:T(8,128)(2,1)} %maximum_maximum_fusion, ...), custom_call_target="tpu_custom_call" | custom-call | tf_op jit(solution)/shard_map/front/pallas_call | solution.py:674
  66.8 9.5 %attention.1 = (bf16[512,256]{1,0:T(8,128)(2,1)}, f32[512,384]{1,0:T(8,128)}, bf16[8,512,384]{2,1,0:T(8,128)(2,1)}) custom-call(bf16[512,384]{1,0:T(8,128)(2,1)} %get-tuple-element.29.qz, bf16[512,384]{1,0:T(8,128)(2,1)} %get-tuple-element.30.zd, bf16[8,512,384]{2,1,0:T(8,128)(2,1)} %get-tuple-element.31.kv), custom_call_target="tpu_custom_call" | custom-call | tf_op jit(solution)/shard_map/attention/pallas_call | solution.py:674
  76.3 1.8 dynamic-slice_bitcast_fusion.tok_part
  78.1 121.5 %back.1 = (bf16[512,192]{1,0:T(8,128)(2,1)}, f32[512,192]{1,0:T(8,128)}, f32[48,1280]{1,0:T(8,128)}, f32[48,128]{1,0:T(8,128)}) custom-call(bf16[8,512,384]{2,1,0:T(8,128)(2,1)} %get-tuple-element.32.dkv, f32[512,384]{1,0:T(8,128)} %get-tuple-element.33.dq, bf16[512,256]{1,0:T(8,128)(2,1)} %get-tuple-element.34.heads, ...), custom_call_target="tpu_custom_call" | custom-call | tf_op jit(solution)/shard_map/back/pallas_call | solution.py:674
  199.6 0.0 copy-start
  199.6 0.0 copy-start.2
  199.6 1.0 fusion.1
  200.7 1.5 pad_maximum_fusion
  202.2 0.8 slice.80
  203.0 0.1 reshape.51
  203.1 0.2 slice_reduce_fusion.1
  203.3 0.1 stack_reshape_squeeze.6
  203.4 0.1 stack_reshape_squeeze.7
  203.5 1.4 slice_bitcast_fusion.1
  204.9 0.6 pad_maximum_fusion.1
  205.5 2.0 copy.91
  207.5 0.0 copy-done
  207.5 0.8 copy.90
  208.3 0.0 copy-done.2
  208.3 0.1 slice_bitcast_fusion.4
  208.4 0.1 fusion.3
  208.4 0.6 copy.92
  209.1 0.6 copy.93
  209.7 0.8 slice_bitcast_fusion.3
  210.5 0.6 copy.96
  211.1 0.8 slice_bitcast_fusion.6
  211.9 0.7 copy.94
  212.6 0.9 slice_reduce_fusion.2
  213.5 0.1 reshape_squeeze.11
  213.5 0.7 copy.95
  (9 shorter events, 0.1 us)
Async XLA Ops:
  0.6 11.4 %copy-start.1 = (bf16[1,512,192]{1,2,0:T(8,128)(2,1)S(1)}, bf16[1,512,192]{1,2,0:T(8,128)(2,1)}, u32[]{:S(2)}) copy-start(bf16[1,512,192]{1,2,0:T(8,128)(2,1)} %param.22) | copy-start | bytes 589828
  199.6 7.9 %copy-start = (bf16[512,192]{1,0:T(8,128)(2,1)S(1)}, bf16[512,192]{1,0:T(8,128)(2,1)}, u32[]{:S(2)}) copy-start(bf16[512,192]{1,0:T(8,128)(2,1)} %get-tuple-element.43) | copy-start | bytes 589828
  199.6 8.7 %copy-start.2 = (f32[48,128]{1,0:T(8,128)S(1)}, f32[48,128]{1,0:T(8,128)}, u32[]{:S(2)}) copy-start(f32[48,128]{1,0:T(8,128)} %get-tuple-element.45) | copy-start | bytes 73732

commit v2 on v0

v2 whole, which is shorter than its diff:
```python
import jax
import jax.numpy as jnp
import numpy as np
from jax import lax
from jax.experimental import pallas as pl
from jax.experimental.pallas import tpu as pltpu
from jax.sharding import PartitionSpec as P

HD = 64
ROT = 16
EPSILON = 1e-05
ROWS = 512
WIDE = 768
HALF = 1280
PART = 192
TILE = 128
MESH = pl.DeviceIdType.MESH
VMEM_LIMIT = 61 << 20
F32 = jnp.float32
BF16 = jnp.bfloat16

QKV = slice(0, 640)
DENSE = slice(640, 896)
FC1 = slice(896, 1664)
FC2 = slice(1664, 2432)
EARLY = 512
SMALL = 64


def dot(a, b):
    return lax.dot_general(a, b, (((1,), (0,)), ((), ())), preferred_element_type=F32)


def dot_nt(a, b):
    return lax.dot_general(a, b, (((1,), (1,)), ((), ())), preferred_element_type=F32)


def dot_tn(a, b):
    return lax.dot_general(a, b, (((0,), (0,)), ((), ())), preferred_element_type=F32)


def device(x, y, z, core):
    return {"dp": (x % 2) * 2 + core, "ctx": (x // 2) * 4 + z, "tensor": y}


class Links:
    def __init__(self, send, recv):
        dp = lax.axis_index("dp")
        cx = lax.axis_index("ctx")
        self.xlo, self.core, self.xhi, self.z = dp // 2, dp % 2, cx // 4, cx % 4
        self.y = lax.axis_index("tensor")
        self.x = self.xhi * 2 + self.xlo
        self.send, self.recv, self.used = send, recv, 0

    def at_x(self, step):
        return device((self.x + step) % 4, self.y, self.z, self.core)

    def at_z(self, step):
        return device(self.x, self.y, (self.z + step) % 4, self.core)

    def at_y(self, step):
        return device(self.x, (self.y + step) % 4, self.z, self.core)

    def twin(self):
        return device(self.x, self.y, self.z, 1 - self.core)

    def pal(self):
        return device((self.x + 2) % 4, self.y, 3 - self.z, self.core)

    def knock(self):
        self.barrier = pltpu.get_barrier_semaphore()
        peers = [self.twin(), self.pal()]
        for step in (1, 2, 3):
            peers += [self.at_x(step), self.at_z(step), self.at_y(step)]
        for peer in peers:
            pl.semaphore_signal(self.barrier, inc=1, device_id=peer, device_id_type=MESH)
        self.expected = len(peers)

    def enter(self):
        pl.semaphore_wait(self.barrier, self.expected)

    def copy(self, source, target, peer):
        number = self.used
        self.used += 1
        return pltpu.make_async_remote_copy(
            src_ref=source,
            dst_ref=target,
            send_sem=self.send.at[number],
            recv_sem=self.recv.at[number],
            device_id=peer,
            device_id_type=MESH,
        )


def start(copies):
    for item in copies:
        item.start()


def wait(copies):
    for item in copies:
        item.wait()


def lanes(shape):
    return lax.broadcasted_iota(jnp.int32, shape, len(shape) - 1)


def low_half(tile):
    return jnp.where(lanes(tile.shape) < HD, tile, 0.0)


def high_half(tile):
    return jnp.where(lanes(tile.shape) >= HD, tile, 0.0)


def swap_halves(tile):
    return pltpu.roll(tile, HD, axis=1)


def turn(tile, cosine, sine_up, sine_down):
    return (
        tile * cosine
        + pltpu.roll(tile, ROT // 2, axis=1) * sine_up
        + pltpu.roll(tile, TILE - ROT // 2, axis=1) * sine_down
    )


def fold(block):
    rows, width = block.shape
    return jnp.sum(block.reshape(rows // 8, 8, width), axis=0)


def column_sum(block):
    return jnp.sum(block, axis=0, keepdims=True)


def standardize(rows_in):
    values = rows_in.astype(F32)
    centred = values - jnp.mean(values, axis=-1, keepdims=True)
    scale = lax.rsqrt(jnp.mean(centred * centred, axis=-1, keepdims=True) + EPSILON)
    return centred * scale, scale


def norm_back(gradient, xhat, scale):
    return scale * (
        gradient
        - jnp.mean(gradient, axis=-1, keepdims=True)
        - xhat * jnp.mean(gradient * xhat, axis=-1, keepdims=True)
    )


def tile_at(index):
    return pl.ds(pl.multiple_of(index * TILE, TILE), TILE)


def quad(position):
    return (position % 2) * 2 + position // 2


class Gather:
    def __init__(self, net, slots, own, low, middle, high):
        self.net, self.slots, self.own = net, slots, own
        self.first, self.second = slice(low, middle), slice(middle, high)

    def one(self):
        net = self.net
        a = self.slots.at[self.own, :, self.first]
        b = self.slots.at[self.own, :, self.second]
        self.a = [net.copy(a, a, net.at_z(step)) for step in (1, 2, 3)]
        self.b = [net.copy(b, b, net.at_x(step)) for step in (1, 2, 3)]
        start(self.a + self.b)

    def two(self):
        net = self.net
        wait(self.a)
        a = self.slots.at[pl.ds(self.own - net.z, 4), :, self.first]
        self.a = [net.copy(a, a, net.at_x(step)) for step in (1, 2, 3)]
        start(self.a)
        wait(self.b)
        self.b = []
        for low in (0, 1):
            for high in (0, 1):
                number = ((low * 2 + net.core) * 2 + high) * 4 + net.z
                b = self.slots.at[number, :, self.second]
                self.b += [net.copy(b, b, net.at_z(step)) for step in (1, 2, 3)]
        start(self.b)

    def three(self):
        net = self.net
        later = []
        for done, span in ((self.a, self.first), (self.b, self.second)):
            wait(done)
            for low in (0, 1):
                part = self.slots.at[pl.ds((low * 2 + net.core) * 8, 8), :, span]
                later.append(net.copy(part, part, net.twin()))
                later[-1].start()
        self.a = later

    def end(self):
        wait(self.a)


class Reduce:
    def __init__(self, net, slots, low, middle, high, twin_in, halves, in_a, in_b, sum_a, sum_b, end_a, end_b):
        self.net, self.slots = net, slots
        self.whole, self.first, self.second = slice(low, high), slice(low, middle), slice(middle, high)
        self.bufs = (twin_in, halves, in_a, in_b, sum_a, sum_b, end_a, end_b)

    def one(self):
        net = self.net
        self.twins = [
            net.copy(
                self.slots.at[pl.ds((low * 2 + 1 - net.core) * 8, 8), :, self.whole],
                self.bufs[0].at[pl.ds(low * 8, 8), :, self.whole],
                net.twin(),
            )
            for low in (0, 1)
        ]
        start(self.twins)

    def two(self):
        net = self.net
        twin_in, halves, in_a, in_b = self.bufs[:4]
        wait(self.twins)

        @pl.loop(0, 16)
        def _(index):
            source = (index // 8 * 2 + net.core) * 8 + index % 8
            halves[index, :, self.whole] = (
                self.slots[source, :, self.whole].astype(F32) + twin_in[index, :, self.whole].astype(F32)
            ).astype(BF16)

        self.a = [
            net.copy(
                halves.at[pl.ds(quad((net.x + step) % 4) * 4, 4), :, self.first],
                in_a.at[step - 1],
                net.at_x(step),
            )
            for step in (1, 2, 3)
        ]
        self.b = [
            net.copy(
                halves.at[which * 4 + (net.z + step) % 4, :, self.second],
                in_b.at[step - 1, which],
                net.at_z(step),
            )
            for step in (1, 2, 3)
            for which in range(4)
        ]
        start(self.a + self.b)

    def three(self):
        net = self.net
        halves, in_a, in_b, sum_a, sum_b, end_a, end_b = self.bufs[1:]
        me = quad(net.x)
        wait(self.a)
        for index in range(4):
            total = halves[me * 4 + index, :, self.first].astype(F32)
            for step in range(3):
                total = total + in_a[step, index].astype(F32)
            sum_a[index] = total.astype(BF16)
        self.a = [
            net.copy(sum_a.at[(net.z + step) % 4], end_a.at[step - 1], net.at_z(step))
            for step in (1, 2, 3)
        ]
        start(self.a)
        wait(self.b)
        for index in range(4):
            total = halves[index * 4 + net.z, :, self.second].astype(F32)
            for step in range(3):
                total = total + in_b[step, index].astype(F32)
            sum_b[index] = total.astype(BF16)
        self.b = [
            net.copy(sum_b.at[quad((net.x + step) % 4)], end_b.at[step - 1], net.at_x(step))
            for step in (1, 2, 3)
        ]
        start(self.b)

    def end(self, target):
        sum_a, sum_b, end_a, end_b = self.bufs[4:]
        for copies, own, arrived, span in (
            (self.a, sum_a.at[self.net.z], end_a, self.first),
            (self.b, sum_b.at[quad(self.net.x)], end_b, self.second),
        ):
            wait(copies)
            total = own[...].astype(F32)
            for step in range(3):
                total = total + arrived[step].astype(F32)
            target[:, span] = total


def layer_kernel(
    tok, gains, shifts, outs, qkv, qkv_small, dense, fc1, fc1_small, fc2, cot_own, perm, angle_rows, angle_block,
    out_t, grad_t, final,
    slots, w2, small, bias, small_rows, narrow, out_col, cosine, sine_up, sine_down, xhat, rstd, tok_t, n1, n2, dhid, act,
    cot_t, cot, mlp_t, dx2, srow, qd, qd_in, qdt, kv, dkv, kv_t, weights, tops, top, totals, summed,
    part_out, part_in, stat_out, stat_in, dq_out, dq_in, kept, gq,
    twin_in, halves, early_a, early_b, early_sa, early_sb, early_ea, early_eb,
    late_a, late_b, late_sa, late_sb, late_ea, late_eb,
    from_z, from_x, out_send, out_recv, dx_send, dx_recv, rowsum, y_send, y_recv,
    send, recv,
):
    net = Links(send, recv)
    xlo, core, xhi, z, y = net.xlo, net.core, net.xhi, net.z, net.y
    own = ((xlo * 2 + core) * 2 + xhi) * 4 + z
    block = xhi * 4 + z
    upper, lower = xhi == 1, xhi == 0
    both = jnp.logical_and
    either = jnp.logical_or
    helps = both(lower, z <= 2)
    helped = both(upper, z >= 1)
    heads = dhid.at[:, 0:256]
    dq_t = kept.at[:, 0:HD, :]
    to_x = act.at[:, 0:384]
    dqkv = n2.at[:, QKV]
    total_kv = gq.at[0:ROWS, 0:384]
    net.knock()

    narrow[...] = jnp.zeros_like(narrow)
    for which in range(3):
        narrow[which, :, 0:HD] = qkv[which, :, TILE:PART].astype(F32)
    narrow[3, :, 0:HD] = dense[:, TILE:PART].astype(F32)
    small_rows[...] = jnp.zeros_like(small_rows)
    small_rows[SMALL : SMALL + 2, 0:24] = gains[...].astype(F32)
    small_rows[SMALL + 2 : SMALL + 4, 0:24] = shifts[...].astype(F32)
    small_rows[SMALL + 4 : SMALL + 6, 0:24] = outs[...].astype(F32)
    small_rows[SMALL + 6 : SMALL + 8, 0:12] = fc1_small[...].astype(F32)
    for which in range(3):
        at = SMALL + 8 + 2 * which
        small_rows[at : at + 2, 0:3] = qkv_small[which].astype(F32)
    columns = small_rows[...].T[0:24]
    key = qkv[1, :, 0:TILE].astype(F32)
    value = qkv[2, :, 0:TILE].astype(F32)
    left = lanes((24, TILE)) < HD
    top_half = jnp.concatenate(
        [
            jnp.where(left, key, swap_halves(value)),
            jnp.where(left, swap_halves(key), value),
            narrow[1] + swap_halves(narrow[2]),
            dense[:, 0:TILE].astype(F32),
        ],
        axis=1,
    )
    bottom_half = jnp.concatenate(
        [qkv[0, :, 0:TILE].astype(F32), narrow[0] + columns, narrow[3], jnp.zeros((24, TILE), F32)], axis=1
    )
    slots[own, :, 0:EARLY] = jnp.concatenate([top_half, bottom_half], axis=0).astype(BF16)
    slots[own, :, EARLY:HALF] = jnp.concatenate([fc1[...].astype(F32), fc2[...].astype(F32)], axis=0).astype(BF16)
    net.enter()
    early = Gather(net, slots, own, 0, 256, EARLY)
    late = Gather(net, slots, own, EARLY, 896, HALF)
    early.one()

    row_cos, row_sin = angle_rows[0], angle_rows[1]
    block_cos, block_sin = angle_block[0, pl.ds(block, 1), :], angle_block[1, pl.ds(block, 1), :]
    cosine[...] = row_cos * block_cos - row_sin * block_sin
    sine = row_sin * block_cos + row_cos * block_sin
    upward = lanes((ROWS, TILE)) >= ROT // 2
    sine_up[...] = jnp.where(upward, sine, 0.0)
    sine_down[...] = jnp.where(upward, 0.0, -sine)

    @pl.loop(0, 4)
    def _(index):
        rows = tile_at(index)
        normed, scale = standardize(tok[rows, :])
        xhat[rows, :] = normed
        rstd[rows, :] = jnp.broadcast_to(scale, (TILE, TILE))

    early.two()
    late.one()
    mine_t = cot_t.at[pl.ds(pl.multiple_of(y * PART, 16), PART), :]
    gather_y = [net.copy(cot_own, mine_t, net.at_y(step)) for step in (1, 2, 3)]
    start(gather_y)
    mine_t[...] = cot_own[...]
    for index in range(4):
        rows = slice(index * TILE, index * TILE + TILE)
        tok_t[:, rows] = tok[rows, :].astype(F32).T.astype(BF16)
    dkv[...] = jnp.zeros_like(dkv)
    early.three()
    late.two()
    early.end()

    @pl.loop(0, 16)
    def _(pair):
        rows = pl.ds(pl.multiple_of(pair * 48, 16), 48)
        one = slots[2 * pair, :, 0:EARLY].astype(F32)
        two = slots[2 * pair + 1, :, 0:EARLY].astype(F32)
        upper_rows = jnp.concatenate([one[0:24], two[0:24]], axis=0).astype(BF16)
        lower_rows = jnp.concatenate([one[24:48], two[24:48]], axis=0).astype(BF16)
        w2[rows, 0:384] = upper_rows[:, 0:384]
        w2[rows, 640:768] = upper_rows[:, 384:512]
        w2[rows, 384:640] = lower_rows[:, 0:256]
        w2[rows, 768:896] = lower_rows[:, 256:384]

    column_form = w2[:, 512:640].astype(F32)
    out_col[...] = jnp.broadcast_to(
        column_form[:, SMALL + 4 : SMALL + 5] + column_form[:, SMALL + 5 : SMALL + 6], (WIDE, TILE)
    )
    turned = column_form.T[SMALL : SMALL + 16, :]
    small[...] = turned
    spread = dot(turned.astype(BF16), perm[...])
    lane = lanes((1, 640))
    inner = lane % TILE
    qkv_row = [
        spread[8 + 2 * which : 9 + 2 * which, 0:640]
        + pltpu.roll(jnp.broadcast_to(spread[9 + 2 * which : 10 + 2 * which, 0:640], (8, 640)), 1, axis=1)[0:1]
        for which in range(3)
    ]
    bias[0:1, 0:640] = jnp.where(lane >= 384, qkv_row[0], jnp.where(inner < HD, qkv_row[1], qkv_row[2]))
    bias[1:2, :] = (
        spread[6:7, 640:1408] + pltpu.roll(jnp.broadcast_to(spread[7:8, 640:1408], (8, WIDE)), 1, axis=1)[0:1]
    )

    @pl.loop(0, 4)
    def _(index):
        rows = tile_at(index)
        normed = xhat[rows, :]
        one = (normed * small[0:1, :] + small[2:3, :]).astype(BF16)
        n1[rows, :] = one
        n2[rows, :] = (normed * small[1:2, :] + small[3:4, :]).astype(BF16)
        projected = dot(one, w2[:, QKV]) + bias[0:1, 0:640]
        turning = (cosine[rows, :], sine_up[rows, :], sine_down[rows, :])
        for head in range(3):
            span = slice(head * TILE, head * TILE + TILE)
            kv[block, rows, span] = turn(projected[:, span], *turning).astype(BF16)
        pair, last = projected[:, 384:512], projected[:, 512:640]
        for head, tile in enumerate((pair, swap_halves(pair), last)):
            span = slice(head * TILE, head * TILE + TILE)
            qd[rows, span] = (low_half(turn(low_half(tile), *turning)) * 0.125).astype(BF16)

    spans = [slice(head * TILE, head * TILE + TILE) for head in range(3)]
    send_own, send_prior, receive, given = [], [], [], []
    for step in (1, 2, 3):
        behind = z + step <= 3
        send_own.append(either(behind, both(lower, both(z + step == 4, z <= 2))))
        send_prior.append(both(upper, z + step > 3))
        receive.append(either(upper, either(z - step >= 0, both(z == 0, step >= 2))))
        given.append((z - step + 4) % 4 + 4 * xhi * ((z - step + 4) // 4))
    across, along = [], []
    for head in range(3):
        mine = kv.at[block, :, spans[head]]
        across.append(net.copy(mine, mine, net.at_x(2)))
        along.append([])
        for step in (1, 2, 3):
            piece = kv.at[block - 4 * xhi * ((z + step) // 4), :, spans[head]]
            along[head].append(net.copy(piece, piece, net.at_z(step)))
    for head in range(3):
        pl.when(lower)(across[head].start)
        for step in range(3):
            pl.when(send_own[step])(along[head][step].start)
    late.three()

    wait(gather_y)
    for index in range(4):
        rows = slice(index * TILE, index * TILE + TILE)
        cot[rows, :] = cot_t[:, rows].astype(F32).T.astype(BF16)
    out_sums = jnp.sum(cot_t[...].astype(F32), axis=1, keepdims=True)

    @pl.loop(0, 4)
    def _(index):
        rows = tile_at(index)
        d_heads = dot(cot[rows, :], w2[:, DENSE])
        pair, last = d_heads[:, 0:TILE], d_heads[:, TILE : 2 * TILE]
        for head, tile in enumerate((swap_halves(pair), pair, swap_halves(last))):
            qd[rows, spans[head]] = (qd[rows, spans[head]].astype(F32) + high_half(tile)).astype(BF16)

    lend = net.copy(qd, qd_in, net.pal())
    pl.when(helped)(lend.start)
    for head in range(3):

        @pl.when(upper)
        def _():
            across[head].wait_recv()

        for step in range(3):
            pl.when(send_prior[step])(along[head][step].start)
    late.end()

    @pl.loop(0, 16)
    def _(pair):
        rows = pl.ds(pl.multiple_of(pair * 48, 16), 48)
        one = slots[2 * pair, :, EARLY:HALF].astype(F32)
        two = slots[2 * pair + 1, :, EARLY:HALF].astype(F32)
        w2[rows, FC1] = jnp.concatenate([one[0:24], two[0:24]], axis=0).astype(BF16)
        w2[rows, FC2] = jnp.concatenate([one[24:48], two[24:48]], axis=0).astype(BF16)

    srow[...] = jnp.zeros_like(srow)

    @pl.loop(0, 4)
    def _(index):
        rows = tile_at(index)
        hidden = dot(n2[rows, :], w2[:, FC1]) + bias[1:2, :]
        spread_to = 0.5 + 0.5 * lax.erf(hidden * (0.5**0.5))
        act[rows, :] = (hidden * spread_to).astype(BF16)
        slope = spread_to + hidden * jnp.exp(-0.5 * hidden * hidden) * 0.3989422804014327
        d_hidden = (slope * dot(cot[rows, :], w2[:, FC2])).astype(BF16)
        dhid[rows, :] = d_hidden
        d_norm = dot_nt(d_hidden, w2[:, FC1])
        normed = xhat[rows, :]
        dx2[rows, :] = norm_back(small[1:2, :] * d_norm, normed, rstd[rows, 0:1])
        srow[0:8, :] += fold(d_norm * normed)
        srow[8:16, :] += fold(d_norm)
        srow[16:24, :] += fold(d_hidden.astype(F32))

    for half in (0, 1):
        span = slice(half * 384, half * 384 + 384)
        mlp_t[span, :] = dot_nt(w2[span, FC2], act[...])
        gq[0:384, 0:WIDE] = dot_tn(n2[:, span], dhid[...])
        gq[384:768, 0:WIDE] = dot(cot_t[span, :], act[...])

        @pl.loop(0, 16)
        def _(index):
            first = pl.ds(pl.multiple_of(index * 24, 8), 24)
            second = pl.ds(pl.multiple_of(384 + index * 24, 8), 24)
            slots[half * 16 + index, :, EARLY:HALF] = jnp.concatenate(
                [gq[first, 0:WIDE], gq[second, 0:WIDE]], axis=0
            ).astype(BF16)

    fc_sum = Reduce(
        net, slots, EARLY, 896, HALF, twin_in, halves, late_a, late_b, late_sa, late_sb, late_ea, late_eb
    )
    fc_sum.one()

    row_is_low = lax.broadcasted_iota(jnp.int32, (TILE, ROWS), 0) < HD

    def absorb(head, slot, at, query_t, masked):
        tile = kv[at, :, spans[head]]
        tile_t = tile.astype(F32).T.astype(BF16)
        chunk = head * 5 + slot
        kv_t[chunk] = tile_t
        score = dot(tile, query_t)
        if masked:
            key_at = lax.broadcasted_iota(jnp.int32, score.shape, 0)
            query_at = lax.broadcasted_iota(jnp.int32, score.shape, 1)
            score = jnp.where(key_at <= query_at, score, -1e30)
        before = top[0:1, :]
        peak = jnp.maximum(before, jnp.max(score, axis=0, keepdims=True))
        weight = jnp.exp(score - peak)
        shrink = jnp.exp(before - peak)
        rounded = weight.astype(BF16)
        weights[chunk] = rounded
        tops[chunk] = jnp.broadcast_to(peak, (8, ROWS))
        top[...] = jnp.broadcast_to(peak, (8, ROWS))
        totals[...] = totals[...] * shrink + fold(weight)
        summed[...] = summed[...] * shrink + dot(tile_t, rounded)

    def fresh():
        top[...] = jnp.full_like(top, -1e30)
        totals[...] = jnp.zeros_like(totals)
        summed[...] = jnp.zeros_like(summed)

    first_own = 4 * xhi * 0 + z * xhi
    own_count = block - first_own
    stats = []
    partials = [net.copy(part_out.at[head], part_in.at[head], net.pal()) for head in range(3)]

    @pl.when(jnp.logical_not(helped))
    def _():
        part_in[...] = jnp.zeros_like(part_in)
        part_in[:, HD : HD + 8, :] = jnp.full((3, 8, ROWS), -1e30, F32)
        dq_in[...] = jnp.zeros_like(dq_in)

    @pl.when(helps)
    def _():
        lend.wait_recv()

    for head in range(3):
        pl.when(jnp.logical_and(lower, True))(across[head].wait_send)
        for step in range(3):
            pl.when(receive[step])(along[head][step].wait_recv)

        @pl.when(helps)
        def _():
            turned_in = qd_in[:, spans[head]].astype(F32).T
            qdt[3 + head] = turned_in.astype(BF16)
            query_t = jnp.where(row_is_low, turned_in, 0.0).astype(BF16)
            fresh()

            @pl.loop(0, 3 - z)
            def _(index):
                absorb(head, z + 1 + index, index, query_t, False)

            part_out[head, 0:HD, :] = summed[HD:TILE, :]
            part_out[head, HD : HD + 8, :] = top[...]
            part_out[head, HD + 8 : HD + 16, :] = jnp.broadcast_to(column_sum(totals[...]), (8, ROWS))
            partials[head].start()

        turned_own = qd[:, spans[head]].astype(F32).T
        qdt[head] = turned_own.astype(BF16)
        query_t = jnp.where(row_is_low, turned_own, 0.0).astype(BF16)
        fresh()

        @pl.loop(0, own_count)
        def _(index):
            absorb(head, index, first_own + index, query_t, False)

        absorb(head, own_count, block, query_t, True)
        kept[head, 0:HD, :] = summed[HD:TILE, :]
        kept[head, HD : HD + 8, :] = top[...]
        kept[head, HD + 8 : HD + 16, :] = jnp.broadcast_to(column_sum(totals[...]), (8, ROWS))
        if head == 0:
            fc_sum.two()

    stat_copies = [net.copy(stat_out.at[head], stat_in.at[head], net.pal()) for head in range(3)]
    for head in range(3):
        pl.when(helped)(partials[head].wait_recv)
        top_one, top_two = kept[head, HD : HD + 1, :], part_in[head, HD : HD + 1, :]
        peak = jnp.maximum(top_one, top_two)
        share_one, share_two = jnp.exp(top_one - peak), jnp.exp(top_two - peak)
        total = kept[head, HD + 8 : HD + 9, :] * share_one + part_in[head, HD + 8 : HD + 9, :] * share_two
        inverse = 1.0 / total
        result = (kept[head, 0:HD, :] * share_one + part_in[head, 0:HD, :] * share_two) * inverse
        delta = column_sum(qdt[head, HD:TILE, :].astype(F32) * result)
        kept[head, 0:HD, :] = result
        stat_out[head, 0:8, :] = jnp.broadcast_to(peak, (8, ROWS))
        stat_out[head, 8:16, :] = jnp.broadcast_to(inverse, (8, ROWS))
        stat_out[head, 16:24, :] = jnp.broadcast_to(delta, (8, ROWS))
        pl.when(helped)(stat_copies[head].start)
    heads[:, 0:TILE] = jnp.concatenate([kept[0, 0:HD, :], kept[1, 0:HD, :]], axis=0).T.astype(BF16)
    heads[:, TILE : 2 * TILE] = jnp.concatenate(
        [kept[2, 0:HD, :], jnp.zeros((HD, ROWS), F32)], axis=0
    ).T.astype(BF16)
    fc_sum.three()

    for half in (0, 1):
        span = slice(half * 384, half * 384 + 384)
        out_send[span, :] = (mlp_t[span, :] + dot_nt(w2[span, DENSE], heads[...])).astype(BF16)
        gq[span, DENSE] = dot(cot_t[span, :], heads[...])

    def part_of(number):
        return pl.ds(pl.multiple_of(number * PART, 16), PART)

    out_copies = [
        net.copy(out_send.at[part_of((y + step) % 4), :], out_recv.at[step - 1], net.at_y(step))
        for step in (1, 2, 3)
    ]
    start(out_copies)

    def revert(head, slot, at, stat, query, dout_t):
        chunk = head * 5 + slot
        factor = jnp.exp(tops[chunk, 0:1, :] - stat[head, 0:1, :]) * stat[head, 8:9, :]
        weight = weights[chunk]
        scaled = dout_t * factor
        d_weight = dot(kv[at, :, spans[head]], scaled.astype(BF16))
        d_score = (weight.astype(F32) * (d_weight - stat[head, 16:17, :] * factor)).astype(BF16)
        change = dot(d_score, query) + dot(weight, scaled.T.astype(BF16))
        dkv[at, :, spans[head]] = (dkv[at, :, spans[head]].astype(F32) + change).astype(BF16)
        summed[...] += dot(kv_t[chunk], d_score)

    dq_copies = [net.copy(dq_out.at[head], dq_in.at[head], net.pal()) for head in range(3)]
    returns, relays = [], []
    for head in range(3):
        returns.append(
            [
                net.copy(dkv.at[given[step - 1], :, spans[head]], from_z.at[step - 1, :, spans[head]], net.at_z(4 - step))
                for step in (1, 2, 3)
            ]
        )
        relays.append(net.copy(to_x.at[:, spans[head]], from_x.at[:, spans[head]], net.at_x(2)))

    def relay(head):
        for step in range(3):
            pl.when(either(send_own[step], send_prior[step]))(returns[head][step].wait_recv)

        @pl.when(upper)
        def _():
            total_kv[:, spans[head]] = dkv[z, :, spans[head]].astype(F32)
            for step in range(3):

                @pl.when(send_prior[step])
                def _():
                    total_kv[:, spans[head]] += from_z[step, :, spans[head]].astype(F32)

            to_x[:, spans[head]] = total_kv[:, spans[head]].astype(BF16)
            relays[head].start()

    for head in range(3):
        turned_own = qdt[head].astype(F32)
        dout_t = jnp.where(row_is_low, 0.0, turned_own)
        query = low_half(qd[:, spans[head]].astype(F32)).astype(BF16)
        summed[...] = jnp.zeros_like(summed)

        @pl.loop(0, own_count + 1)
        def _(index):
            revert(head, index, first_own + index, stat_out, query, dout_t)

        dq_t[head] = summed[0:HD, :]

        @pl.when(helps)
        def _():
            stat_copies[head].wait_recv()
            turned_in = qdt[3 + head].astype(F32)
            dout_in = jnp.where(row_is_low, 0.0, turned_in)
            query_in = low_half(qd_in[:, spans[head]].astype(F32)).astype(BF16)
            summed[...] = jnp.zeros_like(summed)

            @pl.loop(0, 3 - z)
            def _(index):
                revert(head, z + 1 + index, index, stat_in, query_in, dout_in)

            dq_out[head] = summed[0:HD, :].astype(BF16)
            dq_copies[head].start()

        for step in range(3):
            pl.when(receive[step])(returns[head][step].start)
        if head > 0:
            relay(head - 1)
        if head == 1:
            fc_sum.end(final)
    relay(2)

    for head in range(3):
        pl.when(helped)(dq_copies[head].wait_recv)
        pl.when(lower)(relays[head].wait_recv)
    total_kv[...] = dkv[block].astype(F32)
    for step in range(3):

        @pl.when(send_own[step])
        def _():
            total_kv[...] += from_z[step].astype(F32)

    @pl.when(lower)
    def _():
        total_kv[...] += from_x[...].astype(F32)

    rowsum[...] = jnp.zeros_like(rowsum)
    for index in range(4):
        rows = slice(index * TILE, index * TILE + TILE)
        turning = (cosine[rows, :], -sine_up[rows, :], -sine_down[rows, :])
        pieces = [turn(total_kv[rows, spans[head]], *turning) for head in range(3)]
        query = []
        for head in range(3):
            grad = (dq_t[head, :, rows] + dq_in[head, :, rows].astype(F32)) * 0.125
            grad = jnp.concatenate([grad, jnp.zeros((HD, TILE), F32)], axis=0).T
            query.append(turn(grad, *turning))
        pieces.append(low_half(query[0]) + swap_halves(low_half(query[1])))
        pieces.append(low_half(query[2]))
        stacked = jnp.concatenate(pieces, axis=1).astype(BF16)
        dqkv[rows, :] = stacked
        d_norm = dot_nt(stacked, w2[:, QKV])
        normed = xhat[rows, :]
        d_input = dx2[rows, :] + norm_back(small[0:1, :] * d_norm, normed, rstd[rows, 0:1])
        rowsum[0:8, :] += fold(d_norm * normed)
        rowsum[8:16, :] += fold(d_norm)
        rowsum[16:24, 0:640] += fold(stacked.astype(F32))
        dx_send[:, rows] = d_input.T.astype(BF16)

    dx_copies = [
        net.copy(dx_send.at[part_of((y + step) % 4), :], dx_recv.at[step - 1], net.at_y(step))
        for step in (1, 2, 3)
    ]

    def whole(ref, at):
        return column_sum(ref[at : at + 8, :])

    y_send[...] = jnp.concatenate(
        [whole(rowsum, 0), whole(srow, 0), whole(rowsum, 8), whole(srow, 8), jnp.zeros((4, WIDE), F32)], axis=0
    )
    y_copies = [net.copy(y_send, y_recv.at[step - 1], net.at_y(step)) for step in (1, 2, 3)]
    start(y_copies + dx_copies)
    for half in (0, 1):
        span = slice(half * 384, half * 384 + 384)
        gq[span, QKV] = dot_tn(n1[:, span], dqkv[...])
    row_id = lax.broadcasted_iota(jnp.int32, (8, 640), 0)
    lane = lanes((8, 640))
    target = jnp.where(lane >= 384, 0, jnp.where(lane % TILE < HD, 1, 2))
    qkv_rows = jnp.where(row_id == target, whole(rowsum, 16)[:, 0:640], 0.0)
    qkv_rows = jnp.concatenate([qkv_rows, pltpu.roll(qkv_rows, 640 - 1, axis=1)], axis=0)
    qkv_cols = dot_nt(qkv_rows.astype(BF16), perm[:, 0:640])
    fc1_rows = jnp.broadcast_to(whole(srow, 16), (8, WIDE))
    fc1_rows = jnp.concatenate([fc1_rows, pltpu.roll(fc1_rows, WIDE - 1, axis=1)], axis=0)
    fc1_cols = dot_nt(fc1_rows.astype(BF16), perm[:, 640:1408])
    wait(y_copies)
    shared = y_send[...] + y_recv[0] + y_recv[1] + y_recv[2]
    columns = jnp.concatenate(
        [
            jnp.zeros((SMALL, WIDE), F32),
            shared[0:4],
            jnp.zeros((2, WIDE), F32),
            fc1_cols[0:1],
            fc1_cols[8:9],
            qkv_cols[0:1],
            qkv_cols[8:9],
            qkv_cols[1:2],
            qkv_cols[9:10],
            qkv_cols[2:3],
            qkv_cols[10:11],
            jnp.zeros((50, WIDE), F32),
        ],
        axis=0,
    ).T
    lane = lanes((WIDE, TILE))
    columns = jnp.where((lane == SMALL + 4) | (lane == SMALL + 5), out_sums, columns)
    gq[:, 512:640] = jnp.where(lane < HD, gq[:, 512:640], columns)

    @pl.loop(0, 32)
    def _(index):
        rows = pl.ds(pl.multiple_of(index * 24, 8), 24)
        first = jnp.concatenate([gq[rows, 0:384], gq[rows, 640:768]], axis=1)
        second = jnp.concatenate([gq[rows, 384:640], gq[rows, 768:896], jnp.zeros((24, TILE), F32)], axis=1)
        slots[index, :, 0:EARLY] = jnp.concatenate([first, second], axis=0).astype(BF16)

    qkv_sum = Reduce(
        net, slots, 0, 256, EARLY, twin_in, halves, early_a, early_b, early_sa, early_sb, early_ea, early_eb
    )
    qkv_sum.one()
    qkv_sum.two()

    wait(out_copies + dx_copies)
    mine = part_of(y)
    total = out_send[mine, :].astype(F32) + tok_t[mine, :].astype(F32) + out_col[mine, 0:1]
    grad = dx_send[mine, :].astype(F32) + cot_own[...].astype(F32)
    for step in range(3):
        total = total + out_recv[step].astype(F32)
        grad = grad + dx_recv[step].astype(F32)
    out_t[...] = total.astype(BF16)
    grad_t[...] = grad
    qkv_sum.three()

    for head in range(3):
        pl.when(helps)(partials[head].wait_send)
        pl.when(helped)(stat_copies[head].wait_send)
        pl.when(helps)(dq_copies[head].wait_send)
        pl.when(upper)(relays[head].wait_send)
        for step in range(3):
            pl.when(either(send_own[step], send_prior[step]))(along[head][step].wait_send)
            pl.when(receive[step])(returns[head][step].wait_send)
    pl.when(helped)(lend.wait_send)
    qkv_sum.end(final)


def finish_kernel(
    out_in, grad_in, final, out_t, grad_t, gain, shift, qkv, qkv_small, dense, fc1, fc1_small, fc2, outs
):
    out_t[...] = out_in[...]
    grad_t[...] = grad_in[...]
    fc1[...] = final[0:24, EARLY:HALF]
    fc2[...] = final[24:48, EARLY:HALF]
    left = lanes((24, TILE)) < HD
    one, two, three = (final[0:24, head * TILE : head * TILE + TILE] for head in range(3))
    qkv[1, :, 0:TILE] = jnp.where(left, one, swap_halves(two))
    qkv[1, :, TILE:PART] = three[:, 0:HD]
    qkv[2, :, 0:TILE] = jnp.where(left, swap_halves(one), two)
    qkv[2, :, TILE:PART] = swap_halves(three)[:, 0:HD]
    qkv[0, :, 0:TILE] = final[24:48, 0:TILE]
    mixed = final[24:48, TILE : 2 * TILE]
    qkv[0, :, TILE:PART] = mixed[:, 0:HD]
    dense[:, 0:TILE] = final[0:24, 384:512]
    dense[:, TILE:PART] = final[24:48, 256 : 256 + HD]
    rows = jnp.concatenate([mixed, jnp.zeros((TILE - 24, TILE), F32)], axis=0).T
    gain[...] = rows[SMALL : SMALL + 2, 0:24]
    shift[...] = rows[SMALL + 2 : SMALL + 4, 0:24]
    outs[...] = rows[SMALL + 4 : SMALL + 6, 0:24]
    fc1_small[...] = rows[SMALL + 6 : SMALL + 8, 0:12]
    for which in range(3):
        at = SMALL + 8 + 2 * which
        qkv_small[which] = rows[at : at + 2, 0:3]


def permutation():
    table = np.zeros((WIDE, 1408), np.float32)
    for number in range(32):
        for row in range(12):
            source = 24 * number + row
            table[source, 640 + 64 * row + 2 * number] = 1
            if row < 3:
                table[source, 128 * row + 2 * number] = 1
                table[source, 128 * row + 64 + 2 * number] = 1
                table[source, 384 + 64 * row + 2 * number] = 1
    return table


def angle_tables():
    frequency = 10000.0 ** (-2.0 * np.arange(ROT // 2) / ROT)
    result = []
    for positions in (np.arange(ROWS), ROWS * np.arange(8)):
        phases = np.zeros((len(positions), TILE))
        phases[:, 0:ROT] = positions[:, None] * np.concatenate([frequency, frequency])[None, :]
        result.append(np.stack([np.cos(phases), np.sin(phases)]).astype(np.float32))
    return result


def call(kernel, name, shapes, scratch, collective, inputs):
    options = dict(vmem_limit_bytes=VMEM_LIMIT)
    if collective is not None:
        options.update(collective_id=collective, has_side_effects=True)
    return pl.pallas_call(
        kernel,
        name=name,
        out_shape=[jax.ShapeDtypeStruct(shape, kind) for shape, kind in shapes],
        in_specs=[pl.BlockSpec(memory_space=pltpu.VMEM)] * len(inputs),
        out_specs=[pl.BlockSpec(memory_space=pltpu.VMEM)] * len(shapes),
        scratch_shapes=scratch,
        compiler_params=pltpu.CompilerParams(**options),
    )(*inputs)


def shards(
    tokens,
    norm_gain,
    norm_bias,
    qkv_weight,
    qkv_bias,
    dense_weight,
    fc1_weight,
    fc1_bias,
    fc2_weight,
    out_bias,
    cotangent,
):
    vm = pltpu.VMEM
    dma = pltpu.SemaphoreType.DMA
    wide = (ROWS, WIDE)
    row_angles, block_angles = angle_tables()
    out_t, grad_t, final = call(
        layer_kernel,
        "layer",
        [((PART, ROWS), BF16), ((PART, ROWS), F32), ((48, HALF), F32)],
        [
            vm((32, 48, HALF), BF16),
            vm((WIDE, 2432), BF16),
            vm((16, WIDE), F32),
            vm((8, WIDE), F32),
            vm((TILE, TILE), F32),
            vm((4, 24, TILE), F32),
            vm((WIDE, TILE), F32),
            vm((ROWS, TILE), F32),
            vm((ROWS, TILE), F32),
            vm((ROWS, TILE), F32),
            vm(wide, F32),
            vm((ROWS, TILE), F32),
            vm((WIDE, ROWS), BF16),
            vm(wide, BF16),
            vm(wide, BF16),
            vm(wide, BF16),
            vm(wide, BF16),
            vm((WIDE, ROWS), BF16),
            vm(wide, BF16),
            vm((WIDE, ROWS), F32),
            vm(wide, F32),
            vm((24, WIDE), F32),
            vm((ROWS, 384), BF16),
            vm((ROWS, 384), BF16),
            vm((6, TILE, ROWS), BF16),
            vm((8, ROWS, 384), BF16),
            vm((8, ROWS, 384), BF16),
            vm((15, TILE, ROWS), BF16),
            vm((15, ROWS, ROWS), BF16),
            vm((15, 8, ROWS), F32),
            vm((8, ROWS), F32),
            vm((8, ROWS), F32),
            vm((TILE, ROWS), F32),
            vm((3, 80, ROWS), F32),
            vm((3, 80, ROWS), F32),
            vm((3, 24, ROWS), F32),
            vm((3, 24, ROWS), F32),
            vm((3, HD, ROWS), BF16),
            vm((3, HD, ROWS), BF16),
            vm((3, 80, ROWS), F32),
            vm((WIDE, 896), F32),
            vm((16, 48, HALF), BF16),
            vm((16, 48, HALF), BF16),
            vm((3, 4, 48, 256), BF16),
            vm((3, 4, 48, 256), BF16),
            vm((4, 48, 256), BF16),
            vm((4, 48, 256), BF16),
            vm((3, 48, 256), BF16),
            vm((3, 48, 256), BF16),
            vm((3, 4, 48, 384), BF16),
            vm((3, 4, 48, 384), BF16),
            vm((4, 48, 384), BF16),
            vm((4, 48, 384), BF16),
            vm((3, 48, 384), BF16),
            vm((3, 48, 384), BF16),
            vm((3, ROWS, 384), BF16),
            vm((ROWS, 384), BF16),
            vm((WIDE, ROWS), BF16),
            vm((3, PART, ROWS), BF16),
            vm((WIDE, ROWS), BF16),
            vm((3, PART, ROWS), BF16),
            vm((24, WIDE), F32),
            vm((8, WIDE), F32),
            vm((3, 8, WIDE), F32),
            dma((144,)),
            dma((144,)),
        ],
        0,
        [
            tokens[0],
            norm_gain,
            norm_bias,
            out_bias,
            jnp.transpose(qkv_weight, (1, 0, 2)),
            jnp.transpose(qkv_bias, (0, 2, 1)),
            dense_weight.T,
            fc1_weight,
            fc1_bias.T,
            fc2_weight.T,
            cotangent[0].T,
            jnp.asarray(permutation(), BF16),
            jnp.asarray(row_angles),
            jnp.asarray(block_angles),
        ],
    )
    out_t, grad_t, gain, shift, qkv, qkv_small, dense, fc1, fc1_small, fc2, outs = call(
        finish_kernel,
        "finish",
        [
            ((PART, ROWS), BF16),
            ((PART, ROWS), F32),
            ((2, 24), F32),
            ((2, 24), F32),
            ((3, 24, PART), F32),
            ((3, 2, 3), F32),
            ((24, PART), F32),
            ((24, WIDE), F32),
            ((2, 12), F32),
            ((24, WIDE), F32),
            ((2, 24), F32),
        ],
        [],
        None,
        [out_t, grad_t, final],
    )
    return (
        out_t.T[None],
        grad_t.T[None],
        gain,
        shift,
        jnp.transpose(qkv, (1, 0, 2)),
        jnp.transpose(qkv_small, (0, 2, 1)),
        dense.T,
        fc1,
        fc1_small.T,
        fc2.T,
        outs,
    )


def solution(mesh):
    return jax.shard_map(
        shards,
        mesh=mesh,
        in_specs=(
            P("dp", "ctx", None),
            P(None, ("dp", "ctx")),
            P(None, ("dp", "ctx")),
            P(("dp", "ctx"), None, "tensor"),
            P(None, "tensor", ("dp", "ctx")),
            P("tensor", ("dp", "ctx")),
            P(("dp", "ctx"), "tensor"),
            P("tensor", ("dp", "ctx")),
            P("tensor", ("dp", "ctx")),
            P(None, ("dp", "ctx")),
            P("dp", "ctx", "tensor"),
        ),
        out_specs=(
            P("dp", "ctx", "tensor"),
            P("dp", "ctx", "tensor"),
            P(None, ("dp", "ctx")),
            P(None, ("dp", "ctx")),
            P(("dp", "ctx"), None, "tensor"),
            P(None, "tensor", ("dp", "ctx")),
            P("tensor", ("dp", "ctx")),
            P(("dp", "ctx"), "tensor"),
            P("tensor", ("dp", "ctx")),
            P("tensor", ("dp", "ctx")),
            P(None, ("dp", "ctx")),
        ),
        check_vma=False,
    )
```

time: 1380 us -> 124 us (0.09)
  blocking collectives: 736 us -> 0 us
  waiting for transfers between devices: 528 us -> 0 us
  Pallas kernels: 0 us -> 122 us
  matrix products: 37.9 us -> 0 us
  local copies, waits for them, and re-layouts: 32.4 us -> 0 us
  other arithmetic: 23.7 us -> 0 us
  between operations: 16.4 us -> 0.78 us
    all_gather x8 -> x0, blocking collectives: 580 us -> none  [the longest x1 134 us: shards(): lax.all_gather(fc1_bias, ('dp', 'ctx'), axis=1, tiled=True)]
    reduce_scatter x5 -> x0, waiting for transfers between devices: 479 us -> none  [the longest x1 149 us: shards(): lax.psum_scatter(grad_fc2.astype(jnp.bfloat16), ('dp', 'ctx'), scatter_di...]
    unnamed x1 -> x0, blocking collectives: 144 us -> none
    pallas_call x0 -> x2, Pallas kernels: none -> 122 us  [call(): pl.pallas_call(kernel, name=name, out_shape=[jax.ShapeDtypeStruct(shape,...]
    dot_general x19 -> x0, matrix products: 37.9 us -> none  [the longest x1 6.8 us: shards(): jnp.einsum('std,df->stf', norm_two, fc1_full, preferred_element_type=jnp....]
    unnamed x15 -> x0, waiting for transfers between devices: 29.5 us -> none
    all_gather x4 -> x0, waiting for transfers between devices: 19.6 us -> none  [the longest x1 10.7 us: shards(): lax.all_gather(value_flat, 'ctx', axis=1, tiled=True)]
    unnamed x115 -> x0, local copies, waits for them, and re-layouts: 18.8 us -> none
  transfers between devices with their start and end apart: 12 -> 0, of which waited for: 7 -> 0; matrix products, arithmetic and copies ran while one was open for 6% -> 0% of each run, Pallas kernels for 0% -> 0%
where the time goes in v2:
time: 124 us; the launch traced here: 123 us
  Pallas kernels  122 us (98%)
    pallas_call x2, Pallas kernels, call(): pl.pallas_call(kernel, name=name, out_shape=[jax.ShapeDtypeStruct(shape,...  122 us

profile of v2, /device:TPU:0, one launch (start us, length us, event | category | flops | bytes accessed | tf_op | source)
XLA Modules:
  0.0 122.8 jit_solution(5003114555373155875)
XLA Ops:
  0.6 119.9 %layer.1 = (bf16[192,512]{1,0:T(8,128)(2,1)}, f32[192,512]{1,0:T(8,128)}, f32[48,1280]{1,0:T(8,128)}) custom-call(bf16[512,768]{1,0:T(8,128)(2,1)} %bitcast.20, bf16[2,24]{1,0:T(2,128)(2,1)} %gains.1, bf16[2,24]{1,0:T(2,128)(2,1)} %shifts.1, bf16[2,24]{1,0:T(2,128)(2,1)} %outs.1, bf16[3,24,192]{2,1,0:T(8,128)(2,1)} %bitcast.22, bf16[3,2,3]{2,1,0:T(2,128)(2,1)} %bitcast.25, ...), custom_call_target="tpu_custom_call" | custom-call | tf_op jit(solution)/shard_map/layer/pallas_call | solution.py:888
  120.5 2.1 %finish.1 = (bf16[192,512]{1,0:T(8,128)(2,1)}, f32[192,512]{1,0:T(8,128)}, f32[2,24]{1,0:T(2,128)}, f32[2,24]{1,0:T(2,128)}, f32[3,24,192]{2,1,0:T(8,128)}, /*in...) custom-call(bf16[192,512]{1,0:T(8,128)(2,1)} %get-tuple-element.25.o, ...), custom_call_target="tpu_custom_call" | custom-call | tf_op jit(solution)/shard_map/finish/pallas_call | solution.py:888

commit v3 on v2

v3 whole, which is shorter than its diff:
```python
import jax
import jax.numpy as jnp
import numpy as np
from jax import lax
from jax.experimental import pallas as pl
from jax.experimental.pallas import tpu as pltpu
from jax.sharding import PartitionSpec as P

HD = 64
ROT = 16
EPSILON = 1e-05
ROWS = 512
WIDE = 768
HALF = 1280
PART = 192
TILE = 128
MESH = pl.DeviceIdType.MESH
VMEM_LIMIT = 61 << 20
F32 = jnp.float32
BF16 = jnp.bfloat16

QKV = slice(0, 640)
DENSE = slice(640, 896)
FC1 = slice(896, 1664)
FC2 = slice(1664, 2432)
EARLY = 512
SMALL = 64


def dot(a, b):
    return lax.dot_general(a, b, (((1,), (0,)), ((), ())), preferred_element_type=F32)


def dot_nt(a, b):
    return lax.dot_general(a, b, (((1,), (1,)), ((), ())), preferred_element_type=F32)


def dot_tn(a, b):
    return lax.dot_general(a, b, (((0,), (0,)), ((), ())), preferred_element_type=F32)


def device(x, y, z, core):
    return {"dp": (x % 2) * 2 + core, "ctx": (x // 2) * 4 + z, "tensor": y}


class Links:
    def __init__(self, send, recv):
        dp = lax.axis_index("dp")
        cx = lax.axis_index("ctx")
        self.xlo, self.core, self.xhi, self.z = dp // 2, dp % 2, cx // 4, cx % 4
        self.y = lax.axis_index("tensor")
        self.x = self.xhi * 2 + self.xlo
        self.send, self.recv, self.used = send, recv, 0

    def at_x(self, step):
        return device((self.x + step) % 4, self.y, self.z, self.core)

    def at_z(self, step):
        return device(self.x, self.y, (self.z + step) % 4, self.core)

    def at_y(self, step):
        return device(self.x, (self.y + step) % 4, self.z, self.core)

    def twin(self):
        return device(self.x, self.y, self.z, 1 - self.core)

    def pal(self):
        return device((self.x + 2) % 4, self.y, 3 - self.z, self.core)

    def knock(self):
        self.barrier = pltpu.get_barrier_semaphore()
        peers = [self.twin(), self.pal()]
        for step in (1, 2, 3):
            peers += [self.at_x(step), self.at_z(step), self.at_y(step)]
        for peer in peers:
            pl.semaphore_signal(self.barrier, inc=1, device_id=peer, device_id_type=MESH)
        self.expected = len(peers)

    def enter(self):
        pl.semaphore_wait(self.barrier, self.expected)

    def take(self, count):
        self.used += count
        return self.used - count

    def copy(self, source, target, peer, number=None):
        if number is None:
            number = self.take(1)
        return pltpu.make_async_remote_copy(
            src_ref=source,
            dst_ref=target,
            send_sem=self.send.at[number],
            recv_sem=self.recv.at[number],
            device_id=peer,
            device_id_type=MESH,
        )


def start(copies):
    for item in copies:
        item.start()


def wait(copies):
    for item in copies:
        item.wait()


def lanes(shape):
    return lax.broadcasted_iota(jnp.int32, shape, len(shape) - 1)


def low_half(tile):
    return jnp.where(lanes(tile.shape) < HD, tile, 0.0)


def high_half(tile):
    return jnp.where(lanes(tile.shape) >= HD, tile, 0.0)


def swap_halves(tile):
    return pltpu.roll(tile, HD, axis=1)


def turn(tile, cosine, sine_up, sine_down):
    return (
        tile * cosine
        + pltpu.roll(tile, ROT // 2, axis=1) * sine_up
        + pltpu.roll(tile, TILE - ROT // 2, axis=1) * sine_down
    )


def fold(block):
    rows, width = block.shape
    return jnp.sum(block.reshape(rows // 8, 8, width), axis=0)


def column_sum(block):
    return jnp.sum(block, axis=0, keepdims=True)


def standardize(rows_in):
    values = rows_in.astype(F32)
    centred = values - jnp.mean(values, axis=-1, keepdims=True)
    scale = lax.rsqrt(jnp.mean(centred * centred, axis=-1, keepdims=True) + EPSILON)
    return centred * scale, scale


def norm_back(gradient, xhat, scale):
    return scale * (
        gradient
        - jnp.mean(gradient, axis=-1, keepdims=True)
        - xhat * jnp.mean(gradient * xhat, axis=-1, keepdims=True)
    )


def tile_at(index):
    return pl.ds(pl.multiple_of(index * TILE, TILE), TILE)


def quad(position):
    return (position % 2) * 2 + position // 2


class Gather:
    def __init__(self, net, slots, own, low, middle, high):
        first, second = slice(low, middle), slice(middle, high)
        mine_a, mine_b = slots.at[own, :, first], slots.at[own, :, second]
        four = slots.at[pl.ds(own - net.z, 4), :, first]
        steps = (1, 2, 3)
        self.a = [net.copy(mine_a, mine_a, net.at_z(step)) for step in steps]
        self.b = [net.copy(mine_b, mine_b, net.at_x(step)) for step in steps]
        self.mid_a = [net.copy(four, four, net.at_x(step)) for step in steps]
        self.mid_b, self.last_a, self.last_b = [], [], []
        for low in (0, 1):
            for high in (0, 1):
                piece = slots.at[((low * 2 + net.core) * 2 + high) * 4 + net.z, :, second]
                self.mid_b += [net.copy(piece, piece, net.at_z(step)) for step in steps]
            for span, copies in ((first, self.last_a), (second, self.last_b)):
                piece = slots.at[pl.ds((low * 2 + net.core) * 8, 8), :, span]
                copies.append(net.copy(piece, piece, net.twin()))

    def one(self):
        start(self.a + self.b)

    def two(self):
        wait(self.a)
        start(self.mid_a)
        wait(self.b)
        start(self.mid_b)

    def three(self):
        wait(self.mid_a)
        start(self.last_a)
        wait(self.mid_b)
        start(self.last_b)

    def end(self):
        wait(self.last_a + self.last_b)


class Reduce:
    def __init__(self, net, slots, low, middle, high, twin_in, halves, in_a, in_b, sum_a, sum_b, end_a, end_b):
        self.net, self.slots = net, slots
        self.whole, self.first, self.second = slice(low, high), slice(low, middle), slice(middle, high)
        self.bufs = (twin_in, halves, in_a, in_b, sum_a, sum_b, end_a, end_b)
        self.me = quad(net.x)
        self.twins = [
            net.copy(
                slots.at[pl.ds((low * 2 + 1 - net.core) * 8, 8), :, self.whole],
                twin_in.at[pl.ds(low * 8, 8), :, self.whole],
                net.twin(),
            )
            for low in (0, 1)
        ]
        self.mid_a, self.mid_b, self.last_a, self.last_b = [], [], [], []
        for step in (1, 2, 3):
            there = quad((net.x + step) % 4)
            self.mid_a.append(
                net.copy(halves.at[pl.ds(there * 4, 4), :, self.first], in_a.at[step - 1], net.at_x(step))
            )
            for which in range(4):
                self.mid_b.append(
                    net.copy(
                        halves.at[which * 4 + (net.z + step) % 4, :, self.second],
                        in_b.at[step - 1, which],
                        net.at_z(step),
                    )
                )
            self.last_a.append(net.copy(sum_a.at[(net.z + step) % 4], end_a.at[step - 1], net.at_z(step)))
            self.last_b.append(net.copy(sum_b.at[there], end_b.at[step - 1], net.at_x(step)))

    def one(self):
        start(self.twins)

    def two(self):
        twin_in, halves = self.bufs[:2]
        wait(self.twins)

        @pl.loop(0, 16)
        def _(index):
            source = (index // 8 * 2 + self.net.core) * 8 + index % 8
            halves[index, :, self.whole] = (
                self.slots[source, :, self.whole].astype(F32) + twin_in[index, :, self.whole].astype(F32)
            ).astype(BF16)

        start(self.mid_a + self.mid_b)

    def three(self):
        halves, in_a, in_b, sum_a, sum_b = self.bufs[1:6]
        wait(self.mid_a)

        @pl.loop(0, 4)
        def _(index):
            total = halves[self.me * 4 + index, :, self.first].astype(F32)
            for step in range(3):
                total = total + in_a[step, index].astype(F32)
            sum_a[index] = total.astype(BF16)

        start(self.last_a)
        wait(self.mid_b)

        @pl.loop(0, 4)
        def _(index):
            total = halves[index * 4 + self.net.z, :, self.second].astype(F32)
            for step in range(3):
                total = total + in_b[step, index].astype(F32)
            sum_b[index] = total.astype(BF16)

        start(self.last_b)

    def end(self, target):
        sum_a, sum_b, end_a, end_b = self.bufs[4:]
        for copies, own, arrived, span in (
            (self.last_a, sum_a.at[self.net.z], end_a, self.first),
            (self.last_b, sum_b.at[self.me], end_b, self.second),
        ):
            wait(copies)
            total = own[...].astype(F32)
            for step in range(3):
                total = total + arrived[step].astype(F32)
            target[:, span] = total


def layer_kernel(
    tok_in, gains, shifts, outs, qkv_in, qkv_small, dense_in, fc1_in, fc1_small, fc2_in, cot_in, angle_in, angle_block,
    out_t, grad_t, final,
    tok, qkv, dense, fc1, fc2, cot_own, angle_rows, loads,
    slots, w2, small, bias, small_rows, narrow, bias_rows, out_col, cosine, sine_up, sine_down, xhat, rstd, tok_t, n1, n2, dhid, act,
    cot_t, cot, mlp_t, dx2, srow, qd, qd_in, qdt, kv, dkv, kv_t, weights, tops, top, totals, summed, query_t, query_n,
    part_out, part_in, stat, dq_out, dq_in, kept, gq,
    twin_in, halves, early_a, early_b, early_sa, early_sb, early_ea, early_eb,
    late_a, late_b, late_sa, late_sb, late_ea, late_eb,
    from_z, from_x, to_x, heads, out_send, out_recv, dx_send, dx_recv, rowsum, y_send, y_recv,
    send, recv,
):
    net = Links(send, recv)
    xlo, core, xhi, z, y = net.xlo, net.core, net.xhi, net.z, net.y
    own = ((xlo * 2 + core) * 2 + xhi) * 4 + z
    block = xhi * 4 + z
    upper, lower = xhi == 1, xhi == 0
    both = jnp.logical_and
    either = jnp.logical_or
    brought = [
        pltpu.make_async_copy(source, target, loads.at[number])
        for number, (source, target) in enumerate(
            (
                (qkv_in, qkv),
                (dense_in, dense),
                (fc1_in, fc1),
                (fc2_in, fc2),
                (angle_in, angle_rows),
                (tok_in, tok),
                (cot_in, cot_own),
            )
        )
    ]
    start(brought)
    helps = both(lower, z <= 2)
    helped = both(upper, z >= 1)
    dq_t = kept.at[:, 0:HD, :]
    dqkv = n2.at[:, QKV]
    total_kv = gq.at[0:ROWS, 0:384]
    net.knock()

    wait(brought[0:4])
    narrow[...] = jnp.zeros_like(narrow)
    for which in range(3):
        narrow[which, :, 0:HD] = qkv[which, :, TILE:PART].astype(F32)
    narrow[3, :, 0:HD] = dense[:, TILE:PART].astype(F32)
    small_rows[...] = jnp.zeros_like(small_rows)
    small_rows[SMALL : SMALL + 2, 0:24] = gains[...].astype(F32)
    small_rows[SMALL + 2 : SMALL + 4, 0:24] = shifts[...].astype(F32)
    small_rows[SMALL + 4 : SMALL + 6, 0:24] = outs[...].astype(F32)
    columns = small_rows[...].T[0:24]

    small_rows[...] = jnp.zeros_like(small_rows)
    small_rows[0:2, 0:12] = fc1_small[...].astype(F32)
    for which in range(3):
        small_rows[8 + 8 * which : 10 + 8 * which, 0:3] = qkv_small[which].astype(F32)
    turned = small_rows[...].T[0:16]
    pair_lane = lanes((16, TILE)) < 2
    bias_rows[0:16, :] = jnp.where(pair_lane, turned, 0.0)
    bias_rows[16:24, :] = jnp.zeros((8, TILE), F32)
    for which in range(3):
        moved = pltpu.roll(turned, TILE - 8 - 8 * which, axis=1)
        bias_rows[12 + 3 * which : 15 + 3 * which, :] = jnp.where(pair_lane, moved, 0.0)[0:3]
    biases = pltpu.roll(bias_rows[...], 2 * own, axis=1)
    key = qkv[1, :, 0:TILE].astype(F32)
    value = qkv[2, :, 0:TILE].astype(F32)
    left = lanes((24, TILE)) < HD
    top_half = jnp.concatenate(
        [
            jnp.where(left, key, swap_halves(value)),
            jnp.where(left, swap_halves(key), value),
            narrow[1] + swap_halves(narrow[2]),
            dense[:, 0:TILE].astype(F32),
        ],
        axis=1,
    )
    bottom_half = jnp.concatenate(
        [qkv[0, :, 0:TILE].astype(F32), narrow[0] + columns, narrow[3], biases], axis=1
    )
    slots[own, :, 0:EARLY] = jnp.concatenate([top_half, bottom_half], axis=0).astype(BF16)
    slots[own, :, EARLY:HALF] = jnp.concatenate([fc1[...].astype(F32), fc2[...].astype(F32)], axis=0).astype(BF16)
    net.enter()
    early = Gather(net, slots, own, 0, 256, EARLY)
    late = Gather(net, slots, own, EARLY, 896, HALF)
    early.one()

    wait(brought[4:7])
    row_cos, row_sin = angle_rows[0], angle_rows[1]
    block_cos, block_sin = angle_block[0, pl.ds(block, 1), :], angle_block[1, pl.ds(block, 1), :]
    cosine[...] = row_cos * block_cos - row_sin * block_sin
    sine = row_sin * block_cos + row_cos * block_sin
    upward = lanes((ROWS, TILE)) >= ROT // 2
    sine_up[...] = jnp.where(upward, sine, 0.0)
    sine_down[...] = jnp.where(upward, 0.0, -sine)

    early.two()
    late.one()
    mine_t = cot_t.at[pl.ds(pl.multiple_of(y * PART, 16), PART), :]
    gather_y = [net.copy(cot_own, mine_t, net.at_y(step)) for step in (1, 2, 3)]
    start(gather_y)
    mine_t[...] = cot_own[...]

    @pl.loop(0, 4)
    def _(index):
        rows = tile_at(index)
        normed, scale = standardize(tok[rows, :])
        xhat[rows, :] = normed
        rstd[rows, :] = jnp.broadcast_to(scale, (TILE, TILE))


    @pl.loop(0, 4)
    def _(index):
        rows = tile_at(index)
        tok_t[:, rows] = tok[rows, :].astype(F32).T.astype(BF16)

    early.three()
    dkv[...] = jnp.zeros_like(dkv)
    early.end()
    bias_rows[...] = jnp.zeros_like(bias_rows)

    @pl.loop(0, 16)
    def _(pair):
        rows = pl.ds(pl.multiple_of(pair * 48, 16), 48)
        one = slots[2 * pair, :, 0:EARLY].astype(F32)
        two = slots[2 * pair + 1, :, 0:EARLY].astype(F32)
        upper_rows = jnp.concatenate([one[0:24], two[0:24]], axis=0).astype(BF16)
        lower_rows = jnp.concatenate([one[24:48], two[24:48]], axis=0).astype(BF16)
        w2[rows, 0:384] = upper_rows[:, 0:384]
        w2[rows, 640:768] = upper_rows[:, 384:512]
        w2[rows, 384:640] = lower_rows[:, 0:256]
        w2[rows, 768:896] = lower_rows[:, 256:384]
        bias_rows[...] += one[24:48, 384:512] + two[24:48, 384:512]

    column_form = w2[:, 512:640].astype(F32)
    out_col[...] = jnp.broadcast_to(
        column_form[:, SMALL + 4 : SMALL + 5] + column_form[:, SMALL + 5 : SMALL + 6], (WIDE, TILE)
    )
    turned = column_form.T[SMALL : SMALL + 16, :]
    small[...] = turned
    even, odd = bias_rows[...], swap_halves(bias_rows[...])
    for number in range(6):
        bias[1:2, number * TILE : number * TILE + TILE] = (
            even[2 * number : 2 * number + 1] + odd[2 * number + 1 : 2 * number + 2]
        )
    for head in range(3):
        bias[0:1, head * TILE : head * TILE + TILE] = even[15 + head : 16 + head] + odd[18 + head : 19 + head]
    bias[0:1, 384:512] = even[12:13] + odd[13:14]
    bias[0:1, 512:640] = even[14:15]

    @pl.loop(0, 4)
    def _(index):
        rows = tile_at(index)
        normed = xhat[rows, :]
        one = (normed * small[0:1, :] + small[2:3, :]).astype(BF16)
        n1[rows, :] = one
        n2[rows, :] = (normed * small[1:2, :] + small[3:4, :]).astype(BF16)
        projected = dot(one, w2[:, QKV]) + bias[0:1, 0:640]
        turning = (cosine[rows, :], sine_up[rows, :], sine_down[rows, :])
        for head in range(3):
            span = slice(head * TILE, head * TILE + TILE)
            kv[block, rows, span] = turn(projected[:, span], *turning).astype(BF16)
        pair, last = projected[:, 384:512], projected[:, 512:640]
        for head, tile in enumerate((pair, swap_halves(pair), last)):
            span = slice(head * TILE, head * TILE + TILE)
            qd[rows, span] = (low_half(turn(low_half(tile), *turning)) * 0.125).astype(BF16)

    spans = [slice(head * TILE, head * TILE + TILE) for head in range(3)]
    send_own, send_prior, receive, given = [], [], [], []
    for step in (1, 2, 3):
        behind = z + step <= 3
        send_own.append(either(behind, both(lower, both(z + step == 4, z <= 2))))
        send_prior.append(both(upper, z + step > 3))
        receive.append(either(upper, either(z - step >= 0, both(z == 0, step >= 2))))
        given.append((z - step + 4) % 4 + 4 * xhi * ((z - step + 4) // 4))
    head_span = lambda head: pl.ds(pl.multiple_of(head * TILE, TILE), TILE)
    across_at, along_at, return_at, relay_at, part_at, stat_at, dq_at = (
        net.take(count) for count in (3, 9, 9, 3, 3, 3, 3)
    )

    def across(head):
        mine = kv.at[block, :, head_span(head)]
        return net.copy(mine, mine, net.at_x(2), across_at + head)

    def along(head, step):
        piece = kv.at[block - 4 * xhi * ((z + step + 1) // 4), :, head_span(head)]
        return net.copy(piece, piece, net.at_z(step + 1), along_at + 3 * head + step)

    @pl.loop(0, 3)
    def _(head):
        pl.when(lower)(across(head).start)
        for step in range(3):
            pl.when(send_own[step])(along(head, step).start)


    wait(gather_y)

    @pl.loop(0, 4)
    def _(index):
        rows = tile_at(index)
        cot[rows, :] = cot_t[:, rows].astype(F32).T.astype(BF16)

    out_sums = jnp.sum(cot_t[...].astype(F32), axis=1, keepdims=True)

    @pl.loop(0, 4)
    def _(index):
        rows = tile_at(index)
        d_heads = dot(cot[rows, :], w2[:, DENSE])
        pair, last = d_heads[:, 0:TILE], d_heads[:, TILE : 2 * TILE]
        for head, tile in enumerate((swap_halves(pair), pair, swap_halves(last))):
            qd[rows, spans[head]] = (qd[rows, spans[head]].astype(F32) + high_half(tile)).astype(BF16)

    lend = net.copy(qd, qd_in, net.pal())
    pl.when(helped)(lend.start)

    @pl.loop(0, 3)
    def _(head):
        pl.when(upper)(across(head).wait_recv)
        for step in range(3):
            pl.when(send_prior[step])(along(head, step).start)

    row_is_low = lax.broadcasted_iota(jnp.int32, (TILE, ROWS), 0) < HD
    lent_count = (1 - xhi) * (3 - z)
    chunk_count = 4 + xhi

    def chunk_place(index):
        which = (lent_count + 7 - index) // 8
        return which, index - lent_count * (1 - which) + xhi * z

    def partial(head):
        return net.copy(part_out.at[head], part_in.at[head], net.pal(), part_at + head)

    def stat_copy(head):
        return net.copy(stat.at[0, head], stat.at[1, head], net.pal(), stat_at + head)

    def dq_copy(head):
        return net.copy(dq_out.at[head], dq_in.at[head], net.pal(), dq_at + head)

    def outcome(target, head, which):
        target[head, 0:HD, :] = summed[which, HD:TILE, :]
        target[head, HD : HD + 8, :] = top[which]
        target[head, HD + 8 : HD + 16, :] = jnp.broadcast_to(column_sum(totals[which]), (8, ROWS))

    @pl.when(jnp.logical_not(helped))
    def _():
        part_in[...] = jnp.zeros_like(part_in)
        part_in[:, HD : HD + 8, :] = jnp.full((3, 8, ROWS), -1e30, F32)
        dq_in[...] = jnp.zeros_like(dq_in)

    pl.when(helps)(lend.wait_recv)

    @pl.loop(0, 3)
    def _(head):
        span = head_span(head)
        pl.when(lower)(across(head).wait_send)
        for step in range(3):
            pl.when(receive[step])(along(head, step).wait_recv)

        def turn_queries(source, which):
            turned = source[:, span].astype(F32).T
            qdt[which * 3 + head] = turned.astype(BF16)
            query_t[which] = jnp.where(row_is_low, turned, 0.0).astype(BF16)

        turn_queries(qd, 0)
        pl.when(helps)(lambda: turn_queries(qd_in, 1))
        top[...] = jnp.full_like(top, -1e30)
        totals[...] = jnp.zeros_like(totals)
        summed[...] = jnp.zeros_like(summed)

        @pl.loop(0, chunk_count)
        def _(index):
            which, at = chunk_place(index)
            chunk = head * 5 + index
            tile = kv[at, :, span]
            tile_t = tile.astype(F32).T.astype(BF16)
            kv_t[chunk] = tile_t
            key_shift = (at - block - which * (7 - 2 * block)) * ROWS
            parts = [slice(half * 256, half * 256 + 256) for half in (0, 1)]
            scores = [dot(tile, query_t[which, :, part]) for part in parts]
            before = [top[which, 0:1, part] for part in parts]
            old_total = [totals[which, :, part] for part in parts]
            old_sum = [summed[which, :, part] for part in parts]
            for half, part in enumerate(parts):
                score = scores[half]
                key_at = lax.broadcasted_iota(jnp.int32, score.shape, 0) + key_shift
                query_at = lax.broadcasted_iota(jnp.int32, score.shape, 1) + half * 256
                score = jnp.where(key_at <= query_at, score, -1e30)
                peak = jnp.maximum(before[half], jnp.max(score, axis=0, keepdims=True))
                weight = jnp.exp(score - peak)
                shrink = jnp.exp(before[half] - peak)
                rounded = weight.astype(BF16)
                weights[chunk, :, part] = rounded
                peaks = jnp.broadcast_to(peak, (8, 256))
                tops[chunk, :, part] = peaks
                top[which, :, part] = peaks
                totals[which, :, part] = old_total[half] * shrink + fold(weight)
                summed[which, :, part] = old_sum[half] * shrink + dot(tile_t, rounded)

            @pl.when(both(helps, index == lent_count - 1))
            def _():
                outcome(part_out, head, 1)
                partial(head).start()

        outcome(kept, head, 0)
        pl.when(head == 1)(late.two)

    @pl.loop(0, 3)
    def _(head):
        pl.when(helped)(partial(head).wait_recv)
        top_one, top_two = kept[head, HD : HD + 1, :], part_in[head, HD : HD + 1, :]
        peak = jnp.maximum(top_one, top_two)
        share_one, share_two = jnp.exp(top_one - peak), jnp.exp(top_two - peak)
        total = kept[head, HD + 8 : HD + 9, :] * share_one + part_in[head, HD + 8 : HD + 9, :] * share_two
        inverse = 1.0 / total
        result = (kept[head, 0:HD, :] * share_one + part_in[head, 0:HD, :] * share_two) * inverse
        delta = column_sum(qdt[head, HD:TILE, :].astype(F32) * result)
        kept[head, 0:HD, :] = result
        stat[0, head, 0:8, :] = jnp.broadcast_to(peak, (8, ROWS))
        stat[0, head, 8:16, :] = jnp.broadcast_to(inverse, (8, ROWS))
        stat[0, head, 16:24, :] = jnp.broadcast_to(delta, (8, ROWS))
        pl.when(helped)(stat_copy(head).start)

    heads[:, 0:TILE] = jnp.concatenate([kept[0, 0:HD, :], kept[1, 0:HD, :]], axis=0).T.astype(BF16)
    heads[:, TILE : 2 * TILE] = jnp.concatenate(
        [kept[2, 0:HD, :], jnp.zeros((HD, ROWS), F32)], axis=0
    ).T.astype(BF16)
    late.three()

    def give_back(head, step):
        return net.copy(
            dkv.at[given[step], :, head_span(head)],
            from_z.at[step, :, head_span(head)],
            net.at_z(3 - step),
            return_at + 3 * head + step,
        )

    def relay_copy(head):
        return net.copy(to_x.at[:, head_span(head)], from_x.at[:, head_span(head)], net.at_x(2), relay_at + head)

    def relay(head):
        span = head_span(head)
        for step in range(3):
            pl.when(either(send_own[step], send_prior[step]))(give_back(head, step).wait_recv)

        @pl.when(upper)
        def _():
            total_kv[:, span] = dkv[z, :, span].astype(F32)
            for step in range(3):

                @pl.when(send_prior[step])
                def _():
                    total_kv[:, span] += from_z[step, :, span].astype(F32)

            to_x[:, span] = total_kv[:, span].astype(BF16)
            relay_copy(head).start()

    @pl.loop(0, 3)
    def _(head):
        span = head_span(head)
        query_n[0] = low_half(qd[:, span].astype(F32)).astype(BF16)

        @pl.when(helps)
        def _():
            query_n[1] = low_half(qd_in[:, span].astype(F32)).astype(BF16)

        summed[...] = jnp.zeros_like(summed)

        @pl.loop(0, chunk_count)
        def _(turn_of):
            index = (turn_of + lent_count) % chunk_count
            which, at = chunk_place(index)
            chunk = head * 5 + index
            pl.when(both(helps, turn_of == chunk_count - lent_count))(stat_copy(head).wait_recv)
            change = dkv[at, :, span].astype(F32)
            for half in (0, 1):
                part = slice(half * 256, half * 256 + 256)
                factor = jnp.exp(tops[chunk, 0:1, part] - stat[which, head, 0:1, part]) * stat[which, head, 8:9, part]
                weight = weights[chunk, :, part]
                scaled = jnp.where(
                    row_is_low[:, 0:256], 0.0, qdt[which * 3 + head, :, part].astype(F32) * factor
                )
                d_weight = dot(kv[at, :, span], scaled.astype(BF16))
                d_score = (
                    weight.astype(F32) * (d_weight - stat[which, head, 16:17, part] * factor)
                ).astype(BF16)
                change = change + dot(d_score, query_n[which, part, :]) + dot(weight, scaled.T.astype(BF16))
                summed[which, :, part] += dot(kv_t[chunk], d_score)
            dkv[at, :, span] = change.astype(BF16)

        dq_t[head] = summed[0, 0:HD, :]

        @pl.when(helps)
        def _():
            dq_out[head] = summed[1, 0:HD, :].astype(BF16)
            dq_copy(head).start()

        for step in range(3):
            pl.when(receive[step])(give_back(head, step).start)
        pl.when(head > 0)(lambda: relay(head - 1))

    late.end()

    @pl.loop(0, 16)
    def _(pair):
        rows = pl.ds(pl.multiple_of(pair * 48, 16), 48)
        one = slots[2 * pair, :, EARLY:HALF].astype(F32)
        two = slots[2 * pair + 1, :, EARLY:HALF].astype(F32)
        w2[rows, FC1] = jnp.concatenate([one[0:24], two[0:24]], axis=0).astype(BF16)
        w2[rows, FC2] = jnp.concatenate([one[24:48], two[24:48]], axis=0).astype(BF16)

    srow[...] = jnp.zeros_like(srow)

    @pl.loop(0, 4)
    def _(index):
        rows = tile_at(index)
        hidden = dot(n2[rows, :], w2[:, FC1]) + bias[1:2, :]
        spread_to = 0.5 + 0.5 * lax.erf(hidden * (0.5**0.5))
        act[rows, :] = (hidden * spread_to).astype(BF16)
        slope = spread_to + hidden * jnp.exp(-0.5 * hidden * hidden) * 0.3989422804014327
        d_hidden = (slope * dot(cot[rows, :], w2[:, FC2])).astype(BF16)
        dhid[rows, :] = d_hidden
        d_norm = dot_nt(d_hidden, w2[:, FC1])
        normed = xhat[rows, :]
        dx2[rows, :] = norm_back(small[1:2, :] * d_norm, normed, rstd[rows, 0:1])
        srow[0:8, :] += fold(d_norm * normed)
        srow[8:16, :] += fold(d_norm)
        srow[16:24, :] += fold(d_hidden.astype(F32))

    relay(2)

    for half in (0, 1):
        span = slice(half * 384, half * 384 + 384)
        mlp_t[span, :] = dot_nt(w2[span, FC2], act[...])
        gq[0:384, 0:WIDE] = dot_tn(n2[:, span], dhid[...])
        gq[384:768, 0:WIDE] = dot(cot_t[span, :], act[...])

        @pl.loop(0, 16)
        def _(index):
            first = pl.ds(pl.multiple_of(index * 24, 8), 24)
            second = pl.ds(pl.multiple_of(384 + index * 24, 8), 24)
            slots[half * 16 + index, :, EARLY:HALF] = jnp.concatenate(
                [gq[first, 0:WIDE], gq[second, 0:WIDE]], axis=0
            ).astype(BF16)

    fc_sum = Reduce(
        net, slots, EARLY, 896, HALF, twin_in, halves, late_a, late_b, late_sa, late_sb, late_ea, late_eb
    )
    fc_sum.one()

    for half in (0, 1):
        span = slice(half * 384, half * 384 + 384)
        out_send[span, :] = (mlp_t[span, :] + dot_nt(w2[span, DENSE], heads[...])).astype(BF16)
        gq[span, DENSE] = dot(cot_t[span, :], heads[...])

    def part_of(number):
        return pl.ds(pl.multiple_of(number * PART, 16), PART)

    out_copies = [
        net.copy(out_send.at[part_of((y + step) % 4), :], out_recv.at[step - 1], net.at_y(step))
        for step in (1, 2, 3)
    ]
    start(out_copies)


    @pl.loop(0, 3)
    def _(head):
        pl.when(helped)(dq_copy(head).wait_recv)
        pl.when(lower)(relay_copy(head).wait_recv)

    total_kv[...] = dkv[block].astype(F32)
    for step in range(3):

        @pl.when(send_own[step])
        def _():
            total_kv[...] += from_z[step].astype(F32)

    @pl.when(lower)
    def _():
        total_kv[...] += from_x[...].astype(F32)

    fc_sum.two()
    rowsum[...] = jnp.zeros_like(rowsum)

    @pl.loop(0, 4)
    def _(index):
        rows = tile_at(index)
        turning = (cosine[rows, :], -sine_up[rows, :], -sine_down[rows, :])
        pieces = [turn(total_kv[rows, spans[head]], *turning) for head in range(3)]
        query = []
        for head in range(3):
            grad = (dq_t[head, :, rows] + dq_in[head, :, rows].astype(F32)) * 0.125
            grad = jnp.concatenate([grad, jnp.zeros((HD, TILE), F32)], axis=0).T
            query.append(turn(grad, *turning))
        pieces.append(low_half(query[0]) + swap_halves(low_half(query[1])))
        pieces.append(low_half(query[2]))
        stacked = jnp.concatenate(pieces, axis=1).astype(BF16)
        dqkv[rows, :] = stacked
        d_norm = dot_nt(stacked, w2[:, QKV])
        normed = xhat[rows, :]
        d_input = dx2[rows, :] + norm_back(small[0:1, :] * d_norm, normed, rstd[rows, 0:1])
        rowsum[0:8, :] += fold(d_norm * normed)
        rowsum[8:16, :] += fold(d_norm)
        rowsum[16:24, 0:640] += fold(stacked.astype(F32))
        dx_send[:, rows] = d_input.T.astype(BF16)

    dx_copies = [
        net.copy(dx_send.at[part_of((y + step) % 4), :], dx_recv.at[step - 1], net.at_y(step))
        for step in (1, 2, 3)
    ]

    def whole(ref, at):
        return column_sum(ref[at : at + 8, :])

    y_send[...] = jnp.concatenate(
        [whole(rowsum, 0), whole(srow, 0), whole(rowsum, 8), whole(srow, 8), jnp.zeros((4, WIDE), F32)], axis=0
    )
    y_copies = [net.copy(y_send, y_recv.at[step - 1], net.at_y(step)) for step in (1, 2, 3)]
    start(y_copies + dx_copies)
    for half in (0, 1):
        span = slice(half * 384, half * 384 + 384)
        gq[span, QKV] = dot_tn(n1[:, span], dqkv[...])
    fc1_sum, qkv_total = whole(srow, 16), whole(rowsum, 16)
    pieces = []
    for number in range(12):
        pieces.append(fc1_sum[:, number // 2 * TILE : number // 2 * TILE + TILE])
    for number in (3, 3, 4, 0, 1, 2, 0, 1, 2):
        pieces.append(qkv_total[:, number * TILE : number * TILE + TILE])
    pieces.append(jnp.zeros((3, TILE), F32))
    bias_grads = jnp.concatenate(pieces, axis=0)
    row = lax.broadcasted_iota(jnp.int32, (24, TILE), 0)
    swapped = ((row < 12) & (row % 2 == 1)) | (row == 13) | (row >= 18)
    bias_rows[...] = jnp.where(swapped, swap_halves(bias_grads), bias_grads)
    wait(y_copies)
    shared = y_send[...] + y_recv[0] + y_recv[1] + y_recv[2]
    columns = jnp.concatenate(
        [
            jnp.zeros((SMALL, WIDE), F32),
            shared[0:4],
            jnp.zeros((2, WIDE), F32),
            jnp.zeros((58, WIDE), F32),
        ],
        axis=0,
    ).T
    lane = lanes((WIDE, TILE))
    columns = jnp.where((lane == SMALL + 4) | (lane == SMALL + 5), out_sums, columns)
    gq[:, 512:640] = jnp.where(lane < HD, gq[:, 512:640], columns)

    @pl.loop(0, 32)
    def _(index):
        rows = pl.ds(pl.multiple_of(index * 24, 8), 24)
        first = jnp.concatenate([gq[rows, 0:384], gq[rows, 640:768]], axis=1)
        second = jnp.concatenate([gq[rows, 384:640], gq[rows, 768:896], bias_rows[...]], axis=1)
        slots[index, :, 0:EARLY] = jnp.concatenate([first, second], axis=0).astype(BF16)

    fc_sum.three()
    qkv_sum = Reduce(
        net, slots, 0, 256, EARLY, twin_in, halves, early_a, early_b, early_sa, early_sb, early_ea, early_eb
    )
    qkv_sum.one()
    qkv_sum.two()

    wait(out_copies + dx_copies)
    mine = part_of(y)
    total = out_send[mine, :].astype(F32) + tok_t[mine, :].astype(F32) + out_col[mine, 0:1]
    grad = dx_send[mine, :].astype(F32) + cot_own[...].astype(F32)
    for step in range(3):
        total = total + out_recv[step].astype(F32)
        grad = grad + dx_recv[step].astype(F32)
    out_t[...] = total.astype(BF16)
    grad_t[...] = grad
    qkv_sum.three()

    @pl.loop(0, 3)
    def _(head):
        pl.when(helps)(partial(head).wait_send)
        pl.when(helped)(stat_copy(head).wait_send)
        pl.when(helps)(dq_copy(head).wait_send)
        pl.when(upper)(relay_copy(head).wait_send)
        for step in range(3):
            pl.when(either(send_own[step], send_prior[step]))(along(head, step).wait_send)
            pl.when(receive[step])(give_back(head, step).wait_send)

    pl.when(helped)(lend.wait_send)
    fc_sum.end(final)
    qkv_sum.end(final)


def finish_kernel(
    out_in, grad_in, final, out_t, grad_t, gain, shift, qkv, qkv_small, dense, fc1, fc1_small, fc2, outs
):
    out_t[...] = out_in[...]
    grad_t[...] = grad_in[...]
    fc1[...] = final[0:24, EARLY:HALF]
    fc2[...] = final[24:48, EARLY:HALF]
    left = lanes((24, TILE)) < HD
    one, two, three = (final[0:24, head * TILE : head * TILE + TILE] for head in range(3))
    qkv[1, :, 0:TILE] = jnp.where(left, one, swap_halves(two))
    qkv[1, :, TILE:PART] = three[:, 0:HD]
    qkv[2, :, 0:TILE] = jnp.where(left, swap_halves(one), two)
    qkv[2, :, TILE:PART] = swap_halves(three)[:, 0:HD]
    qkv[0, :, 0:TILE] = final[24:48, 0:TILE]
    mixed = final[24:48, TILE : 2 * TILE]
    qkv[0, :, TILE:PART] = mixed[:, 0:HD]
    dense[:, 0:TILE] = final[0:24, 384:512]
    dense[:, TILE:PART] = final[24:48, 256 : 256 + HD]
    rows = jnp.concatenate([mixed, jnp.zeros((TILE - 24, TILE), F32)], axis=0).T
    gain[...] = rows[SMALL : SMALL + 2, 0:24]
    shift[...] = rows[SMALL + 2 : SMALL + 4, 0:24]
    outs[...] = rows[SMALL + 4 : SMALL + 6, 0:24]
    own = lax.axis_index("dp") * 8 + lax.axis_index("ctx")
    moved = pltpu.roll(final[24:48, 384:512], TILE - 2 * own, axis=1)
    rows = jnp.concatenate([moved, jnp.zeros((TILE - 24, TILE), F32)], axis=0).T
    fc1_small[...] = rows[0:2, 0:12]
    for which in range(3):
        qkv_small[which] = pltpu.roll(rows[0:8], TILE - 12 - 3 * which, axis=1)[0:2, 0:3]


def angle_tables():
    frequency = 10000.0 ** (-2.0 * np.arange(ROT // 2) / ROT)
    result = []
    for positions in (np.arange(ROWS), ROWS * np.arange(8)):
        phases = np.zeros((len(positions), TILE))
        phases[:, 0:ROT] = positions[:, None] * np.concatenate([frequency, frequency])[None, :]
        result.append(np.stack([np.cos(phases), np.sin(phases)]).astype(np.float32))
    return result


def call(kernel, name, shapes, scratch, collective, inputs, outside=()):
    options = dict(vmem_limit_bytes=VMEM_LIMIT)
    if collective is not None:
        options.update(collective_id=collective, has_side_effects=True)
    return pl.pallas_call(
        kernel,
        name=name,
        out_shape=[jax.ShapeDtypeStruct(shape, kind) for shape, kind in shapes],
        in_specs=[
            pl.BlockSpec(memory_space=pl.ANY if number in outside else pltpu.VMEM)
            for number in range(len(inputs))
        ],
        out_specs=[pl.BlockSpec(memory_space=pltpu.VMEM)] * len(shapes),
        scratch_shapes=scratch,
        compiler_params=pltpu.CompilerParams(**options),
    )(*inputs)


def shards(
    tokens,
    norm_gain,
    norm_bias,
    qkv_weight,
    qkv_bias,
    dense_weight,
    fc1_weight,
    fc1_bias,
    fc2_weight,
    out_bias,
    cotangent,
):
    vm = pltpu.VMEM
    dma = pltpu.SemaphoreType.DMA
    wide = (ROWS, WIDE)
    row_angles, block_angles = angle_tables()
    out_t, grad_t, final = call(
        layer_kernel,
        "layer",
        [((PART, ROWS), BF16), ((PART, ROWS), F32), ((48, HALF), F32)],
        [
            vm(wide, BF16),
            vm((3, 24, PART), BF16),
            vm((24, PART), BF16),
            vm((24, WIDE), BF16),
            vm((24, WIDE), BF16),
            vm((PART, ROWS), BF16),
            vm((2, ROWS, TILE), F32),
            dma((7,)),
            vm((32, 48, HALF), BF16),
            vm((WIDE, 2432), BF16),
            vm((16, WIDE), F32),
            vm((8, WIDE), F32),
            vm((TILE, TILE), F32),
            vm((4, 24, TILE), F32),
            vm((24, TILE), F32),
            vm((WIDE, TILE), F32),
            vm((ROWS, TILE), F32),
            vm((ROWS, TILE), F32),
            vm((ROWS, TILE), F32),
            vm(wide, F32),
            vm((ROWS, TILE), F32),
            vm((WIDE, ROWS), BF16),
            vm(wide, BF16),
            vm(wide, BF16),
            vm(wide, BF16),
            vm(wide, BF16),
            vm((WIDE, ROWS), BF16),
            vm(wide, BF16),
            vm((WIDE, ROWS), F32),
            vm(wide, F32),
            vm((24, WIDE), F32),
            vm((ROWS, 384), BF16),
            vm((ROWS, 384), BF16),
            vm((6, TILE, ROWS), BF16),
            vm((8, ROWS, 384), BF16),
            vm((8, ROWS, 384), BF16),
            vm((15, TILE, ROWS), BF16),
            vm((15, ROWS, ROWS), BF16),
            vm((15, 8, ROWS), F32),
            vm((2, 8, ROWS), F32),
            vm((2, 8, ROWS), F32),
            vm((2, TILE, ROWS), F32),
            vm((2, TILE, ROWS), BF16),
            vm((2, ROWS, TILE), BF16),
            vm((3, 80, ROWS), F32),
            vm((3, 80, ROWS), F32),
            vm((2, 3, 24, ROWS), F32),
            vm((3, HD, ROWS), BF16),
            vm((3, HD, ROWS), BF16),
            vm((3, 80, ROWS), F32),
            vm((WIDE, 896), F32),
            vm((16, 48, HALF), BF16),
            vm((16, 48, HALF), BF16),
            vm((3, 4, 48, 256), BF16),
            vm((3, 4, 48, 256), BF16),
            vm((4, 48, 256), BF16),
            vm((4, 48, 256), BF16),
            vm((3, 48, 256), BF16),
            vm((3, 48, 256), BF16),
            vm((3, 4, 48, 384), BF16),
            vm((3, 4, 48, 384), BF16),
            vm((4, 48, 384), BF16),
            vm((4, 48, 384), BF16),
            vm((3, 48, 384), BF16),
            vm((3, 48, 384), BF16),
            vm((3, ROWS, 384), BF16),
            vm((ROWS, 384), BF16),
            vm((ROWS, 384), BF16),
            vm((ROWS, 256), BF16),
            vm((WIDE, ROWS), BF16),
            vm((3, PART, ROWS), BF16),
            vm((WIDE, ROWS), BF16),
            vm((3, PART, ROWS), BF16),
            vm((24, WIDE), F32),
            vm((8, WIDE), F32),
            vm((3, 8, WIDE), F32),
            dma((144,)),
            dma((144,)),
        ],
        0,
        [
            tokens[0],
            norm_gain,
            norm_bias,
            out_bias,
            jnp.transpose(qkv_weight, (1, 0, 2)),
            jnp.transpose(qkv_bias, (0, 2, 1)),
            dense_weight.T,
            fc1_weight,
            fc1_bias.T,
            fc2_weight.T,
            cotangent[0].T,
            jnp.asarray(row_angles),
            jnp.asarray(block_angles),
        ],
        (0, 4, 6, 7, 9, 10, 11),
    )
    out_t, grad_t, gain, shift, qkv, qkv_small, dense, fc1, fc1_small, fc2, outs = call(
        finish_kernel,
        "finish",
        [
            ((PART, ROWS), BF16),
            ((PART, ROWS), F32),
            ((2, 24), F32),
            ((2, 24), F32),
            ((3, 24, PART), F32),
            ((3, 2, 3), F32),
            ((24, PART), F32),
            ((24, WIDE), F32),
            ((2, 12), F32),
            ((24, WIDE), F32),
            ((2, 24), F32),
        ],
        [],
        None,
        [out_t, grad_t, final],
    )
    return (
        out_t.T[None],
        grad_t.T[None],
        gain,
        shift,
        jnp.transpose(qkv, (1, 0, 2)),
        jnp.transpose(qkv_small, (0, 2, 1)),
        dense.T,
        fc1,
        fc1_small.T,
        fc2.T,
        outs,
    )


def solution(mesh):
    return jax.shard_map(
        shards,
        mesh=mesh,
        in_specs=(
            P("dp", "ctx", None),
            P(None, ("dp", "ctx")),
            P(None, ("dp", "ctx")),
            P(("dp", "ctx"), None, "tensor"),
            P(None, "tensor", ("dp", "ctx")),
            P("tensor", ("dp", "ctx")),
            P(("dp", "ctx"), "tensor"),
            P("tensor", ("dp", "ctx")),
            P("tensor", ("dp", "ctx")),
            P(None, ("dp", "ctx")),
            P("dp", "ctx", "tensor"),
        ),
        out_specs=(
            P("dp", "ctx", "tensor"),
            P("dp", "ctx", "tensor"),
            P(None, ("dp", "ctx")),
            P(None, ("dp", "ctx")),
            P(("dp", "ctx"), None, "tensor"),
            P(None, "tensor", ("dp", "ctx")),
            P("tensor", ("dp", "ctx")),
            P(("dp", "ctx"), "tensor"),
            P("tensor", ("dp", "ctx")),
            P("tensor", ("dp", "ctx")),
            P(None, ("dp", "ctx")),
        ),
        check_vma=False,
    )
```

time: 124 us -> 126 us (1.016)
  Pallas kernels: 122 us -> 125 us
    pallas_call x2, Pallas kernels: 122 us -> 125 us  [call(): pl.pallas_call(kernel, name=name, out_shape=[jax.ShapeDtypeStruct(shape,...]
where the time goes in v3:
time: 126 us
  Pallas kernels  125 us (99%)
    pallas_call x2, Pallas kernels, call(): pl.pallas_call(kernel, name=name, out_shape=[jax.ShapeDtypeStruct(shape,...  125 us

profile of v3, /device:TPU:0, one launch (start us, length us, event | category | flops | bytes accessed | tf_op | source)
XLA Modules:
  0.0 125.6 jit_solution(3367981608394194603)
XLA Ops:
  0.6 122.7 %layer.1 = (bf16[192,512]{1,0:T(8,128)(2,1)}, f32[192,512]{1,0:T(8,128)}, f32[48,1280]{1,0:T(8,128)}) custom-call(bf16[512,768]{1,0:T(8,128)(2,1)} %bitcast.20, bf16[2,24]{1,0:T(2,128)(2,1)} %gains.1, bf16[2,24]{1,0:T(2,128)(2,1)} %shifts.1, bf16[2,24]{1,0:T(2,128)(2,1)} %outs.1, bf16[3,24,192]{2,1,0:T(8,128)(2,1)} %bitcast.22, bf16[3,2,3]{2,1,0:T(2,128)(2,1)} %bitcast.25, ...), custom_call_target="tpu_custom_call" | custom-call | tf_op jit(solution)/shard_map/layer/pallas_call | solution.py:915
  123.3 2.2 %finish.1 = (bf16[192,512]{1,0:T(8,128)(2,1)}, f32[192,512]{1,0:T(8,128)}, f32[2,24]{1,0:T(2,128)}, f32[2,24]{1,0:T(2,128)}, f32[3,24,192]{2,1,0:T(8,128)}, /*in...) custom-call(bf16[192,512]{1,0:T(8,128)(2,1)} %get-tuple-element.25.o, ...), custom_call_target="tpu_custom_call" | custom-call | tf_op jit(solution)/shard_map/finish/pallas_call | solution.py:915

commit v4 on v3

--- a/solution.py
+++ b/solution.py
@@ -288,7 +288,7 @@
     tok, qkv, dense, fc1, fc2, cot_own, angle_rows, loads,
     slots, w2, small, bias, small_rows, narrow, bias_rows, out_col, cosine, sine_up, sine_down, xhat, rstd, tok_t, n1, n2, dhid, act,
     cot_t, cot, mlp_t, dx2, srow, qd, qd_in, qdt, kv, dkv, kv_t, weights, tops, top, totals, summed, query_t, query_n,
-    part_out, part_in, stat, dq_out, dq_in, kept, gq,
+    part_out, part_in, stat, dq_out, dq_in, dq_t, kept, gq,
     twin_in, halves, early_a, early_b, early_sa, early_sb, early_ea, early_eb,
     late_a, late_b, late_sa, late_sb, late_ea, late_eb,
     from_z, from_x, to_x, heads, out_send, out_recv, dx_send, dx_recv, rowsum, y_send, y_recv,
@@ -318,7 +318,6 @@
     start(brought)
     helps = both(lower, z <= 2)
     helped = both(upper, z >= 1)
-    dq_t = kept.at[:, 0:HD, :]
     dqkv = n2.at[:, QKV]
     total_kv = gq.at[0:ROWS, 0:384]
     net.knock()
@@ -530,10 +529,7 @@
         part_in[:, HD : HD + 8, :] = jnp.full((3, 8, ROWS), -1e30, F32)
         dq_in[...] = jnp.zeros_like(dq_in)
 
-    pl.when(helps)(lend.wait_recv)
-
-    @pl.loop(0, 3)
-    def _(head):
+    def ahead(head):
         span = head_span(head)
         pl.when(lower)(across(head).wait_send)
         for step in range(3):
@@ -545,13 +541,19 @@
             query_t[which] = jnp.where(row_is_low, turned, 0.0).astype(BF16)
 
         turn_queries(qd, 0)
-        pl.when(helps)(lambda: turn_queries(qd_in, 1))
         top[...] = jnp.full_like(top, -1e30)
         totals[...] = jnp.zeros_like(totals)
         summed[...] = jnp.zeros_like(summed)
 
         @pl.loop(0, chunk_count)
-        def _(index):
+        def _(turn_of):
+            index = (turn_of + lent_count) % chunk_count
+
+            @pl.when(both(helps, turn_of == chunk_count - lent_count))
+            def _():
+                pl.when(head == 0)(lend.wait_recv)
+                turn_queries(qd_in, 1)
+
             which, at = chunk_place(index)
             chunk = head * 5 + index
             tile = kv[at, :, span]
@@ -579,7 +581,7 @@
                 totals[which, :, part] = old_total[half] * shrink + fold(weight)
                 summed[which, :, part] = old_sum[half] * shrink + dot(tile_t, rounded)
 
-            @pl.when(both(helps, index == lent_count - 1))
+            @pl.when(both(helps, turn_of == chunk_count - 1))
             def _():
                 outcome(part_out, head, 1)
                 partial(head).start()
@@ -587,8 +589,7 @@
         outcome(kept, head, 0)
         pl.when(head == 1)(late.two)
 
-    @pl.loop(0, 3)
-    def _(head):
+    def merge(head):
         pl.when(helped)(partial(head).wait_recv)
         top_one, top_two = kept[head, HD : HD + 1, :], part_in[head, HD : HD + 1, :]
         peak = jnp.maximum(top_one, top_two)
@@ -603,12 +604,6 @@
         stat[0, head, 16:24, :] = jnp.broadcast_to(delta, (8, ROWS))
         pl.when(helped)(stat_copy(head).start)
 
-    heads[:, 0:TILE] = jnp.concatenate([kept[0, 0:HD, :], kept[1, 0:HD, :]], axis=0).T.astype(BF16)
-    heads[:, TILE : 2 * TILE] = jnp.concatenate(
-        [kept[2, 0:HD, :], jnp.zeros((HD, ROWS), F32)], axis=0
-    ).T.astype(BF16)
-    late.three()
-
     def give_back(head, step):
         return net.copy(
             dkv.at[given[step], :, head_span(head)],
@@ -637,8 +632,7 @@
             to_x[:, span] = total_kv[:, span].astype(BF16)
             relay_copy(head).start()
 
-    @pl.loop(0, 3)
-    def _(head):
+    def back(head):
         span = head_span(head)
         query_n[0] = low_half(qd[:, span].astype(F32)).astype(BF16)
 
@@ -679,7 +673,19 @@
 
         for step in range(3):
             pl.when(receive[step])(give_back(head, step).start)
-        pl.when(head > 0)(lambda: relay(head - 1))
+
+    @pl.loop(0, 4)
+    def _(index):
+        pl.when(index < 3)(lambda: ahead(index))
+        pl.when(index == 3)(late.three)
+        pl.when(index > 0)(lambda: back(index - 1))
+        pl.when(index < 3)(lambda: merge(index))
+
+    heads[:, 0:TILE] = jnp.concatenate([kept[0, 0:HD, :], kept[1, 0:HD, :]], axis=0).T.astype(BF16)
+    heads[:, TILE : 2 * TILE] = jnp.concatenate(
+        [kept[2, 0:HD, :], jnp.zeros((HD, ROWS), F32)], axis=0
+    ).T.astype(BF16)
+
 
     late.end()
 
@@ -691,6 +697,7 @@
         w2[rows, FC1] = jnp.concatenate([one[0:24], two[0:24]], axis=0).astype(BF16)
         w2[rows, FC2] = jnp.concatenate([one[24:48], two[24:48]], axis=0).astype(BF16)
 
+    relay(0)
     srow[...] = jnp.zeros_like(srow)
 
     @pl.loop(0, 4)
@@ -708,8 +715,7 @@
         srow[0:8, :] += fold(d_norm * normed)
         srow[8:16, :] += fold(d_norm)
         srow[16:24, :] += fold(d_hidden.astype(F32))
-
-    relay(2)
+        pl.when(index == 2)(lambda: relay(1))
 
     for half in (0, 1):
         span = slice(half * 384, half * 384 + 384)
@@ -744,6 +750,8 @@
     ]
     start(out_copies)
 
+
+    relay(2)
 
     @pl.loop(0, 3)
     def _(head):
@@ -997,6 +1005,7 @@
             vm((2, 3, 24, ROWS), F32),
             vm((3, HD, ROWS), BF16),
             vm((3, HD, ROWS), BF16),
+            vm((3, HD, ROWS), F32),
             vm((3, 80, ROWS), F32),
             vm((WIDE, 896), F32),
             vm((16, 48, HALF), BF16),

time: 126 us -> 122 us (0.968)
  Pallas kernels: 125 us -> 121 us
    pallas_call x2, Pallas kernels: 125 us -> 121 us  [call(): pl.pallas_call(kernel, name=name, out_shape=[jax.ShapeDtypeStruct(shape,...]
where the time goes in v4:
time: 122 us
  Pallas kernels  121 us (99%)
    pallas_call x2, Pallas kernels, call(): pl.pallas_call(kernel, name=name, out_shape=[jax.ShapeDtypeStruct(shape,...  121 us

profile of v4, /device:TPU:0, one launch (start us, length us, event | category | flops | bytes accessed | tf_op | source)
XLA Modules:
  0.0 121.8 jit_solution(1209274634126661313)
XLA Ops:
  0.6 118.9 %layer.1 = (bf16[192,512]{1,0:T(8,128)(2,1)}, f32[192,512]{1,0:T(8,128)}, f32[48,1280]{1,0:T(8,128)}) custom-call(bf16[512,768]{1,0:T(8,128)(2,1)} %bitcast.20, bf16[2,24]{1,0:T(2,128)(2,1)} %gains.1, bf16[2,24]{1,0:T(2,128)(2,1)} %shifts.1, bf16[2,24]{1,0:T(2,128)(2,1)} %outs.1, bf16[3,24,192]{2,1,0:T(8,128)(2,1)} %bitcast.22, bf16[3,2,3]{2,1,0:T(2,128)(2,1)} %bitcast.25, ...), custom_call_target="tpu_custom_call" | custom-call | tf_op jit(solution)/shard_map/layer/pallas_call | solution.py:923
  119.6 2.2 %finish.1 = (bf16[192,512]{1,0:T(8,128)(2,1)}, f32[192,512]{1,0:T(8,128)}, f32[2,24]{1,0:T(2,128)}, f32[2,24]{1,0:T(2,128)}, f32[3,24,192]{2,1,0:T(8,128)}, /*in...) custom-call(bf16[192,512]{1,0:T(8,128)(2,1)} %get-tuple-element.25.o, ...), custom_call_target="tpu_custom_call" | custom-call | tf_op jit(solution)/shard_map/finish/pallas_call | solution.py:923

commit v5 on v4

--- a/solution.py
+++ b/solution.py
@@ -456,8 +456,8 @@
         receive.append(either(upper, either(z - step >= 0, both(z == 0, step >= 2))))
         given.append((z - step + 4) % 4 + 4 * xhi * ((z - step + 4) // 4))
     head_span = lambda head: pl.ds(pl.multiple_of(head * TILE, TILE), TILE)
-    across_at, along_at, return_at, relay_at, part_at, stat_at, dq_at = (
-        net.take(count) for count in (3, 9, 9, 3, 3, 3, 3)
+    across_at, along_at, return_at, relay_at, part_at, stat_at, dq_at, lend_at = (
+        net.take(count) for count in (3, 9, 9, 3, 3, 3, 3, 3)
     )
 
     def across(head):
@@ -468,11 +468,21 @@
         piece = kv.at[block - 4 * xhi * ((z + step + 1) // 4), :, head_span(head)]
         return net.copy(piece, piece, net.at_z(step + 1), along_at + 3 * head + step)
 
-    @pl.loop(0, 3)
-    def _(head):
+    def send_first(head):
         pl.when(lower)(across(head).start)
         for step in range(3):
             pl.when(send_own[step])(along(head, step).start)
+
+    def send_second(head):
+        pl.when(upper)(across(head).wait_recv)
+        for step in range(3):
+            pl.when(send_prior[step])(along(head, step).start)
+        pl.when(helped)(lend(head).start)
+
+    def lend(head):
+        return net.copy(qd.at[:, head_span(head)], qd_in.at[:, head_span(head)], net.pal(), lend_at + head)
+
+    send_first(0)
 
 
     wait(gather_y)
@@ -492,14 +502,8 @@
         for head, tile in enumerate((swap_halves(pair), pair, swap_halves(last))):
             qd[rows, spans[head]] = (qd[rows, spans[head]].astype(F32) + high_half(tile)).astype(BF16)
 
-    lend = net.copy(qd, qd_in, net.pal())
-    pl.when(helped)(lend.start)
-
-    @pl.loop(0, 3)
-    def _(head):
-        pl.when(upper)(across(head).wait_recv)
-        for step in range(3):
-            pl.when(send_prior[step])(along(head, step).start)
+    send_second(0)
+    send_first(1)
 
     row_is_low = lax.broadcasted_iota(jnp.int32, (TILE, ROWS), 0) < HD
     lent_count = (1 - xhi) * (3 - z)
@@ -534,6 +538,8 @@
         pl.when(lower)(across(head).wait_send)
         for step in range(3):
             pl.when(receive[step])(along(head, step).wait_recv)
+        pl.when(head < 2)(lambda: send_second(head + 1))
+        pl.when(head == 0)(lambda: send_first(2))
 
         def turn_queries(source, which):
             turned = source[:, span].astype(F32).T
@@ -551,7 +557,7 @@
 
             @pl.when(both(helps, turn_of == chunk_count - lent_count))
             def _():
-                pl.when(head == 0)(lend.wait_recv)
+                lend(head).wait_recv()
                 turn_queries(qd_in, 1)
 
             which, at = chunk_place(index)
@@ -587,7 +593,7 @@
                 partial(head).start()
 
         outcome(kept, head, 0)
-        pl.when(head == 1)(late.two)
+        pl.when(head == 2)(late.two)
 
     def merge(head):
         pl.when(helped)(partial(head).wait_recv)
@@ -863,6 +869,7 @@
 
     @pl.loop(0, 3)
     def _(head):
+        pl.when(helped)(lend(head).wait_send)
         pl.when(helps)(partial(head).wait_send)
         pl.when(helped)(stat_copy(head).wait_send)
         pl.when(helps)(dq_copy(head).wait_send)
@@ -871,7 +878,6 @@
             pl.when(either(send_own[step], send_prior[step]))(along(head, step).wait_send)
             pl.when(receive[step])(give_back(head, step).wait_send)
 
-    pl.when(helped)(lend.wait_send)
     fc_sum.end(final)
     qkv_sum.end(final)
 

time: 122 us -> 124 us (1.016)
  Pallas kernels: 121 us -> 123 us
    pallas_call x2, Pallas kernels: 121 us -> 123 us  [call(): pl.pallas_call(kernel, name=name, out_shape=[jax.ShapeDtypeStruct(shape,...]
where the time goes in v5:
time: 124 us
  Pallas kernels  123 us (99%)
    pallas_call x2, Pallas kernels, call(): pl.pallas_call(kernel, name=name, out_shape=[jax.ShapeDtypeStruct(shape,...  123 us

profile of v5, /device:TPU:0, one launch (start us, length us, event | category | flops | bytes accessed | tf_op | source)
XLA Modules:
  0.0 124.0 jit_solution(16066710817180962690)
XLA Ops:
  0.6 121.1 %layer.1 = (bf16[192,512]{1,0:T(8,128)(2,1)}, f32[192,512]{1,0:T(8,128)}, f32[48,1280]{1,0:T(8,128)}) custom-call(bf16[512,768]{1,0:T(8,128)(2,1)} %bitcast.20, bf16[2,24]{1,0:T(2,128)(2,1)} %gains.1, bf16[2,24]{1,0:T(2,128)(2,1)} %shifts.1, bf16[2,24]{1,0:T(2,128)(2,1)} %outs.1, bf16[3,24,192]{2,1,0:T(8,128)(2,1)} %bitcast.22, bf16[3,2,3]{2,1,0:T(2,128)(2,1)} %bitcast.25, ...), custom_call_target="tpu_custom_call" | custom-call | tf_op jit(solution)/shard_map/layer/pallas_call | solution.py:929
  121.8 2.2 %finish.1 = (bf16[192,512]{1,0:T(8,128)(2,1)}, f32[192,512]{1,0:T(8,128)}, f32[2,24]{1,0:T(2,128)}, f32[2,24]{1,0:T(2,128)}, f32[3,24,192]{2,1,0:T(8,128)}, /*in...) custom-call(bf16[192,512]{1,0:T(8,128)(2,1)} %get-tuple-element.25.o, ...), custom_call_target="tpu_custom_call" | custom-call | tf_op jit(solution)/shard_map/finish/pallas_call | solution.py:929

commit v6 on v4

--- a/solution.py
+++ b/solution.py
@@ -288,7 +288,7 @@
     tok, qkv, dense, fc1, fc2, cot_own, angle_rows, loads,
     slots, w2, small, bias, small_rows, narrow, bias_rows, out_col, cosine, sine_up, sine_down, xhat, rstd, tok_t, n1, n2, dhid, act,
     cot_t, cot, mlp_t, dx2, srow, qd, qd_in, qdt, kv, dkv, kv_t, weights, tops, top, totals, summed, query_t, query_n,
-    part_out, part_in, stat, dq_out, dq_in, dq_t, kept, gq,
+    part_out, part_in, part_top, part_top_in, stat, dq_out, dq_in, dq_t, kept, gq,
     twin_in, halves, early_a, early_b, early_sa, early_sb, early_ea, early_eb,
     late_a, late_b, late_sa, late_sb, late_ea, late_eb,
     from_z, from_x, to_x, heads, out_send, out_recv, dx_send, dx_recv, rowsum, y_send, y_recv,
@@ -397,6 +397,7 @@
         tok_t[:, rows] = tok[rows, :].astype(F32).T.astype(BF16)
 
     early.three()
+    late.two()
     dkv[...] = jnp.zeros_like(dkv)
     early.end()
     bias_rows[...] = jnp.zeros_like(bias_rows)
@@ -456,8 +457,8 @@
         receive.append(either(upper, either(z - step >= 0, both(z == 0, step >= 2))))
         given.append((z - step + 4) % 4 + 4 * xhi * ((z - step + 4) // 4))
     head_span = lambda head: pl.ds(pl.multiple_of(head * TILE, TILE), TILE)
-    across_at, along_at, return_at, relay_at, part_at, stat_at, dq_at = (
-        net.take(count) for count in (3, 9, 9, 3, 3, 3, 3)
+    across_at, along_at, return_at, relay_at, part_at, stat_at, dq_at, top_at = (
+        net.take(count) for count in (3, 9, 9, 3, 3, 3, 3, 3)
     )
 
     def across(head):
@@ -473,6 +474,8 @@
         pl.when(lower)(across(head).start)
         for step in range(3):
             pl.when(send_own[step])(along(head, step).start)
+
+    late.three()
 
 
     wait(gather_y)
@@ -501,6 +504,53 @@
         for step in range(3):
             pl.when(send_prior[step])(along(head, step).start)
 
+    late.end()
+
+    @pl.loop(0, 16)
+    def _(pair):
+        rows = pl.ds(pl.multiple_of(pair * 48, 16), 48)
+        one = slots[2 * pair, :, EARLY:HALF].astype(F32)
+        two = slots[2 * pair + 1, :, EARLY:HALF].astype(F32)
+        w2[rows, FC1] = jnp.concatenate([one[0:24], two[0:24]], axis=0).astype(BF16)
+        w2[rows, FC2] = jnp.concatenate([one[24:48], two[24:48]], axis=0).astype(BF16)
+
+    srow[...] = jnp.zeros_like(srow)
+
+    @pl.loop(0, 4)
+    def _(index):
+        rows = tile_at(index)
+        hidden = dot(n2[rows, :], w2[:, FC1]) + bias[1:2, :]
+        spread_to = 0.5 + 0.5 * lax.erf(hidden * (0.5**0.5))
+        act[rows, :] = (hidden * spread_to).astype(BF16)
+        slope = spread_to + hidden * jnp.exp(-0.5 * hidden * hidden) * 0.3989422804014327
+        d_hidden = (slope * dot(cot[rows, :], w2[:, FC2])).astype(BF16)
+        dhid[rows, :] = d_hidden
+        d_norm = dot_nt(d_hidden, w2[:, FC1])
+        normed = xhat[rows, :]
+        dx2[rows, :] = norm_back(small[1:2, :] * d_norm, normed, rstd[rows, 0:1])
+        srow[0:8, :] += fold(d_norm * normed)
+        srow[8:16, :] += fold(d_norm)
+        srow[16:24, :] += fold(d_hidden.astype(F32))
+
+    for half in (0, 1):
+        span = slice(half * 384, half * 384 + 384)
+        mlp_t[span, :] = dot_nt(w2[span, FC2], act[...])
+        gq[0:384, 0:WIDE] = dot_tn(n2[:, span], dhid[...])
+        gq[384:768, 0:WIDE] = dot(cot_t[span, :], act[...])
+
+        @pl.loop(0, 16)
+        def _(index):
+            first = pl.ds(pl.multiple_of(index * 24, 8), 24)
+            second = pl.ds(pl.multiple_of(384 + index * 24, 8), 24)
+            slots[half * 16 + index, :, EARLY:HALF] = jnp.concatenate(
+                [gq[first, 0:WIDE], gq[second, 0:WIDE]], axis=0
+            ).astype(BF16)
+
+    fc_sum = Reduce(
+        net, slots, EARLY, 896, HALF, twin_in, halves, late_a, late_b, late_sa, late_sb, late_ea, late_eb
+    )
+    fc_sum.one()
+
     row_is_low = lax.broadcasted_iota(jnp.int32, (TILE, ROWS), 0) < HD
     lent_count = (1 - xhi) * (3 - z)
     chunk_count = 4 + xhi
@@ -512,21 +562,24 @@
     def partial(head):
         return net.copy(part_out.at[head], part_in.at[head], net.pal(), part_at + head)
 
+    def partial_top(head):
+        return net.copy(part_top.at[head], part_top_in.at[head], net.pal(), top_at + head)
+
     def stat_copy(head):
         return net.copy(stat.at[0, head], stat.at[1, head], net.pal(), stat_at + head)
 
     def dq_copy(head):
         return net.copy(dq_out.at[head], dq_in.at[head], net.pal(), dq_at + head)
 
-    def outcome(target, head, which):
-        target[head, 0:HD, :] = summed[which, HD:TILE, :]
-        target[head, HD : HD + 8, :] = top[which]
-        target[head, HD + 8 : HD + 16, :] = jnp.broadcast_to(column_sum(totals[which]), (8, ROWS))
+    def tops_of(which):
+        total = jnp.broadcast_to(column_sum(totals[which]), (8, ROWS))
+        return jnp.where(lax.broadcasted_iota(jnp.int32, (8, ROWS), 0) == 0, top[which], total)
 
     @pl.when(jnp.logical_not(helped))
     def _():
         part_in[...] = jnp.zeros_like(part_in)
-        part_in[:, HD : HD + 8, :] = jnp.full((3, 8, ROWS), -1e30, F32)
+        is_top = lax.broadcasted_iota(jnp.int32, (3, 8, ROWS), 1) == 0
+        part_top_in[...] = jnp.where(is_top, -1e30, 0.0)
         dq_in[...] = jnp.zeros_like(dq_in)
 
     def ahead(head):
@@ -583,25 +636,27 @@
 
             @pl.when(both(helps, turn_of == chunk_count - 1))
             def _():
-                outcome(part_out, head, 1)
+                part_out[head] = summed[1, HD:TILE, :].astype(BF16)
+                part_top[head] = tops_of(1)
                 partial(head).start()
-
-        outcome(kept, head, 0)
-        pl.when(head == 1)(late.two)
+                partial_top(head).start()
+
+        kept[head, 0:HD, :] = summed[0, HD:TILE, :]
+        kept[head, HD : HD + 8, :] = tops_of(0)
 
     def merge(head):
         pl.when(helped)(partial(head).wait_recv)
-        top_one, top_two = kept[head, HD : HD + 1, :], part_in[head, HD : HD + 1, :]
+        pl.when(helped)(partial_top(head).wait_recv)
+        top_one, top_two = kept[head, HD : HD + 1, :], part_top_in[head, 0:1, :]
         peak = jnp.maximum(top_one, top_two)
         share_one, share_two = jnp.exp(top_one - peak), jnp.exp(top_two - peak)
-        total = kept[head, HD + 8 : HD + 9, :] * share_one + part_in[head, HD + 8 : HD + 9, :] * share_two
+        total = kept[head, HD + 1 : HD + 2, :] * share_one + part_top_in[head, 1:2, :] * share_two
         inverse = 1.0 / total
-        result = (kept[head, 0:HD, :] * share_one + part_in[head, 0:HD, :] * share_two) * inverse
+        result = (kept[head, 0:HD, :] * share_one + part_in[head].astype(F32) * share_two) * inverse
         delta = column_sum(qdt[head, HD:TILE, :].astype(F32) * result)
         kept[head, 0:HD, :] = result
-        stat[0, head, 0:8, :] = jnp.broadcast_to(peak, (8, ROWS))
-        stat[0, head, 8:16, :] = jnp.broadcast_to(inverse, (8, ROWS))
-        stat[0, head, 16:24, :] = jnp.broadcast_to(delta, (8, ROWS))
+        row = lax.broadcasted_iota(jnp.int32, (8, ROWS), 0)
+        stat[0, head] = jnp.where(row == 0, peak, jnp.where(row == 1, inverse, delta))
         pl.when(helped)(stat_copy(head).start)
 
     def give_back(head, step):
@@ -651,14 +706,14 @@
             change = dkv[at, :, span].astype(F32)
             for half in (0, 1):
                 part = slice(half * 256, half * 256 + 256)
-                factor = jnp.exp(tops[chunk, 0:1, part] - stat[which, head, 0:1, part]) * stat[which, head, 8:9, part]
+                factor = jnp.exp(tops[chunk, 0:1, part] - stat[which, head, 0:1, part]) * stat[which, head, 1:2, part]
                 weight = weights[chunk, :, part]
                 scaled = jnp.where(
                     row_is_low[:, 0:256], 0.0, qdt[which * 3 + head, :, part].astype(F32) * factor
                 )
                 d_weight = dot(kv[at, :, span], scaled.astype(BF16))
                 d_score = (
-                    weight.astype(F32) * (d_weight - stat[which, head, 16:17, part] * factor)
+                    weight.astype(F32) * (d_weight - stat[which, head, 2:3, part] * factor)
                 ).astype(BF16)
                 change = change + dot(d_score, query_n[which, part, :]) + dot(weight, scaled.T.astype(BF16))
                 summed[which, :, part] += dot(kv_t[chunk], d_score)
@@ -677,64 +732,17 @@
     @pl.loop(0, 4)
     def _(index):
         pl.when(index < 3)(lambda: ahead(index))
-        pl.when(index == 3)(late.three)
+        pl.when(index == 0)(fc_sum.two)
+        pl.when(index == 3)(fc_sum.three)
         pl.when(index > 0)(lambda: back(index - 1))
         pl.when(index < 3)(lambda: merge(index))
+        pl.when(index > 1)(lambda: relay(index - 2))
 
     heads[:, 0:TILE] = jnp.concatenate([kept[0, 0:HD, :], kept[1, 0:HD, :]], axis=0).T.astype(BF16)
     heads[:, TILE : 2 * TILE] = jnp.concatenate(
         [kept[2, 0:HD, :], jnp.zeros((HD, ROWS), F32)], axis=0
     ).T.astype(BF16)
 
-
-    late.end()
-
-    @pl.loop(0, 16)
-    def _(pair):
-        rows = pl.ds(pl.multiple_of(pair * 48, 16), 48)
-        one = slots[2 * pair, :, EARLY:HALF].astype(F32)
-        two = slots[2 * pair + 1, :, EARLY:HALF].astype(F32)
-        w2[rows, FC1] = jnp.concatenate([one[0:24], two[0:24]], axis=0).astype(BF16)
-        w2[rows, FC2] = jnp.concatenate([one[24:48], two[24:48]], axis=0).astype(BF16)
-
-    relay(0)
-    srow[...] = jnp.zeros_like(srow)
-
-    @pl.loop(0, 4)
-    def _(index):
-        rows = tile_at(index)
-        hidden = dot(n2[rows, :], w2[:, FC1]) + bias[1:2, :]
-        spread_to = 0.5 + 0.5 * lax.erf(hidden * (0.5**0.5))
-        act[rows, :] = (hidden * spread_to).astype(BF16)
-        slope = spread_to + hidden * jnp.exp(-0.5 * hidden * hidden) * 0.3989422804014327
-        d_hidden = (slope * dot(cot[rows, :], w2[:, FC2])).astype(BF16)
-        dhid[rows, :] = d_hidden
-        d_norm = dot_nt(d_hidden, w2[:, FC1])
-        normed = xhat[rows, :]
-        dx2[rows, :] = norm_back(small[1:2, :] * d_norm, normed, rstd[rows, 0:1])
-        srow[0:8, :] += fold(d_norm * normed)
-        srow[8:16, :] += fold(d_norm)
-        srow[16:24, :] += fold(d_hidden.astype(F32))
-        pl.when(index == 2)(lambda: relay(1))
-
-    for half in (0, 1):
-        span = slice(half * 384, half * 384 + 384)
-        mlp_t[span, :] = dot_nt(w2[span, FC2], act[...])
-        gq[0:384, 0:WIDE] = dot_tn(n2[:, span], dhid[...])
-        gq[384:768, 0:WIDE] = dot(cot_t[span, :], act[...])
-
-        @pl.loop(0, 16)
-        def _(index):
-            first = pl.ds(pl.multiple_of(index * 24, 8), 24)
-            second = pl.ds(pl.multiple_of(384 + index * 24, 8), 24)
-            slots[half * 16 + index, :, EARLY:HALF] = jnp.concatenate(
-                [gq[first, 0:WIDE], gq[second, 0:WIDE]], axis=0
-            ).astype(BF16)
-
-    fc_sum = Reduce(
-        net, slots, EARLY, 896, HALF, twin_in, halves, late_a, late_b, late_sa, late_sb, late_ea, late_eb
-    )
-    fc_sum.one()
 
     for half in (0, 1):
         span = slice(half * 384, half * 384 + 384)
@@ -769,7 +777,6 @@
     def _():
         total_kv[...] += from_x[...].astype(F32)
 
-    fc_sum.two()
     rowsum[...] = jnp.zeros_like(rowsum)
 
     @pl.loop(0, 4)
@@ -843,7 +850,6 @@
         second = jnp.concatenate([gq[rows, 384:640], gq[rows, 768:896], bias_rows[...]], axis=1)
         slots[index, :, 0:EARLY] = jnp.concatenate([first, second], axis=0).astype(BF16)
 
-    fc_sum.three()
     qkv_sum = Reduce(
         net, slots, 0, 256, EARLY, twin_in, halves, early_a, early_b, early_sa, early_sb, early_ea, early_eb
     )
@@ -864,6 +870,7 @@
     @pl.loop(0, 3)
     def _(head):
         pl.when(helps)(partial(head).wait_send)
+        pl.when(helps)(partial_top(head).wait_send)
         pl.when(helped)(stat_copy(head).wait_send)
         pl.when(helps)(dq_copy(head).wait_send)
         pl.when(upper)(relay_copy(head).wait_send)
@@ -1000,9 +1007,11 @@
             vm((2, TILE, ROWS), F32),
             vm((2, TILE, ROWS), BF16),
             vm((2, ROWS, TILE), BF16),
-            vm((3, 80, ROWS), F32),
-            vm((3, 80, ROWS), F32),
-            vm((2, 3, 24, ROWS), F32),
+            vm((3, HD, ROWS), BF16),
+            vm((3, HD, ROWS), BF16),
+            vm((3, 8, ROWS), F32),
+            vm((3, 8, ROWS), F32),
+            vm((2, 3, 8, ROWS), F32),
             vm((3, HD, ROWS), BF16),
             vm((3, HD, ROWS), BF16),
             vm((3, HD, ROWS), F32),
@@ -1033,8 +1042,8 @@
             vm((24, WIDE), F32),
             vm((8, WIDE), F32),
             vm((3, 8, WIDE), F32),
-            dma((144,)),
-            dma((144,)),
+            dma((192,)),
+            dma((192,)),
         ],
         0,
         [

time: 122 us -> 118 us (0.967)
  Pallas kernels: 121 us -> 117 us
    pallas_call x2, Pallas kernels: 121 us -> 117 us  [call(): pl.pallas_call(kernel, name=name, out_shape=[jax.ShapeDtypeStruct(shape,...]
where the time goes in v6:
time: 118 us; the launch traced here: 117 us
  Pallas kernels  117 us (99%)
    pallas_call x2, Pallas kernels, call(): pl.pallas_call(kernel, name=name, out_shape=[jax.ShapeDtypeStruct(shape,...  117 us

profile of v6, /device:TPU:0, one launch (start us, length us, event | category | flops | bytes accessed | tf_op | source)
XLA Modules:
  0.0 117.4 jit_solution(6553996334189462742)
XLA Ops:
  0.6 114.5 %layer.1 = (bf16[192,512]{1,0:T(8,128)(2,1)}, f32[192,512]{1,0:T(8,128)}, f32[48,1280]{1,0:T(8,128)}) custom-call(bf16[512,768]{1,0:T(8,128)(2,1)} %bitcast.20, bf16[2,24]{1,0:T(2,128)(2,1)} %gains.1, bf16[2,24]{1,0:T(2,128)(2,1)} %shifts.1, bf16[2,24]{1,0:T(2,128)(2,1)} %outs.1, bf16[3,24,192]{2,1,0:T(8,128)(2,1)} %bitcast.22, bf16[3,2,3]{2,1,0:T(2,128)(2,1)} %bitcast.25, ...), custom_call_target="tpu_custom_call" | custom-call | tf_op jit(solution)/shard_map/layer/pallas_call | solution.py:930
  115.1 2.2 %finish.1 = (bf16[192,512]{1,0:T(8,128)(2,1)}, f32[192,512]{1,0:T(8,128)}, f32[2,24]{1,0:T(2,128)}, f32[2,24]{1,0:T(2,128)}, f32[3,24,192]{2,1,0:T(8,128)}, /*in...) custom-call(bf16[192,512]{1,0:T(8,128)(2,1)} %get-tuple-element.25.o, ...), custom_call_target="tpu_custom_call" | custom-call | tf_op jit(solution)/shard_map/finish/pallas_call | solution.py:930

commit v7 on v6

--- a/solution.py
+++ b/solution.py
@@ -475,8 +475,6 @@
         for step in range(3):
             pl.when(send_own[step])(along(head, step).start)
 
-    late.three()
-
 
     wait(gather_y)
 
@@ -504,6 +502,7 @@
         for step in range(3):
             pl.when(send_prior[step])(along(head, step).start)
 
+    late.three()
     late.end()
 
     @pl.loop(0, 16)

time: 118 us -> 121 us (1.025)
  Pallas kernels: 117 us -> 120 us
    pallas_call x2, Pallas kernels: 117 us -> 120 us  [call(): pl.pallas_call(kernel, name=name, out_shape=[jax.ShapeDtypeStruct(shape,...]
where the time goes in v7:
time: 121 us; the launch traced here: 120 us
  Pallas kernels  120 us (99%)
    pallas_call x2, Pallas kernels, call(): pl.pallas_call(kernel, name=name, out_shape=[jax.ShapeDtypeStruct(shape,...  120 us

profile of v7, /device:TPU:0, one launch (start us, length us, event | category | flops | bytes accessed | tf_op | source)
XLA Modules:
  0.0 120.4 jit_solution(5969060387194466296)
XLA Ops:
  0.6 117.5 %layer.1 = (bf16[192,512]{1,0:T(8,128)(2,1)}, f32[192,512]{1,0:T(8,128)}, f32[48,1280]{1,0:T(8,128)}) custom-call(bf16[512,768]{1,0:T(8,128)(2,1)} %bitcast.20, bf16[2,24]{1,0:T(2,128)(2,1)} %gains.1, bf16[2,24]{1,0:T(2,128)(2,1)} %shifts.1, bf16[2,24]{1,0:T(2,128)(2,1)} %outs.1, bf16[3,24,192]{2,1,0:T(8,128)(2,1)} %bitcast.22, bf16[3,2,3]{2,1,0:T(2,128)(2,1)} %bitcast.25, ...), custom_call_target="tpu_custom_call" | custom-call | tf_op jit(solution)/shard_map/layer/pallas_call | solution.py:929
  118.1 2.2 %finish.1 = (bf16[192,512]{1,0:T(8,128)(2,1)}, f32[192,512]{1,0:T(8,128)}, f32[2,24]{1,0:T(2,128)}, f32[2,24]{1,0:T(2,128)}, f32[3,24,192]{2,1,0:T(8,128)}, /*in...) custom-call(bf16[192,512]{1,0:T(8,128)(2,1)} %get-tuple-element.25.o, ...), custom_call_target="tpu_custom_call" | custom-call | tf_op jit(solution)/shard_map/finish/pallas_call | solution.py:929
